TPU v7x, 256 devices: a whole 4x4x8 slice. The times are simulated.
256 devices in a mesh: dp: 32 (over z, y), head: 8 (over x, core).
Axes of the slice: x: 4, y: 4, z: 8, core: 2. Of those that a mesh axis runs over, the one named last changes fastest.
Arguments:
- queries: bfloat16 [16384, 8192], P('dp', 'head'), may hold values from -128 to 128
- response_keys: bfloat16 [16384, 1024], P('dp', 'head'), may hold values from -6 to 6
- response_values: bfloat16 [16384, 1024], P('dp', 'head'), may hold values from -6 to 6
- output_cotangent: bfloat16 [16384, 8192], P('dp', 'head'), may hold values from -6 to 6
- prompt_key_rows: bfloat16 [4096, 1024], P(('dp', 'head')), may hold values from -6 to 6
- prompt_value_rows: bfloat16 [4096, 1024], P(('dp', 'head')), may hold values from -6 to 6
- resp_len: int32 [32, 32], P('dp'), may hold values from 1 to 32, 512 in all within a row
- resp_owner: int32 [32, 32], P('dp'), may hold values from 0 to 31, each once within a row
- block_mask: int32 [32, 32, 1], P('dp'), may hold values 0 or 1
Outputs:
- query_grads: bfloat16 [16384, 8192], P('dp', 'head')
- key_grads: bfloat16 [16384, 1024], P('dp', 'head')
- value_grads: bfloat16 [16384, 1024], P('dp', 'head')
- prompt_key_grads: bfloat16 [4096, 1024], P('dp', 'head')
- prompt_value_grads: bfloat16 [4096, 1024], P('dp', 'head')
Inputs may be any that keep to these rules, and one draw needn't show every extreme that they name: `resp_len`: row d sums to 512; the longest response on every dp index has exactly 32 tokens. `resp_owner`: each row is a permutation: every dp index holds exactly one response of every prompt, and prompt p is owned by dp index p.
All inputs are finite; a program needn't handle non-finite values. No bound on the sum of `block_mask` on one device may be relied on, other than what follows from the above.
Results may differ from a plain program's by a relative error of at most 0.012.
Values may be sent and summed in bfloat16 or wider, within the bound.
No kernel may reach another device: no remote copies, remote signals or barrier semaphores. Data moves between devices by JAX's collectives and lax.ppermute only.
A program may use at most 128 MiB of HBM per device.

v0:
```python
import math

import jax
import jax.numpy as jnp
from jax import lax
from jax.sharding import PartitionSpec as P

QUERY_HEADS = 64
KEY_VALUE_HEADS = 8
HEAD_DIMENSION = 128
BLK = 128
MOSTLEN = 32


far_below = -1e30


def partial_stats(scores, visible, dots):
    highest = jnp.max(jnp.where(visible, scores, far_below), axis=-1)
    weights = jnp.where(visible, jnp.exp(scores - highest[..., None]), 0.0)
    return (highest, jnp.sum(weights, axis=-1), jnp.sum(weights * dots, axis=-1))


def weights_and_slopes(scores, visible, dots, logsum, delta):
    probs = jnp.where(visible, jnp.exp(scores - logsum[..., None]), 0.0)
    slopes = probs * (dots - delta[..., None])
    return (probs.astype(jnp.bfloat16), slopes.astype(jnp.bfloat16))


def per_device(
    queries,
    response_keys,
    response_values,
    output_cotangent,
    prompt_key_rows,
    prompt_value_rows,
    resp_len,
    resp_owner,
    block_mask,
):
    rows_dev = queries.shape[0]
    kv_local = response_keys.shape[1] // HEAD_DIMENSION
    head_group = QUERY_HEADS // KEY_VALUE_HEADS
    heads_local = kv_local * head_group
    peers = lax.axis_size("dp")
    span = MOSTLEN
    scale = 1.0 / math.sqrt(HEAD_DIMENSION)
    lengths = resp_len[0]
    owners = resp_owner[0]
    masks = block_mask[0]
    starts = jnp.cumsum(lengths) - lengths
    ends = starts + lengths
    row_ids = jnp.arange(rows_dev, dtype=jnp.int32)
    segment = jnp.sum((row_ids[:, None] >= ends[None, :]).astype(jnp.int32), axis=1)
    prompt_ids = jnp.arange(peers, dtype=jnp.int32)
    chosen = (owners[None, :] == prompt_ids[:, None]).astype(jnp.int32)
    first_row = jnp.sum(chosen * starts[None, :], axis=1)
    counted = jnp.sum(chosen * lengths[None, :], axis=1)
    seen_blocks = jnp.sum(chosen[:, :, None] * masks[None, :, :], axis=1)
    offsets = jnp.arange(span, dtype=jnp.int32)
    picked = jnp.clip(first_row[:, None] + offsets[None, :], 0, rows_dev - 1).reshape(-1)
    filled = (offsets[None, :] < counted[:, None]).reshape(-1)
    home_place = jnp.take(owners, segment) * span + row_ids - jnp.take(starts, segment)

    def pack(values):
        taken = jnp.take(values, picked, axis=0)
        taken = jnp.where(filled[:, None], taken, jnp.zeros_like(taken))
        return taken.reshape(peers, span, values.shape[1])

    def unpack(values):
        return jnp.take(values.reshape(peers * span, values.shape[-1]), home_place, axis=0)

    layout_keys, layout_values = (
        lax.all_to_all(prompt_key_rows, "head", split_axis=1, concat_axis=0, tiled=True),
        lax.all_to_all(prompt_value_rows, "head", split_axis=1, concat_axis=0, tiled=True),
    )
    prompt_len = layout_keys.shape[0]
    key_block = jnp.arange(prompt_len, dtype=jnp.int32) // BLK
    owned_keys = layout_keys.reshape(prompt_len, kv_local, HEAD_DIMENSION)
    owned_values = layout_values.reshape(prompt_len, kv_local, HEAD_DIMENSION)
    query_four = queries.reshape(rows_dev, kv_local, head_group, HEAD_DIMENSION)
    grads_four = output_cotangent.reshape(rows_dev, kv_local, head_group, HEAD_DIMENSION)
    front = jnp.zeros((span, kv_local, HEAD_DIMENSION), jnp.bfloat16)
    keys_pad = jnp.concatenate(
        [front, response_keys.reshape(rows_dev, kv_local, HEAD_DIMENSION)], axis=0
    )
    values_pad = jnp.concatenate(
        [front, response_values.reshape(rows_dev, kv_local, HEAD_DIMENSION)], axis=0
    )
    segment_pad = jnp.concatenate([jnp.full((span,), -1, jnp.int32), segment])
    block = min(512, rows_dev)
    first = 0
    key_ids = first - span + jnp.arange(block + span, dtype=jnp.int32)
    visible = segment_pad[None, :] == segment[:, None]
    visible = visible & (key_ids[None, :] <= row_ids[:, None])
    visible = visible[:, None, None, :]
    scores = (
        jnp.einsum("qhgd,khd->qhgk", query_four, keys_pad, preferred_element_type=jnp.float32)
        * scale
    )
    dots = jnp.einsum("qhgd,khd->qhgk", grads_four, values_pad, preferred_element_type=jnp.float32)
    local_blocks = [(scores, dots, visible)]
    local_stats = [partial_stats(scores, visible, dots) for scores, dots, visible in local_blocks]
    top_self = jnp.concatenate([entry[0] for entry in local_stats], axis=0).reshape(
        rows_dev, heads_local
    )
    sum_self = jnp.concatenate([entry[1] for entry in local_stats], axis=0).reshape(
        rows_dev, heads_local
    )
    dsum_self = jnp.concatenate([entry[2] for entry in local_stats], axis=0).reshape(
        rows_dev, heads_local
    )
    got_query, got_grads, got_mask = (
        lax.all_to_all(pack(queries), "dp", split_axis=0, concat_axis=0, tiled=True),
        lax.all_to_all(pack(output_cotangent), "dp", split_axis=0, concat_axis=0, tiled=True),
        lax.all_to_all(
            seen_blocks.astype(jnp.bfloat16), "dp", split_axis=0, concat_axis=0, tiled=True
        ),
    )
    incoming = peers * span
    far_query = got_query.reshape(incoming, kv_local, head_group, HEAD_DIMENSION)
    far_grads = got_grads.reshape(incoming, kv_local, head_group, HEAD_DIMENSION)
    far_visible = jnp.take(got_mask, key_block, axis=1) > 0.5
    far_visible = jnp.broadcast_to(far_visible[:, None, :], (peers, span, prompt_len)).reshape(
        incoming, 1, 1, prompt_len
    )
    far_scores = (
        jnp.einsum("qhgd,khd->qhgk", far_query, owned_keys, preferred_element_type=jnp.float32)
        * scale
    )
    far_dots = jnp.einsum(
        "qhgd,khd->qhgk", far_grads, owned_values, preferred_element_type=jnp.float32
    )
    top_far, sum_far, dsum_far = partial_stats(far_scores, far_visible, far_dots)
    top_back, sum_back, dsum_back = (
        lax.all_to_all(
            top_far.reshape(peers, span, heads_local), "dp", split_axis=0, concat_axis=0, tiled=True
        ),
        lax.all_to_all(
            sum_far.reshape(peers, span, heads_local), "dp", split_axis=0, concat_axis=0, tiled=True
        ),
        lax.all_to_all(
            dsum_far.reshape(peers, span, heads_local),
            "dp",
            split_axis=0,
            concat_axis=0,
            tiled=True,
        ),
    )
    top_far = unpack(top_back)
    highest = jnp.maximum(top_far, top_self)
    far_factor = jnp.exp(top_far - highest)
    near_factor = jnp.exp(top_self - highest)
    total = unpack(sum_back) * far_factor + sum_self * near_factor
    logsum = highest + jnp.log(total)
    delta = (unpack(dsum_back) * far_factor + dsum_self * near_factor) / total
    logsum_far, delta_far = (
        lax.all_to_all(pack(logsum), "dp", split_axis=0, concat_axis=0, tiled=True),
        lax.all_to_all(pack(delta), "dp", split_axis=0, concat_axis=0, tiled=True),
    )
    probs, slopes = weights_and_slopes(
        far_scores,
        far_visible,
        far_dots,
        logsum_far.reshape(incoming, kv_local, head_group),
        delta_far.reshape(incoming, kv_local, head_group),
    )
    far_dq = (
        jnp.einsum("qhgk,khd->qhgd", slopes, owned_keys, preferred_element_type=jnp.float32) * scale
    ).astype(jnp.bfloat16)
    prompt_dk = (
        jnp.einsum("qhgk,qhgd->khd", slopes, far_query, preferred_element_type=jnp.float32) * scale
    )
    prompt_dv = jnp.einsum("qhgk,qhgd->khd", probs, far_grads, preferred_element_type=jnp.float32)
    dq_home = lax.all_to_all(
        far_dq.reshape(peers, span, heads_local * HEAD_DIMENSION),
        "dp",
        split_axis=0,
        concat_axis=0,
        tiled=True,
    )
    cross_dq = unpack(dq_home)
    key_grad = jnp.zeros((rows_dev + span, kv_local, HEAD_DIMENSION), jnp.float32)
    value_grad = jnp.zeros((rows_dev + span, kv_local, HEAD_DIMENSION), jnp.float32)
    first = 0
    scores, dots, visible = local_blocks[0]
    probs, slopes = weights_and_slopes(
        scores,
        visible,
        dots,
        logsum.reshape(block, kv_local, head_group),
        delta.reshape(block, kv_local, head_group),
    )
    self_dq = (
        jnp.einsum("qhgk,khd->qhgd", slopes, keys_pad, preferred_element_type=jnp.float32) * scale
    )
    key_grad = key_grad.at[first : first + block + span].add(
        jnp.einsum("qhgk,qhgd->khd", slopes, query_four, preferred_element_type=jnp.float32) * scale
    )
    value_grad = value_grad.at[first : first + block + span].add(
        jnp.einsum("qhgk,qhgd->khd", probs, grads_four, preferred_element_type=jnp.float32)
    )
    query_total = self_dq.reshape(rows_dev, heads_local * HEAD_DIMENSION) + cross_dq.astype(
        jnp.float32
    )
    return (
        query_total.astype(jnp.bfloat16),
        key_grad[span:].reshape(rows_dev, kv_local * HEAD_DIMENSION).astype(jnp.bfloat16),
        value_grad[span:].reshape(rows_dev, kv_local * HEAD_DIMENSION).astype(jnp.bfloat16),
        prompt_dk.reshape(prompt_len, kv_local * HEAD_DIMENSION).astype(jnp.bfloat16),
        prompt_dv.reshape(prompt_len, kv_local * HEAD_DIMENSION).astype(jnp.bfloat16),
    )


def solution(mesh):
    placed = (
        P("dp", "head"),
        P("dp", "head"),
        P("dp", "head"),
        P("dp", "head"),
        P(("dp", "head"), None),
        P(("dp", "head"), None),
        P("dp", None),
        P("dp", None),
        P("dp", None, None),
    )
    return jax.shard_map(
        per_device,
        mesh=mesh,
        in_specs=placed,
        out_specs=(
            P("dp", "head"),
            P("dp", "head"),
            P("dp", "head"),
            P("dp", "head"),
            P("dp", "head"),
        ),
        check_vma=False,
    )
```

profile of v0, /device:TPU:2, one launch (start us, length us, event | category | flops | bytes accessed | tf_op | source)
XLA Modules:
  0.0 375.3 jit_solution(16809242566602967331)
XLA Ops:
  2.2 11.5 %all-to-all-start = ((bf16[32,1,1]{2,1,0:T(2,128)(2,1)}), bf16[32,1,1]{2,1,0:T(2,128)(2,1)S(1)}, u32[]{:S(2)}, u32[]{:S(2)}) async-start(bf16[32,1,1]{2,1,0:T(2,128)(2,1)} %copy.167), calls=%async_computation | async-start | bytes 32768 | tf_op jit(solution)/shard_map/all_to_all | solution.py:116
  17.7 5.4 %gather_fusion.4 = bf16[1024,1024]{1,0:T(8,128)(2,1)} fusion(bf16[512,1024]{1,0:T(8,128)(2,1)S(1)} %copy-done, s32[1024]{0:T(1024)S(1)} %fusion.69), kind=kCustom, calls=%fused_computation.3.clone | custom fusion | bytes 4198400 | tf_op jit(solution)/shard_map/jit(_take)/gather | solution.py:66
  23.1 5.4 %gather_fusion.1 = bf16[1024,1024]{1,0:T(8,128)(2,1)} fusion(bf16[512,1024]{1,0:T(8,128)(2,1)S(1)} %copy-done.1, s32[1024]{0:T(1024)S(1)} %fusion.69), kind=kCustom, calls=%fused_computation.clone | custom fusion | bytes 4198400 | tf_op jit(solution)/shard_map/jit(_take)/gather | solution.py:66
  28.6 4.8 %all-to-all-start.2 = ((bf16[16,8,128]{2,0,1:T(8,128)(2,1)}), bf16[16,8,128]{2,0,1:T(8,128)(2,1)S(1)}, u32[]{:S(2)}, u32[]{:S(2)}) async-start(bf16[16,8,128]{2,0,1:T(8,128)(2,1)} %copy_bitcast_fusion.1), calls=%async_computation.2 | async-start | bytes 65536 | tf_op jit(solution)/shard_map/all_to_all | solution.py:74
  33.4 4.1 %select_select_fusion = (bf16[1024,1024]{1,0:T(8,128)(2,1)}, bf16[1024,1024]{1,0:T(8,128)(2,1)}) fusion(bf16[1024,1024]{1,0:T(8,128)(2,1)} %gather_fusion.4, pred[1024]{0:T(1024)(128)(4,1)S(1)} %compare_and_fusion, pred[1024]{0:T(1024)(128)(4,1)S(1)} %lt.76, bf16[1024,1024]{1,0:T(8,128)(2,1)} %gather_fusion.1), kind=kLoop, calls=%fused_computation.49 | loop fusion | flops 4194304 | bytes 8390656 | tf_op jit(solution)/shard_map/jit(_where)/select_n | solution.py:67
  37.5 60.9 %all_to_all.81 = bf16[32,32,1024]{2,1,0:T(8,128)(2,1)} all-to-all(bf16[32,32,1024]{2,1,0:T(8,128)(2,1)} %bitcast.375), channel_id=1, replica_groups=mesh['dp'=32,'head'=8] {'dp'}, dimensions={0} | all-to-all | bytes 4194304 | tf_op jit(solution)/shard_map/all_to_all | solution.py:114
  98.4 5.7 %all-to-all-start.5 = ((bf16[32,32,1024]{2,1,0:T(8,128)(2,1)}), bf16[32,32,1024]{2,1,0:T(8,128)(2,1)}, u32[]{:S(2)}, u32[]{:S(2)}) async-start(bf16[32,32,1024]{2,1,0:T(8,128)(2,1)} %bitcast.374), calls=%async_computation.5 | async-start | bytes 4194304 | tf_op jit(solution)/shard_map/all_to_all | solution.py:115
  107.4 1.7 fusion.3
  109.1 3.4 copy-done.2
  112.5 5.1 %fusion.9 = (f32[512,8]{0,1:T(8,128)S(1)}, f32[512,8]{0,1:T(8,128)S(1)}, f32[544,512,8]{1,0,2:T(8,128)}) fusion(f32[544,512,8]{1,0,2:T(8,128)S(1)} %get-tuple-element.160, f32[512,8]{0,1:T(8,128)S(1)} %get-tuple-element.159, pred[512,544]{0,1:T(8,128)(4,1)S(1)} %fusion.47, bf16[512,1,128]{2,0,1:T(8,128)(2,1)S(1)} %bitcast.401, bf16[512,1024]{1,0:T(8,128)(2,1)S(1)} %copy-done), kind=kOutput, calls=%fused_computation.22 | convolution fusion | flops 583786496 | bytes 19333120 | tf_op jit(solution)/shard_map/qhgd,khd->qhgk/dot_general | solution.py:101
  118.3 3.5 copy.205
  121.8 31.7 %all-to-all-done.5 = bf16[32,32,1024]{2,1,0:T(8,128)(2,1)} async-done(((bf16[32,32,1024]{2,1,0:T(8,128)(2,1)}), bf16[32,32,1024]{2,1,0:T(8,128)(2,1)}, u32[]{:S(2)}, u32[]{:S(2)}) %all-to-all-start.5) | async-done | bytes 2097184 | tf_op jit(solution)/shard_map/all_to_all | solution.py:115
  153.5 4.8 %all-to-all-start.6 = ((bf16[16,8,128]{2,0,1:T(8,128)(2,1)}), bf16[16,8,128]{2,0,1:T(8,128)(2,1)S(1)}, u32[]{:S(2)}, u32[]{:S(2)}) async-start(bf16[16,8,128]{2,0,1:T(8,128)(2,1)} %copy_bitcast_fusion), calls=%async_computation.6 | async-start | bytes 65536 | tf_op jit(solution)/shard_map/all_to_all | solution.py:75
  158.3 4.8 %fusion.18 = (f32[1024,8]{0,1:T(8,128)S(1)}, f32[1024,8,128]{0,2,1:T(8,128)}) fusion(pred[1024,128]{0,1:T(8,128)(4,1)S(1)} %copy.168, bf16[128,128,1]{1,0,2:T(8,128)(2,1)S(1)} %bitcast.402, bf16[1024,8,128]{2,1,0:T(8,128)(2,1)} %bitcast.382), kind=kOutput, calls=%fused_computation.35 | convolution fusion | flops 271572992 | bytes 6488064 | tf_op jit(solution)/shard_map/qhgd,khd->qhgk/dot_general | solution.py:128
  163.1 3.6 copy.206
  166.7 6.6 %fusion.24 = (f32[1024,8]{0,1:T(8,128)S(1)}, f32[1024,8]{0,1:T(8,128)S(1)}, f32[1024,8,128]{0,2,1:T(8,128)}) fusion(f32[1024,8,128]{0,2,1:T(8,128)} %get-tuple-element.162, f32[1024,8]{0,1:T(8,128)S(1)} %get-tuple-element.161, pred[1024,128]{0,1:T(8,128)(4,1)S(1)} %copy.168, bf16[128,128,1]{1,0,2:T(8,128)(2,1)S(1)} %bitcast.404, ...), kind=kOutput, calls=%fused_computation.42 | convolution fusion | flops 274710528 | bytes 10747904 | tf_op jit(solution)/shard_map/qhgd,khd->qhgk/dot_general | solution.py:131
  174.3 6.1 %all-to-all-start.7 = ((f32[32,1,256]{2,1,0:T(1,128)}), f32[32,1,256]{2,1,0:T(1,128)S(1)}, u32[]{:S(2)}, u32[]{:S(2)}) async-start(f32[32,1,256]{2,1,0:T(1,128)} %reshape.787), calls=%async_computation.7 | async-start | bytes 65536 | tf_op jit(solution)/shard_map/all_to_all | solution.py:142
  182.0 8.0 %all-to-all-done.7 = f32[32,1,256]{2,1,0:T(1,128)S(1)} async-done(((f32[32,1,256]{2,1,0:T(1,128)}), f32[32,1,256]{2,1,0:T(1,128)S(1)}, u32[]{:S(2)}, u32[]{:S(2)}) %all-to-all-start.7) | async-done | bytes 32800 | tf_op jit(solution)/shard_map/all_to_all | solution.py:142
  190.0 3.9 %all-to-all-start.4 = ((f32[32,1,256]{2,1,0:T(1,128)}), f32[32,1,256]{2,1,0:T(1,128)S(1)}, u32[]{:S(2)}, u32[]{:S(2)}) async-start(f32[32,1,256]{2,1,0:T(1,128)} %reshape.791), calls=%async_computation.4 | async-start | bytes 65536 | tf_op jit(solution)/shard_map/all_to_all | solution.py:139
  193.9 40.4 %compare_and_fusion.1 = (pred[512]{0:T(512)(128)(4,1)S(1)}, s32[512]{0:T(512)S(1)}) fusion(s32[]{:T(128)} %bitcast.71, s32[]{:T(128)} %bitcast.70, s32[]{:T(128)} %bitcast.69, s32[]{:T(128)} %bitcast.68, s32[]{:T(128)} %bitcast.67, s32[]{:T(128)} %bitcast.66, s32[]{:T(128)} %bitcast.65, s32[]{:T(128)} %bitcast.64, s32[]{:T(128)} %bitcast.63, s32[]{:T(128)} %bitcast.62, ...), kind=kLoop, calls=%fused_computation.122 | loop fusion | flops 56320 | bytes 4864 | tf_op jit(solution)/shard_map/jit(_take)/and | solution.py:71
  235.2 9.8 %all-to-all-start.3 = ((f32[32,1,256]{2,1,0:T(1,128)}), f32[32,1,256]{2,1,0:T(1,128)S(1)}, u32[]{:S(2)}, u32[]{:S(2)}) async-start(f32[32,1,256]{2,1,0:T(1,128)} %reshape.789), calls=%async_computation.3 | async-start | bytes 65536 | tf_op jit(solution)/shard_map/all_to_all | solution.py:136
  250.1 4.8 %all-to-all-done.3 = f32[32,1,256]{2,1,0:T(1,128)S(1)} async-done(((f32[32,1,256]{2,1,0:T(1,128)}), f32[32,1,256]{2,1,0:T(1,128)S(1)}, u32[]{:S(2)}, u32[]{:S(2)}) %all-to-all-start.3) | async-done | bytes 32800 | tf_op jit(solution)/shard_map/all_to_all | solution.py:136
  257.3 4.0 %gather_fusion.6 = f32[1024,8]{1,0:T(8,128)} fusion(f32[512,8]{1,0:T(8,128)S(1)} %copy.183, s32[1024]{0:T(1024)S(1)} %fusion.69), kind=kCustom, calls=%fused_computation.2.clone | custom fusion | bytes 69632 | tf_op jit(solution)/shard_map/jit(_take)/gather | solution.py:66
  261.4 4.0 %gather_fusion.7 = f32[1024,8]{1,0:T(8,128)} fusion(f32[512,8]{1,0:T(8,128)S(1)} %copy.186, s32[1024]{0:T(1024)S(1)} %fusion.69), kind=kCustom, calls=%fused_computation.6.clone | custom fusion | bytes 69632 | tf_op jit(solution)/shard_map/jit(_take)/gather | solution.py:66
  265.5 1.6 select_select_fusion.3
  267.9 1.6 reshape.793
  269.5 5.0 %all-to-all-start.9 = ((f32[32,1,256]{2,1,0:T(1,128)}), f32[32,1,256]{2,1,0:T(1,128)S(1)}, u32[]{:S(2)}, u32[]{:S(2)}) async-start(f32[32,1,256]{2,1,0:T(1,128)} %reshape.793), calls=%async_computation.9 | async-start | bytes 65536 | tf_op jit(solution)/shard_map/all_to_all | solution.py:159
  275.5 8.9 %all-to-all-done.9 = f32[32,1,256]{2,1,0:T(1,128)S(1)} async-done(((f32[32,1,256]{2,1,0:T(1,128)}), f32[32,1,256]{2,1,0:T(1,128)S(1)}, u32[]{:S(2)}, u32[]{:S(2)}) %all-to-all-start.9) | async-done | bytes 32800 | tf_op jit(solution)/shard_map/all_to_all | solution.py:159
  284.4 3.9 %all-to-all-start.8 = ((f32[32,1,256]{2,1,0:T(1,128)}), f32[32,1,256]{2,1,0:T(1,128)S(1)}, u32[]{:S(2)}, u32[]{:S(2)}) async-start(f32[32,1,256]{2,1,0:T(1,128)} %reshape.795), calls=%async_computation.8 | async-start | bytes 65536 | tf_op jit(solution)/shard_map/all_to_all | solution.py:158
  289.3 8.8 %all-to-all-done.8 = f32[32,1,256]{2,1,0:T(1,128)S(1)} async-done(((f32[32,1,256]{2,1,0:T(1,128)}), f32[32,1,256]{2,1,0:T(1,128)S(1)}, u32[]{:S(2)}, u32[]{:S(2)}) %all-to-all-start.8) | async-done | bytes 32800 | tf_op jit(solution)/shard_map/all_to_all | solution.py:158
  299.0 6.2 %fusion.25 = (bf16[1024,8,128]{0,2,1:T(8,128)(2,1)}, bf16[1024,8,128]{0,2,1:T(8,128)(2,1)S(1)}) fusion(f32[1024,8,128]{0,2,1:T(8,128)} %get-tuple-element.162, f32[1024,8]{0,1:T(8,128)S(1)} %sub.90, pred[1024,128]{0,1:T(8,128)(4,1)S(1)} %copy.168, f32[1024,8]{0,1:T(8,128)S(1)} %sub.93, f32[1024,8,128]{0,2,1:T(8,128)} %get-tuple-element.164), kind=kLoop, calls=%fused_computation.43 | loop fusion | flops 7340032 | bytes 12779520 | tf_op jit(solution)/shard_map/reshape.138
  306.6 2.3 fusion.31
  308.9 4.2 %copy.191 = bf16[1024,1,8,128]{3,2,0,1:T(8,128)(2,1)} copy(bf16[1024,1,8,128]{0,3,2,1:T(8,128)(2,1)} %fusion.31) | data formatting | bytes 4194304 | tf_op jit(solution)/shard_map/convert_element_type | solution.py:170
  313.0 4.2 %reshape.540 = bf16[32,32,1024]{2,1,0:T(8,128)(2,1)} reshape(bf16[1024,1,8,128]{3,2,0,1:T(8,128)(2,1)} %copy.191) | data formatting | bytes 4194304 | tf_op jit(solution)/shard_map/reshape | solution.py:176
  317.2 5.0 %all-to-all-start.10 = ((bf16[32,32,1024]{2,1,0:T(8,128)(2,1)}), bf16[32,32,1024]{2,1,0:T(8,128)(2,1)}, u32[]{:S(2)}, u32[]{:S(2)}) async-start(bf16[32,32,1024]{2,1,0:T(8,128)(2,1)} %reshape.540), calls=%async_computation.10 | async-start | bytes 4194304 | tf_op jit(solution)/shard_map/all_to_all | solution.py:175
  322.2 7.4 %fusion.11 = bf16[512,8,544]{0,2,1:T(8,128)(2,1)S(1)} fusion(f32[544,512,8]{1,0,2:T(8,128)} %get-tuple-element.163, f32[544,512,8]{1,0,2:T(8,128)} %copy-done.2, f32[512,8]{0,1:T(8,128)S(1)} %copy-done.11, f32[512,8]{0,1:T(8,128)S(1)} %copy-done.9, pred[512,544]{0,1:T(8,128)(4,1)S(1)} %fusion.47), kind=kLoop, calls=%fused_computation.24 | loop fusion | flops 13369344 | bytes 22593536 | tf_op jit(solution)/shard_map/reshape.120
  329.7 2.1 copy-done.4
  331.8 2.3 convolution_multiply_fusion
  334.1 3.0 copy.192
  337.1 3.6 fusion.43
  340.6 5.2 %fusion.40 = bf16[544,1,128]{2,0,1:T(8,128)(2,1)S(1)} fusion(f32[544,512,8]{1,0,2:T(8,128)} %copy-done.2, f32[512,8]{0,1:T(8,128)S(1)} %copy-done.9, pred[512,544]{0,1:T(8,128)(4,1)S(1)} %fusion.47, bf16[512,1024]{1,0:T(8,128)(2,1)S(1)} %copy-done), kind=kOutput, calls=%fused_computation.59 | convolution fusion | flops 579407872 | bytes 10395648 | tf_op jit(solution)/shard_map/qhgk,qhgd->khd/dot_general | solution.py:201
  346.5 4.1 %copy.195 = bf16[1024,8,128]{2,1,0:T(8,128)(2,1)} copy(bf16[1024,8,128]{0,2,1:T(8,128)(2,1)} %copy-done.3) | data formatting | bytes 4194304 | tf_op jit(solution)/shard_map/reshape.126
  350.7 4.2 %copy.196 = bf16[1024,8,128]{2,1,0:T(8,128)(2,1)} copy(bf16[1024,8,128]{0,2,1:T(8,128)(2,1)} %get-tuple-element.87) | data formatting | bytes 4194304 | tf_op jit(solution)/shard_map/reshape.138
  354.8 3.0 fusion.48
  358.5 3.0 fusion.49
  362.3 5.6 %all-to-all-done.10 = bf16[32,32,1024]{2,1,0:T(8,128)(2,1)} async-done(((bf16[32,32,1024]{2,1,0:T(8,128)(2,1)}), bf16[32,32,1024]{2,1,0:T(8,128)(2,1)}, u32[]{:S(2)}, u32[]{:S(2)}) %all-to-all-start.10) | async-done | bytes 2097184 | tf_op jit(solution)/shard_map/all_to_all | solution.py:175
  367.8 4.6 %gather_fusion = bf16[512,1024]{1,0:T(8,128)(2,1)S(1)} fusion(bf16[1024,1024]{1,0:T(8,128)(2,1)} %bitcast.116, s32[1024]{0:T(1024)S(1)} %copy-done.16), kind=kCustom, calls=%fused_computation.7 | custom fusion | bytes 2099200 | tf_op jit(solution)/shard_map/jit(_take)/gather | solution.py:71
  372.5 2.9 add_convert_fusion
  (121 shorter events, 27.9 us)
Async XLA Ops:
  0.6 17.1 %copy-start = (bf16[512,1024]{1,0:T(8,128)(2,1)S(1)}, bf16[512,1024]{1,0:T(8,128)(2,1)}, u32[]{:S(2)}) copy-start(bf16[512,1024]{1,0:T(8,128)(2,1)} %param.28) | copy-start | bytes 3145732
  2.2 26.3 %all-to-all-start = ((bf16[32,1,1]{2,1,0:T(2,128)(2,1)}), bf16[32,1,1]{2,1,0:T(2,128)(2,1)S(1)}, u32[]{:S(2)}, u32[]{:S(2)}) async-start(bf16[32,1,1]{2,1,0:T(2,128)(2,1)} %copy.167), calls=%async_computation | async-start | bytes 32768 | tf_op jit(solution)/shard_map/all_to_all | solution.py:116
  16.3 17.1 %copy-start.18 = (pred[1024]{0:T(1024)(128)(4,1)}, pred[1024]{0:T(1024)(128)(4,1)S(1)}, u32[]{:S(2)}) copy-start(pred[1024]{0:T(1024)(128)(4,1)S(1)} %compare_and_fusion) | copy-start | bytes 3076
  17.7 5.4 %copy-start.1 = (bf16[512,1024]{1,0:T(8,128)(2,1)S(1)}, bf16[512,1024]{1,0:T(8,128)(2,1)}, u32[]{:S(2)}) copy-start(bf16[512,1024]{1,0:T(8,128)(2,1)} %param.25) | copy-start | bytes 3145732
  28.5 8.9 %copy-start.19 = (pred[1024]{0:T(1024)(128)(4,1)}, pred[1024]{0:T(1024)(128)(4,1)S(1)}, u32[]{:S(2)}) copy-start(pred[1024]{0:T(1024)(128)(4,1)S(1)} %lt.76) | copy-start | bytes 3076
  28.6 8.9 %all-to-all-start.2 = ((bf16[16,8,128]{2,0,1:T(8,128)(2,1)}), bf16[16,8,128]{2,0,1:T(8,128)(2,1)S(1)}, u32[]{:S(2)}, u32[]{:S(2)}) async-start(bf16[16,8,128]{2,0,1:T(8,128)(2,1)} %copy_bitcast_fusion.1), calls=%async_computation.2 | async-start | bytes 65536 | tf_op jit(solution)/shard_map/all_to_all | solution.py:74
  37.5 120.8 %copy-start.13 = (bf16[16,8,128]{2,0,1:T(8,128)(2,1)}, bf16[16,8,128]{2,0,1:T(8,128)(2,1)S(1)}, u32[]{:S(2)}) copy-start(bf16[16,8,128]{2,0,1:T(8,128)(2,1)S(1)} %all-to-all-done.2) | copy-start | bytes 98308
  37.5 66.8 %copy-start.22 = (s32[1,32]{1,0:T(1,128)S(1)}, s32[1,32]{1,0:T(1,128)}, u32[]{:S(2)}) copy-start(s32[1,32]{1,0:T(1,128)} %param.31) | copy-start | bytes 388
  37.5 68.2 %copy-start.5 = (s32[1,32]{1,0:T(1,128)S(1)}, s32[1,32]{1,0:T(1,128)}, u32[]{:S(2)}) copy-start(s32[1,32]{1,0:T(1,128)} %param.32) | copy-start | bytes 388
  37.5 69.0 %copy-start.17 = (bf16[16,1024]{1,0:T(8,128)(2,1)S(1)}, bf16[16,1024]{1,0:T(8,128)(2,1)}, u32[]{:S(2)}) copy-start(bf16[16,1024]{1,0:T(8,128)(2,1)} %param.30) | copy-start | bytes 98308
  37.5 69.9 %copy-start.6 = (bf16[512,128]{1,0:T(8,128)(2,1)S(1)}, bf16[512,128]{1,0:T(8,128)(2,1)}, u32[]{:S(2)}) copy-start(bf16[512,128]{1,0:T(8,128)(2,1)} %param.26) | copy-start | bytes 393220
  98.4 55.1 %all-to-all-start.5 = ((bf16[32,32,1024]{2,1,0:T(8,128)(2,1)}), bf16[32,32,1024]{2,1,0:T(8,128)(2,1)}, u32[]{:S(2)}, u32[]{:S(2)}) async-start(bf16[32,32,1024]{2,1,0:T(8,128)(2,1)} %bitcast.374), calls=%async_computation.5 | async-start | bytes 4194304 | tf_op jit(solution)/shard_map/all_to_all | solution.py:115
  107.4 5.1 %copy-start.12 = (bf16[512,128]{1,0:T(8,128)(2,1)S(1)}, bf16[512,128]{1,0:T(8,128)(2,1)}, u32[]{:S(2)}) copy-start(bf16[512,128]{1,0:T(8,128)(2,1)} %param.27) | copy-start | bytes 393220
  109.1 3.4 copy-start.2
  153.5 13.3 %all-to-all-start.6 = ((bf16[16,8,128]{2,0,1:T(8,128)(2,1)}), bf16[16,8,128]{2,0,1:T(8,128)(2,1)S(1)}, u32[]{:S(2)}, u32[]{:S(2)}) async-start(bf16[16,8,128]{2,0,1:T(8,128)(2,1)} %copy_bitcast_fusion), calls=%async_computation.6 | async-start | bytes 65536 | tf_op jit(solution)/shard_map/all_to_all | solution.py:75
  174.3 15.7 %all-to-all-start.7 = ((f32[32,1,256]{2,1,0:T(1,128)}), f32[32,1,256]{2,1,0:T(1,128)S(1)}, u32[]{:S(2)}, u32[]{:S(2)}) async-start(f32[32,1,256]{2,1,0:T(1,128)} %reshape.787), calls=%async_computation.7 | async-start | bytes 65536 | tf_op jit(solution)/shard_map/all_to_all | solution.py:142
  190.0 45.2 %all-to-all-start.4 = ((f32[32,1,256]{2,1,0:T(1,128)}), f32[32,1,256]{2,1,0:T(1,128)S(1)}, u32[]{:S(2)}, u32[]{:S(2)}) async-start(f32[32,1,256]{2,1,0:T(1,128)} %reshape.791), calls=%async_computation.4 | async-start | bytes 65536 | tf_op jit(solution)/shard_map/all_to_all | solution.py:139
  234.3 22.8 %copy-start.20 = (pred[512]{0:T(512)(128)(4,1)}, pred[512]{0:T(512)(128)(4,1)S(1)}, u32[]{:S(2)}) copy-start(pred[512]{0:T(512)(128)(4,1)S(1)} %get-tuple-element.85) | copy-start | bytes 1540
  235.2 19.6 %all-to-all-start.3 = ((f32[32,1,256]{2,1,0:T(1,128)}), f32[32,1,256]{2,1,0:T(1,128)S(1)}, u32[]{:S(2)}, u32[]{:S(2)}) async-start(f32[32,1,256]{2,1,0:T(1,128)} %reshape.789), calls=%async_computation.3 | async-start | bytes 65536 | tf_op jit(solution)/shard_map/all_to_all | solution.py:136
  245.0 12.0 %copy-start.15 = (s32[1024]{0:T(1024)}, s32[1024]{0:T(1024)S(1)}, u32[]{:S(2)}) copy-start(s32[1024]{0:T(1024)S(1)} %pad_clamp_fusion) | copy-start | bytes 12292
  257.1 4.3 %copy-start.8 = (f32[512,8]{0,1:T(8,128)}, f32[512,8]{0,1:T(8,128)S(1)}, u32[]{:S(2)}) copy-start(f32[512,8]{0,1:T(8,128)S(1)} %get-tuple-element.89) | copy-start | bytes 49156
  257.1 4.3 %copy-start.10 = (f32[512,8]{0,1:T(8,128)}, f32[512,8]{0,1:T(8,128)S(1)}, u32[]{:S(2)}) copy-start(f32[512,8]{0,1:T(8,128)S(1)} %get-tuple-element.90) | copy-start | bytes 49156
  269.5 14.9 %all-to-all-start.9 = ((f32[32,1,256]{2,1,0:T(1,128)}), f32[32,1,256]{2,1,0:T(1,128)S(1)}, u32[]{:S(2)}, u32[]{:S(2)}) async-start(f32[32,1,256]{2,1,0:T(1,128)} %reshape.793), calls=%async_computation.9 | async-start | bytes 65536 | tf_op jit(solution)/shard_map/all_to_all | solution.py:159
  284.4 13.6 %all-to-all-start.8 = ((f32[32,1,256]{2,1,0:T(1,128)}), f32[32,1,256]{2,1,0:T(1,128)S(1)}, u32[]{:S(2)}, u32[]{:S(2)}) async-start(f32[32,1,256]{2,1,0:T(1,128)} %reshape.795), calls=%async_computation.8 | async-start | bytes 65536 | tf_op jit(solution)/shard_map/all_to_all | solution.py:158
  299.0 7.6 %copy-start.14 = (bf16[16,8,128]{2,0,1:T(8,128)(2,1)S(1)}, bf16[16,8,128]{2,0,1:T(8,128)(2,1)}, u32[]{:S(2)}) copy-start(bf16[16,8,128]{2,0,1:T(8,128)(2,1)} %copy-done.13) | copy-start | bytes 98308
  305.2 1.4 copy-start.3
  313.0 9.2 %copy-start.9 = (f32[512,8]{0,1:T(8,128)S(1)}, f32[512,8]{0,1:T(8,128)}, u32[]{:S(2)}) copy-start(f32[512,8]{0,1:T(8,128)} %copy-done.8) | copy-start | bytes 49156
  313.0 9.2 %copy-start.11 = (f32[512,8]{0,1:T(8,128)S(1)}, f32[512,8]{0,1:T(8,128)}, u32[]{:S(2)}) copy-start(f32[512,8]{0,1:T(8,128)} %copy-done.10) | copy-start | bytes 49156
  317.2 50.6 %all-to-all-start.10 = ((bf16[32,32,1024]{2,1,0:T(8,128)(2,1)}), bf16[32,32,1024]{2,1,0:T(8,128)(2,1)}, u32[]{:S(2)}, u32[]{:S(2)}) async-start(bf16[32,32,1024]{2,1,0:T(8,128)(2,1)} %reshape.540), calls=%async_computation.10 | async-start | bytes 4194304 | tf_op jit(solution)/shard_map/all_to_all | solution.py:175
  322.2 9.6 %copy-start.7 = (bf16[512,128]{1,0:T(8,128)(2,1)S(1)}, bf16[512,128]{1,0:T(8,128)(2,1)}, u32[]{:S(2)}) copy-start(bf16[512,128]{1,0:T(8,128)(2,1)} %param.26) | copy-start | bytes 393220
  329.7 2.1 copy-start.4
  358.5 9.3 %copy-start.16 = (s32[1024]{0:T(1024)S(1)}, s32[1024]{0:T(1024)}, u32[]{:S(2)}) copy-start(s32[1024]{0:T(1024)} %copy-done.15) | copy-start | bytes 12292
  367.8 4.6 %copy-start.21 = (pred[512]{0:T(512)(128)(4,1)S(1)}, pred[512]{0:T(512)(128)(4,1)}, u32[]{:S(2)}) copy-start(pred[512]{0:T(512)(128)(4,1)} %copy-done.20) | copy-start | bytes 1540
where the time goes:
time: 378 us; the launch traced here: 375 us
  local copies, waits for them, and re-layouts  77.9 us (21%)
  other arithmetic  69.8 us (18%)
  waiting for transfers between devices  67.7 us (18%)
  blocking collectives  60.9 us (16%)
  starting transfers between devices  60.4 us (16%)
  matrix products  37.4 us (10%)
    all_to_all x1, blocking collectives, per_device(): lax.all_to_all(pack(queries), 'dp', split_axis=0, concat_axis=0, tiled=True)  60.9 us
    and x1, other arithmetic, unpack(): jnp.take(values.reshape(peers * span, values.shape[-1]), home_place, axis=0)  40.4 us
    all_to_all x1, waiting for transfers between devices, per_device(): lax.all_to_all(pack(output_cotangent), 'dp', split_axis=0, concat_axis=0,...  31.7 us
    unnamed x60, local copies, waits for them, and re-layouts  20.6 us
    gather x4, local copies, waits for them, and re-layouts, pack(): taken = jnp.take(values, picked, axis=0)  18.8 us
    another operation x4, other arithmetic  13.7 us
    all_to_all x1, starting transfers between devices, per_device(): lax.all_to_all(seen_blocks.astype(jnp.bfloat16), 'dp', split_axis=0, conc...  11.5 us
    all_to_all x1, starting transfers between devices, per_device(): lax.all_to_all(top_far.reshape(peers, span, heads_local), 'dp', split_axi...  9.77 us
  transfers between devices with their start and end apart: 10, of which 6 were waited for; matrix products, arithmetic and copies ran while one was open for 34% of the time, Pallas kernels for 0%

commit v1 on v0

v1 whole, which is shorter than its diff:
```python
import functools
import math

import jax
import jax.numpy as jnp
from jax import lax
from jax.experimental import pallas as pl
from jax.experimental.pallas import tpu as pltpu
from jax.sharding import PartitionSpec as P

QUERY_HEADS = 64
KEY_VALUE_HEADS = 8
HEAD_DIMENSION = 128
GROUP = QUERY_HEADS // KEY_VALUE_HEADS
PROMPT = 128
SPAN = 32
WINDOW = 48
NY = 4
NZ = 8
HEADS = 8

far_below = -1e30
scale = 1.0 / math.sqrt(HEAD_DIMENSION)
exp2_scale = scale * math.log2(math.e)


def one_hot(shape, token_dim, offset, length):
    token = lax.broadcasted_iota(jnp.int32, shape, token_dim)
    place = lax.broadcasted_iota(jnp.int32, shape, 1 - token_dim)
    hit = (place == token + offset) & (token < length)
    return jnp.where(hit, 1.0, 0.0).astype(jnp.bfloat16)


def dot(a, b, dims=((1,), (0,))):
    return lax.dot_general(a, b, (dims, ((), ())), preferred_element_type=jnp.float32)


def attend(n_groups, turns, *refs):
    own_y, lengths, owners, masks, query, cotangent, key, value = refs[:8]
    prompts = refs[8 : 8 + n_groups]
    dq, dk, dv = refs[8 + n_groups : 11 + n_groups]
    dprompts = refs[11 + n_groups : 11 + 2 * n_groups]
    first_of, count_of, mask_of = refs[11 + 2 * n_groups :]
    rows = query.shape[0]

    def place(s, start):
        owner = owners[0, s]
        first_of[owner] = start
        count_of[owner] = lengths[0, s]
        mask_of[owner] = masks[0, s]
        return start + lengths[0, s]

    lax.fori_loop(0, NY * NZ, place, jnp.int32(0))
    dq[...] = jnp.zeros_like(dq)
    dk[...] = jnp.zeros_like(dk)
    dv[...] = jnp.zeros_like(dv)

    key_at = lax.broadcasted_iota(jnp.int32, (SPAN, GROUP * SPAN), 0)
    token_at = lax.broadcasted_iota(jnp.int32, (SPAN, GROUP * SPAN), 1) % SPAN
    near_bias = jnp.where(key_at <= token_at, 0.0, far_below)

    def response(prompt, prompt_ref, dprompt_ref, z):
        start, length, seen = first_of[prompt], count_of[prompt], mask_of[prompt]
        base = pl.multiple_of(jnp.minimum((start // 16) * 16, rows - WINDOW), 16)
        window = pl.ds(base, WINDOW)
        pick = one_hot((SPAN, WINDOW), 0, start - base, length)

        def take(ref):
            return dot(pick, ref[window, :]).astype(jnp.bfloat16)

        def stack(rows_of):
            return jnp.concatenate(
                [rows_of[:, h * HEAD_DIMENSION : (h + 1) * HEAD_DIMENSION] for h in range(GROUP)],
                axis=0,
            )

        q = stack(take(query))
        g = stack(take(cotangent))
        far_k = prompt_ref[z, :, 0].reshape(PROMPT, HEAD_DIMENSION)
        far_v = prompt_ref[z, :, 1].reshape(PROMPT, HEAD_DIMENSION)
        k = jnp.concatenate([far_k, take(key)], axis=0)
        v = jnp.concatenate([far_v, take(value)], axis=0)
        scores = dot(k, q, ((1,), (1,)))
        dots = dot(v, g, ((1,), (1,)))
        far_bias = jnp.where(seen > 0, 0.0, far_below).astype(jnp.float32)
        scores = jnp.concatenate([scores[:PROMPT] + far_bias, scores[PROMPT:] + near_bias], axis=0)
        highest = jnp.max(scores, axis=0, keepdims=True)
        weights = jnp.exp2((scores - highest) * exp2_scale)
        total = jnp.sum(weights, axis=0, keepdims=True)
        inverse = 1.0 / total
        delta = jnp.sum(weights * dots, axis=0, keepdims=True) * inverse
        probs = weights * inverse
        slopes = (probs * (dots - delta)).astype(jnp.bfloat16)
        probs = probs.astype(jnp.bfloat16)
        k_grad = (dot(slopes, q) * scale).astype(jnp.bfloat16)
        v_grad = dot(probs, g).astype(jnp.bfloat16)
        q_grad = (dot(slopes, k, ((0,), (0,))) * scale).astype(jnp.bfloat16)
        dprompt_ref[z, :, :HEAD_DIMENSION] = k_grad[:PROMPT]
        dprompt_ref[z, :, HEAD_DIMENSION:] = v_grad[:PROMPT]
        q_rows = jnp.concatenate(
            [q_grad[h * SPAN : (h + 1) * SPAN] for h in range(GROUP)], axis=1
        )
        put = one_hot((WINDOW, SPAN), 1, start - base, length)

        def finish():
            for ref, grads in ((dq, q_rows), (dk, k_grad[PROMPT:]), (dv, v_grad[PROMPT:])):
                ref[window, :] = ref[window, :] + dot(put, grads).astype(jnp.bfloat16)

        return finish

    for group in range(n_groups):
        y = lax.rem(own_y[0] + turns[group], NY)

        def pair(i, carry):
            ends = []
            for j in range(2):
                z = 2 * i + j
                ends.append(response(z * NY + y, prompts[group], dprompts[group], z))
            for end in ends:
                end()
            return carry

        lax.fori_loop(0, NZ // 2, pair, 0)


def attention(own_y, lengths, owners, masks, query, cotangent, key, value, prompts, turns):
    n_groups = len(prompts)
    rows = query.shape[0]
    smem = pl.BlockSpec(memory_space=pltpu.SMEM)
    vmem = pl.BlockSpec(memory_space=pltpu.VMEM)
    grads = [jax.ShapeDtypeStruct(a.shape, jnp.bfloat16) for a in (query, key, value)]
    grads += [jax.ShapeDtypeStruct((NZ, PROMPT, 2 * HEAD_DIMENSION), jnp.bfloat16)] * n_groups
    return pl.pallas_call(
        functools.partial(attend, n_groups, turns),
        out_shape=grads,
        in_specs=[smem] * 4 + [vmem] * (4 + n_groups),
        out_specs=[vmem] * len(grads),
        scratch_shapes=[pltpu.SMEM((NY * NZ,), jnp.int32)] * 3,
        compiler_params=pltpu.CompilerParams(vmem_limit_bytes=40 * 1024 * 1024),
        cost_estimate=pl.CostEstimate(
            flops=n_groups * NZ * 10 * 160 * 256 * 128,
            bytes_accessed=4 * rows * 1024,
            transcendentals=n_groups * NZ * 160 * 256,
        ),
    )(own_y, lengths, owners, masks, query, cotangent, key, value, *prompts)


def along_y(turn):
    return [(z * NY + y, z * NY + (y + turn) % NY) for z in range(NZ) for y in range(NY)]


same_y_head = [[(z * NY + y) * HEADS + h for z in range(NZ) for h in range(HEADS)] for y in range(NY)]
same_y = [[z * NY + y for z in range(NZ)] for y in range(NY)]


def per_device(
    queries,
    response_keys,
    response_values,
    output_cotangent,
    prompt_key_rows,
    prompt_value_rows,
    resp_len,
    resp_owner,
    block_mask,
):
    part = prompt_key_rows.shape[0]
    mine = jnp.stack(
        [
            a.reshape(part, HEADS, HEAD_DIMENSION).transpose(1, 0, 2)
            for a in (prompt_key_rows, prompt_value_rows)
        ],
        axis=1,
    )
    mine = jnp.broadcast_to(mine[None], (NZ,) + mine.shape).reshape((NZ * HEADS,) + mine.shape[1:])
    column = lax.all_to_all(
        mine,
        ("dp", "head"),
        split_axis=0,
        concat_axis=0,
        axis_index_groups=same_y_head,
        tiled=True,
    ).reshape(NZ, HEADS, 2, part, HEAD_DIMENSION)
    turns = (0, 1, 3, 2)
    prompts = [column] + [lax.ppermute(column, "dp", along_y(NY - turn)) for turn in turns[1:]]
    own_y = lax.rem(lax.axis_index("dp"), NY).reshape(1).astype(jnp.int32)
    dq, dk, dv, *dprompts = attention(
        own_y,
        resp_len,
        resp_owner,
        block_mask.reshape(block_mask.shape[:2]),
        queries,
        output_cotangent,
        response_keys,
        response_values,
        prompts,
        turns,
    )
    parts = [dprompts[0]] + [
        lax.ppermute(a, "dp", along_y(turn)) for a, turn in zip(dprompts[1:], turns[1:])
    ]
    summed = sum(a.astype(jnp.float32) for a in parts).astype(jnp.bfloat16)
    shares = lax.all_to_all(
        summed, "dp", split_axis=0, concat_axis=0, axis_index_groups=same_y, tiled=True
    )
    whole = jnp.sum(shares.astype(jnp.float32), axis=0).astype(jnp.bfloat16)
    return (dq, dk, dv, whole[:, :HEAD_DIMENSION], whole[:, HEAD_DIMENSION:])


def solution(mesh):
    placed = (
        P("dp", "head"),
        P("dp", "head"),
        P("dp", "head"),
        P("dp", "head"),
        P(("dp", "head"), None),
        P(("dp", "head"), None),
        P("dp", None),
        P("dp", None),
        P("dp", None, None),
    )
    return jax.shard_map(
        per_device,
        mesh=mesh,
        in_specs=placed,
        out_specs=(
            P("dp", "head"),
            P("dp", "head"),
            P("dp", "head"),
            P("dp", "head"),
            P("dp", "head"),
        ),
        check_vma=False,
    )
```

time: 378 us -> 131 us (0.35)
  local copies, waits for them, and re-layouts: 77.9 us -> 4.24 us
  other arithmetic: 69.8 us -> 0.36 us
  starting transfers between devices: 60.4 us -> 10.5 us
  matrix products: 37.4 us -> 0 us
  waiting for transfers between devices: 67.7 us -> 43.6 us
  Pallas kernels: 0 us -> 22.1 us
  blocking collectives: 60.9 us -> 49 us
    all_to_all x10 -> x0, waiting for transfers between devices: 67.7 us -> none  [the longest x1 31.7 us: per_device(): lax.all_to_all(pack(output_cotangent), 'dp', split_axis=0, concat_axis=0,...]
    all_to_all x10 -> x0, starting transfers between devices: 60.4 us -> none  [the longest x1 11.5 us: per_device(): lax.all_to_all(seen_blocks.astype(jnp.bfloat16), 'dp', split_axis=0, conc...]
    ppermute x0 -> x6, waiting for transfers between devices: none -> 43.6 us  [the longest x3 23.1 us: per_device(): lax.ppermute(a, 'dp', along_y(turn))]
    and x4 -> x0, other arithmetic: 40.7 us -> none  [the longest x1 40.4 us: unpack(): jnp.take(values.reshape(peers * span, values.shape[-1]), home_place, axis=0)]
    dot_general x10 -> x0, matrix products: 37.4 us -> none  [the longest x1 6.62 us: per_device(): jnp.einsum('qhgd,khd->qhgk', far_grads, owned_values, preferred_element_t...]
    gather x15 -> x0, local copies, waits for them, and re-layouts: 29.6 us -> none  [the longest x4 18.8 us: pack(): taken = jnp.take(values, picked, axis=0)]
    pallas_call x0 -> x1, Pallas kernels: none -> 22.1 us  [attention(): pl.pallas_call(functools.partial(attend, n_groups, turns), out_shape=grad...]
    unnamed x60 -> x16, local copies, waits for them, and re-layouts: 20.6 us -> 3.52 us
  transfers between devices with their start and end apart: 10 -> 6, of which waited for: 6 -> 6; matrix products, arithmetic and copies ran while one was open for 34% -> 0% of each run, Pallas kernels for 0% -> 0%
where the time goes in v1:
time: 131 us
  blocking collectives  49 us (37%)
  waiting for transfers between devices  43.6 us (33%)
  Pallas kernels  22.1 us (17%)
  starting transfers between devices  10.5 us (8%)
  local copies, waits for them, and re-layouts  4.24 us (3%)
    all_to_all x1, blocking collectives, per_device(): lax.all_to_all(mine, ('dp', 'head'), split_axis=0, concat_axis=0, axis_in...  29.5 us
    ppermute x3, waiting for transfers between devices, per_device(): lax.ppermute(a, 'dp', along_y(turn))  23.1 us
    pallas_call x1, Pallas kernels, attention(): pl.pallas_call(functools.partial(attend, n_groups, turns), out_shape=grad...  22.1 us
    ppermute x3, waiting for transfers between devices, per_device(): lax.ppermute(column, 'dp', along_y(NY - turn))  20.5 us
    all_to_all x1, blocking collectives, per_device(): lax.all_to_all(summed, 'dp', split_axis=0, concat_axis=0, axis_index_grou...  19.5 us
    ppermute x3, starting transfers between devices, per_device(): lax.ppermute(column, 'dp', along_y(NY - turn))  6.43 us
    ppermute x3, starting transfers between devices, per_device(): lax.ppermute(a, 'dp', along_y(turn))  4.09 us
    unnamed x16, local copies, waits for them, and re-layouts  3.52 us
  transfers between devices with their start and end apart: 6, of which 6 were waited for; matrix products, arithmetic and copies ran while one was open for 0% of the time, Pallas kernels for 0%

profile of v1, /device:TPU:2, one launch (start us, length us, event | category | flops | bytes accessed | tf_op | source)
XLA Modules:
  0.0 130.5 jit_solution(12303364720073338756)
XLA Ops:
  0.6 0.0 copy-start
  0.6 0.9 copy.15
  1.5 0.8 copy.16
  2.3 0.1 broadcast_in_dim.2
  2.4 0.0 copy-start.2
  2.4 0.0 copy-start.3
  2.4 29.5 %all_to_all.10 = bf16[64,2,16,128]{3,2,1,0:T(8,128)(2,1)S(1)} all-to-all(bf16[64,2,16,128]{3,2,1,0:T(8,128)(2,1)S(1)} %bitcast.21), channel_id=1, replica_groups={{0,1,2,3,4,5,6,7,32,33,34,35,36,37,38,39,64,65,66,67,68,69,70,71,96,97,..., dimensions={0} | all-to-all | bytes 1048576 | tf_op jit(solution)/shard_map/all_to_all | solution.py:176
  31.9 3.2 %collective-permute-start.2 = (bf16[8,8,2,16,128]{4,3,2,1,0:T(8,128)(2,1)S(1)}, bf16[8,8,2,16,128]{4,3,2,1,0:T(8,128)(2,1)S(1)}, u32[]{:S(2)}, u32[]{:S(2)}) collective-permute-start(bf16[8,8,2,16,128]{4,3,2,1,0:T(8,128)(2,1)S(1)} %bitcast.16), channel_id=1, source_target_pairs={{0,16},{8,24},{16,0},{24,8},{32,48},{40,56},{48,32},{56,40},{64,80... | collective-permute-start | bytes 1572872 | tf_op jit(solution)/shard_map/ppermute | solution.py:185
  35.1 0.7 collective-permute-start.1
  35.8 2.6 %collective-permute-start = (bf16[8,8,2,16,128]{4,3,2,1,0:T(8,128)(2,1)S(1)}, bf16[8,8,2,16,128]{4,3,2,1,0:T(8,128)(2,1)S(1)}, u32[]{:S(2)}, u32[]{:S(2)}) collective-permute-start(bf16[8,8,2,16,128]{4,3,2,1,0:T(8,128)(2,1)S(1)} %bitcast.18), channel_id=1, source_target_pairs={{0,24},{8,0},{16,8},{24,16},{32,56},{40,32},{48,40},{56,48},{64,88... | collective-permute-start | bytes 1572872 | tf_op jit(solution)/shard_map/ppermute | solution.py:185
  38.3 9.9 %collective-permute-done.2.refs_11_ = bf16[8,8,2,16,128]{4,3,2,1,0:T(8,128)(2,1)S(1)} collective-permute-done((bf16[8,8,2,16,128]{4,3,2,1,0:T(8,128)(2,1)S(1)}, bf16[8,8,2,16,128]{4,3,2,1,0:T(8,128)(2,1)S(1)}, u32[]{:S(2)}, u32[]{:S(2)}) %collective-permute-start.2) | collective-permute-done | bytes 524320 | tf_op jit(solution)/shard_map/ppermute | solution.py:185
  48.2 10.3 %collective-permute-done.1.refs_10_ = bf16[8,8,2,16,128]{4,3,2,1,0:T(8,128)(2,1)S(1)} collective-permute-done((bf16[8,8,2,16,128]{4,3,2,1,0:T(8,128)(2,1)S(1)}, bf16[8,8,2,16,128]{4,3,2,1,0:T(8,128)(2,1)S(1)}, u32[]{:S(2)}, u32[]{:S(2)}) %collective-permute-start.1) | collective-permute-done | bytes 524320 | tf_op jit(solution)/shard_map/ppermute | solution.py:185
  58.5 0.4 collective-permute-done.refs_9_
  58.9 0.0 copy-start.4
  58.9 0.0 copy-start.5
  58.9 0.0 copy-start.6
  58.9 0.0 copy-done
  58.9 0.0 copy-done.2
  58.9 0.0 copy-done.3
  58.9 0.6 copy-done.4
  59.5 0.0 copy-done.5
  59.6 0.0 copy-done.6
  59.6 0.0 copy-start.1
  59.6 1.2 copy-done.1
  60.8 22.1 %shard_map.128 = (bf16[512,1024]{1,0:T(8,128)(2,1)}, bf16[512,128]{1,0:T(8,128)(2,1)}, bf16[512,128]{1,0:T(8,128)(2,1)}, bf16[8,128,256]{2,1,0:T(8,128)(2,1)S(1)...) custom-call(s32[1]{0:T(128)} %bitcast.refs_0_, ...), custom_call_target="tpu_custom_call" | custom-call | flops 1677721600 | bytes 2097152 | tf_op jit(solution)/shard_map/pallas_call | solution.py:133
  82.9 1.4 %collective-permute-start.3 = (bf16[8,128,256]{2,1,0:T(8,128)(2,1)S(1)}, bf16[8,128,256]{2,1,0:T(8,128)(2,1)S(1)}, u32[]{:S(2)}, u32[]{:S(2)}) collective-permute-start(bf16[8,128,256]{2,1,0:T(8,128)(2,1)S(1)} %get-tuple-element.16), channel_id=1, source_target_pairs={{0,8},{8,16},{16,24},{24,0},{32,40},{40,48},{48,56},{56,32},{64,72... | collective-permute-start | bytes 1572872 | tf_op jit(solution)/shard_map/ppermute | solution.py:200
  84.2 1.9 %collective-permute-start.4 = (bf16[8,128,256]{2,1,0:T(8,128)(2,1)S(1)}, bf16[8,128,256]{2,1,0:T(8,128)(2,1)S(1)}, u32[]{:S(2)}, u32[]{:S(2)}) collective-permute-start(bf16[8,128,256]{2,1,0:T(8,128)(2,1)S(1)} %get-tuple-element.17), channel_id=1, source_target_pairs={{0,24},{8,0},{16,8},{24,16},{32,56},{40,32},{48,40},{56,48},{64,88... | collective-permute-start | bytes 1572872 | tf_op jit(solution)/shard_map/ppermute | solution.py:200
  86.1 0.9 collective-permute-start.5
  87.0 10.6 %collective-permute-done.3 = bf16[8,128,256]{2,1,0:T(8,128)(2,1)S(1)} collective-permute-done((bf16[8,128,256]{2,1,0:T(8,128)(2,1)S(1)}, bf16[8,128,256]{2,1,0:T(8,128)(2,1)S(1)}, u32[]{:S(2)}, u32[]{:S(2)}) %collective-permute-start.3) | collective-permute-done | bytes 524320 | tf_op jit(solution)/shard_map/ppermute | solution.py:200
  97.6 1.5 %collective-permute-done.4 = bf16[8,128,256]{2,1,0:T(8,128)(2,1)S(1)} collective-permute-done((bf16[8,128,256]{2,1,0:T(8,128)(2,1)S(1)}, bf16[8,128,256]{2,1,0:T(8,128)(2,1)S(1)}, u32[]{:S(2)}, u32[]{:S(2)}) %collective-permute-start.4) | collective-permute-done | bytes 524320 | tf_op jit(solution)/shard_map/ppermute | solution.py:200
  99.1 10.9 %collective-permute-done.5 = bf16[8,128,256]{2,1,0:T(8,128)(2,1)S(1)} collective-permute-done((bf16[8,128,256]{2,1,0:T(8,128)(2,1)S(1)}, bf16[8,128,256]{2,1,0:T(8,128)(2,1)S(1)}, u32[]{:S(2)}, u32[]{:S(2)}) %collective-permute-start.5) | collective-permute-done | bytes 524320 | tf_op jit(solution)/shard_map/ppermute | solution.py:200
  110.0 0.3 add_convert_fusion
  110.3 19.5 %all_to_all.11 = bf16[8,128,256]{2,1,0:T(8,128)(2,1)S(1)} all-to-all(bf16[8,128,256]{2,1,0:T(8,128)(2,1)S(1)} %add_convert_fusion), channel_id=1, replica_groups={{0,32,64,96,128,160,192,224},{8,40,72,104,136,168,200,232},{16,48,80,11..., dimensions={0} | all-to-all | bytes 1048576 | tf_op jit(solution)/shard_map/all_to_all | solution.py:203
  129.8 0.1 reduce_sum.12
  129.9 0.6 fusion
  (2 shorter events, 0.0 us)
Async XLA Ops:
  0.6 58.3 %copy-start = (bf16[512,1024]{1,0:T(8,128)(2,1)S(1)}, bf16[512,1024]{1,0:T(8,128)(2,1)}, u32[]{:S(2)}) copy-start(bf16[512,1024]{1,0:T(8,128)(2,1)} %refs_4_.1) | copy-start | bytes 3145732
  2.4 56.5 %copy-start.2 = (bf16[512,128]{1,0:T(8,128)(2,1)S(1)}, bf16[512,128]{1,0:T(8,128)(2,1)}, u32[]{:S(2)}) copy-start(bf16[512,128]{1,0:T(8,128)(2,1)} %refs_6_.1) | copy-start | bytes 393220
  2.4 56.5 %copy-start.3 = (bf16[512,128]{1,0:T(8,128)(2,1)S(1)}, bf16[512,128]{1,0:T(8,128)(2,1)}, u32[]{:S(2)}) copy-start(bf16[512,128]{1,0:T(8,128)(2,1)} %refs_7_.1) | copy-start | bytes 393220
  31.9 16.3 %collective-permute-start.2 = (bf16[8,8,2,16,128]{4,3,2,1,0:T(8,128)(2,1)S(1)}, bf16[8,8,2,16,128]{4,3,2,1,0:T(8,128)(2,1)S(1)}, u32[]{:S(2)}, u32[]{:S(2)}) collective-permute-start(bf16[8,8,2,16,128]{4,3,2,1,0:T(8,128)(2,1)S(1)} %bitcast.16), channel_id=1, source_target_pairs={{0,16},{8,24},{16,0},{24,8},{32,48},{40,56},{48,32},{56,40},{64,80... | collective-permute-start | bytes 1572872 | tf_op jit(solution)/shard_map/ppermute | solution.py:185
  35.1 23.4 %collective-permute-start.1 = (bf16[8,8,2,16,128]{4,3,2,1,0:T(8,128)(2,1)S(1)}, bf16[8,8,2,16,128]{4,3,2,1,0:T(8,128)(2,1)S(1)}, u32[]{:S(2)}, u32[]{:S(2)}) collective-permute-start(bf16[8,8,2,16,128]{4,3,2,1,0:T(8,128)(2,1)S(1)} %bitcast.17), channel_id=1, source_target_pairs={{0,8},{8,16},{16,24},{24,0},{32,40},{40,48},{48,56},{56,32},{64,72... | collective-permute-start | bytes 1572872 | tf_op jit(solution)/shard_map/ppermute | solution.py:185
  35.8 23.1 %collective-permute-start = (bf16[8,8,2,16,128]{4,3,2,1,0:T(8,128)(2,1)S(1)}, bf16[8,8,2,16,128]{4,3,2,1,0:T(8,128)(2,1)S(1)}, u32[]{:S(2)}, u32[]{:S(2)}) collective-permute-start(bf16[8,8,2,16,128]{4,3,2,1,0:T(8,128)(2,1)S(1)} %bitcast.18), channel_id=1, source_target_pairs={{0,24},{8,0},{16,8},{24,16},{32,56},{40,32},{48,40},{56,48},{64,88... | collective-permute-start | bytes 1572872 | tf_op jit(solution)/shard_map/ppermute | solution.py:185
  58.9 0.7 copy-start.4
  58.9 0.7 copy-start.5
  58.9 0.7 copy-start.6
  59.6 1.2 copy-start.1
  82.9 14.7 %collective-permute-start.3 = (bf16[8,128,256]{2,1,0:T(8,128)(2,1)S(1)}, bf16[8,128,256]{2,1,0:T(8,128)(2,1)S(1)}, u32[]{:S(2)}, u32[]{:S(2)}) collective-permute-start(bf16[8,128,256]{2,1,0:T(8,128)(2,1)S(1)} %get-tuple-element.16), channel_id=1, source_target_pairs={{0,8},{8,16},{16,24},{24,0},{32,40},{40,48},{48,56},{56,32},{64,72... | collective-permute-start | bytes 1572872 | tf_op jit(solution)/shard_map/ppermute | solution.py:200
  84.2 14.9 %collective-permute-start.4 = (bf16[8,128,256]{2,1,0:T(8,128)(2,1)S(1)}, bf16[8,128,256]{2,1,0:T(8,128)(2,1)S(1)}, u32[]{:S(2)}, u32[]{:S(2)}) collective-permute-start(bf16[8,128,256]{2,1,0:T(8,128)(2,1)S(1)} %get-tuple-element.17), channel_id=1, source_target_pairs={{0,24},{8,0},{16,8},{24,16},{32,56},{40,32},{48,40},{56,48},{64,88... | collective-permute-start | bytes 1572872 | tf_op jit(solution)/shard_map/ppermute | solution.py:200
  86.1 23.9 %collective-permute-start.5 = (bf16[8,128,256]{2,1,0:T(8,128)(2,1)S(1)}, bf16[8,128,256]{2,1,0:T(8,128)(2,1)S(1)}, u32[]{:S(2)}, u32[]{:S(2)}) collective-permute-start(bf16[8,128,256]{2,1,0:T(8,128)(2,1)S(1)} %get-tuple-element.18), channel_id=1, source_target_pairs={{0,16},{8,24},{16,0},{24,8},{32,48},{40,56},{48,32},{56,40},{64,80... | collective-permute-start | bytes 1572872 | tf_op jit(solution)/shard_map/ppermute | solution.py:200

commit v2 on v1

v2 whole, which is shorter than its diff:
```python
import functools
import math

import jax
import jax.numpy as jnp
from jax import lax
from jax.experimental import pallas as pl
from jax.experimental.pallas import tpu as pltpu
from jax.sharding import PartitionSpec as P

QUERY_HEADS = 64
KEY_VALUE_HEADS = 8
HEAD_DIMENSION = 128
GROUP = QUERY_HEADS // KEY_VALUE_HEADS
PROMPT = 128
SPAN = 32
WINDOW = 48
NY = 4
NZ = 8
HEADS = 8

far_below = -1e30
scale = 1.0 / math.sqrt(HEAD_DIMENSION)
exp2_scale = scale * math.log2(math.e)


def one_hot(shape, token_dim, offset, length):
    token = lax.broadcasted_iota(jnp.int32, shape, token_dim)
    place = lax.broadcasted_iota(jnp.int32, shape, 1 - token_dim)
    hit = (place == token + offset) & (token < length)
    return jnp.where(hit, 1.0, 0.0).astype(jnp.bfloat16)


def dot(a, b, dims=((1,), (0,))):
    return lax.dot_general(a, b, (dims, ((), ())), preferred_element_type=jnp.float32)


def locate(lengths, owners, masks, first_of, count_of, mask_of):
    def place(s, start):
        owner = owners[0, s]
        first_of[owner] = start
        count_of[owner] = lengths[0, s]
        if mask_of is not None:
            mask_of[owner] = masks[0, s]
        return start + lengths[0, s]

    lax.fori_loop(0, NY * NZ, place, jnp.int32(0))


def window_of(start, rows):
    base = pl.multiple_of(jnp.minimum((start // 16) * 16, rows - WINDOW), 16)
    return pl.ds(base, WINDOW), start - base


def pack(turns, own_y, lengths, owners, query, cotangent, key, value, *refs):
    n = len(turns)
    wide, near = refs[:n], refs[n : 2 * n]
    first_of, count_of = refs[2 * n :]
    locate(lengths, owners, None, first_of, count_of, None)
    rows = query.shape[0]
    for turn, wide_ref, near_ref in zip(turns, wide, near):
        y = lax.rem(own_y[0] + turn, NY)

        def one(z, carry):
            prompt = z * NY + y
            start = first_of[prompt]
            window, offset = window_of(start, rows)
            pick = one_hot((SPAN, WINDOW), 0, offset, count_of[prompt])
            for j, ref in enumerate((query, cotangent)):
                taken = dot(pick, ref[window, :]).astype(jnp.bfloat16)
                for h in range(GROUP):
                    wide_ref[z, j, h * SPAN : (h + 1) * SPAN, :] = taken[
                        :, h * HEAD_DIMENSION : (h + 1) * HEAD_DIMENSION
                    ]
            for j, ref in enumerate((key, value)):
                near_ref[z, j] = dot(pick, ref[window, :]).astype(jnp.bfloat16)
            return carry

        lax.fori_loop(0, NZ, one, 0, unroll=2)


def unpack(turns, own_y, lengths, owners, *refs):
    n = len(turns)
    wide, near = refs[:n], refs[n : 2 * n]
    dq, dk, dv, first_of, count_of = refs[2 * n :]
    locate(lengths, owners, None, first_of, count_of, None)
    rows = dq.shape[0]
    dq[...] = jnp.zeros_like(dq)
    dk[...] = jnp.zeros_like(dk)
    dv[...] = jnp.zeros_like(dv)
    for turn, wide_ref, near_ref in zip(turns, wide, near):
        y = lax.rem(own_y[0] + turn, NY)

        def one(z, carry):
            prompt = z * NY + y
            window, offset = window_of(first_of[prompt], rows)
            put = one_hot((WINDOW, SPAN), 1, offset, count_of[prompt])
            grads = jnp.concatenate(
                [wide_ref[z, h * SPAN : (h + 1) * SPAN, :] for h in range(GROUP)], axis=1
            )
            dq[window, :] = dq[window, :] + dot(put, grads).astype(jnp.bfloat16)
            for j, ref in enumerate((dk, dv)):
                ref[window, :] = ref[window, :] + dot(put, near_ref[z, j]).astype(jnp.bfloat16)
            return carry

        lax.fori_loop(0, NZ, one, 0, unroll=2)


def attend(turn, n_parts, *refs):
    own_y, owners, masks, wide, near = refs[:5]
    prompts = refs[5 : 5 + n_parts]
    dq, dnear, dprompt, mask_of = refs[5 + n_parts :]
    y = lax.rem(own_y[0] + turn, NY)

    def place(s, carry):
        mask_of[owners[0, s]] = masks[0, s]
        return carry

    lax.fori_loop(0, NY * NZ, place, 0)
    key_at = lax.broadcasted_iota(jnp.int32, (SPAN, GROUP * SPAN), 0)
    token_at = lax.broadcasted_iota(jnp.int32, (SPAN, GROUP * SPAN), 1) % SPAN
    near_bias = jnp.where(key_at <= token_at, 0.0, far_below)

    def response(z, prompt_ref, z_in):
        q, g = wide[z, 0], wide[z, 1]
        k = jnp.concatenate([prompt_ref[z_in, :, 0].reshape(PROMPT, HEAD_DIMENSION), near[z, 0]])
        v = jnp.concatenate([prompt_ref[z_in, :, 1].reshape(PROMPT, HEAD_DIMENSION), near[z, 1]])
        scores = dot(k, q, ((1,), (1,)))
        dots = dot(v, g, ((1,), (1,)))
        far_bias = jnp.where(mask_of[z * NY + y] > 0, 0.0, far_below).astype(jnp.float32)
        scores = jnp.concatenate([scores[:PROMPT] + far_bias, scores[PROMPT:] + near_bias], axis=0)
        highest = jnp.max(scores, axis=0, keepdims=True)
        weights = jnp.exp2((scores - highest) * exp2_scale)
        inverse = 1.0 / jnp.sum(weights, axis=0, keepdims=True)
        delta = jnp.sum(weights * dots, axis=0, keepdims=True) * inverse
        probs = weights * inverse
        slopes = (probs * (dots - delta)).astype(jnp.bfloat16)
        probs = probs.astype(jnp.bfloat16)
        k_grad = (dot(slopes, q) * scale).astype(jnp.bfloat16)
        v_grad = dot(probs, g).astype(jnp.bfloat16)
        dq[z] = (dot(slopes, k, ((0,), (0,))) * scale).astype(jnp.bfloat16)
        dprompt[z, :, :HEAD_DIMENSION] = k_grad[:PROMPT]
        dprompt[z, :, HEAD_DIMENSION:] = v_grad[:PROMPT]
        dnear[z, 0] = k_grad[PROMPT:]
        dnear[z, 1] = v_grad[PROMPT:]

    per_part = NZ // n_parts
    for part, prompt_ref in enumerate(prompts):

        def pair(i, carry):
            for j in range(2):
                response(part * per_part + 2 * i + j, prompt_ref, 2 * i + j)
            return carry

        lax.fori_loop(0, per_part // 2, pair, 0)


smem = pl.BlockSpec(memory_space=pltpu.SMEM)
vmem = pl.BlockSpec(memory_space=pltpu.VMEM)


def shaped(*shape):
    return jax.ShapeDtypeStruct(shape, jnp.bfloat16)


def call(body, outs, n_smem, n_vmem, n_scratch, flops, moved):
    return pl.pallas_call(
        body,
        out_shape=outs,
        in_specs=[smem] * n_smem + [vmem] * n_vmem,
        out_specs=[vmem] * len(outs),
        scratch_shapes=[pltpu.SMEM((NY * NZ,), jnp.int32)] * n_scratch,
        compiler_params=pltpu.CompilerParams(vmem_limit_bytes=24 * 1024 * 1024),
        cost_estimate=pl.CostEstimate(flops=flops, bytes_accessed=moved, transcendentals=0),
    )


def pack_call(turns, *args):
    n = len(turns)
    outs = [shaped(NZ, 2, GROUP * SPAN, HEAD_DIMENSION)] * n
    outs += [shaped(NZ, 2, SPAN, HEAD_DIMENSION)] * n
    got = call(functools.partial(pack, turns), outs, 3, 4, 2, 10**9, 8 * 2**20)(*args)
    return got[:n], got[n:]


def unpack_call(turns, own_y, lengths, owners, wide, near, rows):
    outs = [shaped(rows, GROUP * HEAD_DIMENSION)] + [shaped(rows, HEAD_DIMENSION)] * 2
    body = functools.partial(unpack, turns)
    return call(body, outs, 3, 2 * len(turns), 2, 10**9, 4 * 2**20)(
        own_y, lengths, owners, *wide, *near
    )


def attend_call(turn, own_y, owners, masks, wide, near, prompts):
    outs = [
        shaped(NZ, GROUP * SPAN, HEAD_DIMENSION),
        shaped(NZ, 2, SPAN, HEAD_DIMENSION),
        shaped(NZ, PROMPT, 2 * HEAD_DIMENSION),
    ]
    body = functools.partial(attend, turn, len(prompts))
    return call(body, outs, 3, 2 + len(prompts), 1, 3 * 10**9, 4 * 2**20)(
        own_y, owners, masks, wide, near, *prompts
    )


def along_y(turn):
    return [(z * NY + y, z * NY + (y + turn) % NY) for z in range(NZ) for y in range(NY)]


same_y_head = [[(z * NY + y) * HEADS + h for z in range(NZ) for h in range(HEADS)] for y in range(NY)]
same_y = [[z * NY + y for z in range(NZ)] for y in range(NY)]


def per_device(
    queries,
    response_keys,
    response_values,
    output_cotangent,
    prompt_key_rows,
    prompt_value_rows,
    resp_len,
    resp_owner,
    block_mask,
):
    part = prompt_key_rows.shape[0]
    mine = jnp.stack(
        [
            a.reshape(part, HEADS, HEAD_DIMENSION).transpose(1, 0, 2)
            for a in (prompt_key_rows, prompt_value_rows)
        ],
        axis=1,
    )
    mine = jnp.broadcast_to(mine[None], (NZ,) + mine.shape).reshape((NZ * HEADS,) + mine.shape[1:])
    column = lax.all_to_all(
        mine,
        ("dp", "head"),
        split_axis=0,
        concat_axis=0,
        axis_index_groups=same_y_head,
        tiled=True,
    ).reshape(NZ, HEADS, 2, part, HEAD_DIMENSION)
    turns = (0, 1, 3, 2)
    own_y = lax.rem(lax.axis_index("dp"), NY).reshape(1).astype(jnp.int32)
    masks = block_mask.reshape(block_mask.shape[:2])
    wide, near = pack_call(
        turns, own_y, resp_len, resp_owner, queries, output_cotangent, response_keys, response_values
    )
    after = lax.ppermute(column, "dp", along_y(-1))
    before = lax.ppermute(column, "dp", along_y(1))
    half = NZ // 2
    across = [
        lax.ppermute(after[:half], "dp", along_y(-1)),
        lax.ppermute(before[half:], "dp", along_y(1)),
    ]
    dq, dnear, parts = [], [], []
    for turn, a, b, prompts in zip(turns, wide, near, ([column], [after], [before], across)):
        q_part, near_part, prompt_part = attend_call(turn, own_y, resp_owner, masks, a, b, prompts)
        dq.append(q_part)
        dnear.append(near_part)
        parts.append(lax.ppermute(prompt_part, "dp", along_y(turn)) if turn else prompt_part)
    dq, dk, dv = unpack_call(turns, own_y, resp_len, resp_owner, dq, dnear, queries.shape[0])
    summed = sum(a.astype(jnp.float32) for a in parts).astype(jnp.bfloat16)
    shares = lax.all_to_all(
        summed, "dp", split_axis=0, concat_axis=0, axis_index_groups=same_y, tiled=True
    )
    whole = jnp.sum(shares.astype(jnp.float32), axis=0).astype(jnp.bfloat16)
    return (dq, dk, dv, whole[:, :HEAD_DIMENSION], whole[:, HEAD_DIMENSION:])


def solution(mesh):
    placed = (
        P("dp", "head"),
        P("dp", "head"),
        P("dp", "head"),
        P("dp", "head"),
        P(("dp", "head"), None),
        P(("dp", "head"), None),
        P("dp", None),
        P("dp", None),
        P("dp", None, None),
    )
    return jax.shard_map(
        per_device,
        mesh=mesh,
        in_specs=placed,
        out_specs=(
            P("dp", "head"),
            P("dp", "head"),
            P("dp", "head"),
            P("dp", "head"),
            P("dp", "head"),
        ),
        check_vma=False,
    )
```

time: 131 us -> 106 us (0.81)
  blocking collectives: 49 us -> 29.5 us
  waiting for transfers between devices: 43.6 us -> 28.8 us
  starting transfers between devices: 10.5 us -> 15.3 us
  Pallas kernels: 22.1 us -> 25.7 us
    ppermute x6 -> x7, waiting for transfers between devices: 43.6 us -> 20.1 us  [the longest x3 15.2 us: per_device(): lax.ppermute(prompt_part, 'dp', along_y(turn))]
    all_to_all x1 -> x0, blocking collectives: 19.5 us -> none  [per_device(): lax.all_to_all(summed, 'dp', split_axis=0, concat_axis=0, axis_index_grou...]
    all_to_all x0 -> x1, waiting for transfers between devices: none -> 8.68 us  [per_device(): lax.all_to_all(summed, 'dp', split_axis=0, concat_axis=0, axis_index_grou...]
    pallas_call x1 -> x6, Pallas kernels: 22.1 us -> 25.7 us  [the longest x4 15.7 us: attend_call(): call(body, outs, 3, 2 + len(prompts), 1, 3 * 10 ** 9, 4 * 2 ** 20)]
    all_to_all x0 -> x1, starting transfers between devices: none -> 3.49 us  [per_device(): lax.all_to_all(summed, 'dp', split_axis=0, concat_axis=0, axis_index_grou...]
    ppermute x6 -> x7, starting transfers between devices: 10.5 us -> 11.8 us  [the longest x3 4.92 us: per_device(): lax.ppermute(prompt_part, 'dp', along_y(turn))]
  transfers between devices with their start and end apart: 6 -> 8, of which waited for: 6 -> 3; matrix products, arithmetic and copies ran while one was open for 0% -> 0% of each run, Pallas kernels for 0% -> 24%
where the time goes in v2:
time: 106 us
  blocking collectives  29.5 us (28%)
  waiting for transfers between devices  28.8 us (27%)
  Pallas kernels  25.7 us (24%)
  starting transfers between devices  15.3 us (14%)
  local copies, waits for them, and re-layouts  4.91 us (5%)
  other arithmetic  1.18 us (1%)
    all_to_all x1, blocking collectives, per_device(): lax.all_to_all(mine, ('dp', 'head'), split_axis=0, concat_axis=0, axis_in...  29.5 us
    pallas_call x4, Pallas kernels, attend_call(): call(body, outs, 3, 2 + len(prompts), 1, 3 * 10 ** 9, 4 * 2 ** 20)  15.7 us
    ppermute x3, waiting for transfers between devices, per_device(): lax.ppermute(prompt_part, 'dp', along_y(turn))  15.2 us
    all_to_all x1, waiting for transfers between devices, per_device(): lax.all_to_all(summed, 'dp', split_axis=0, concat_axis=0, axis_index_grou...  8.68 us
    pallas_call x1, Pallas kernels, unpack_call(): call(body, outs, 3, 2 * len(turns), 2, 10 ** 9, 4 * 2 ** 20)  5.42 us
    ppermute x1, waiting for transfers between devices, per_device(): after = lax.ppermute(column, 'dp', along_y(-1))  4.92 us
    ppermute x3, starting transfers between devices, per_device(): lax.ppermute(prompt_part, 'dp', along_y(turn))  4.92 us
    pallas_call x1, Pallas kernels, pack_call(): call(functools.partial(pack, turns), outs, 3, 4, 2, 10 ** 9, 8 * 2 ** 20)  4.54 us
  transfers between devices with their start and end apart: 8, of which 3 were waited for; matrix products, arithmetic and copies ran while one was open for 0% of the time, Pallas kernels for 24%

profile of v2, /device:TPU:2, one launch (start us, length us, event | category | flops | bytes accessed | tf_op | source)
XLA Modules:
  0.0 106.1 jit_solution(11132176839077328012)
XLA Ops:
  0.6 0.0 copy-start
  0.6 0.9 copy.16
  1.5 0.8 copy.15
  2.3 0.1 broadcast_in_dim.2
  2.4 0.0 copy-start.2
  2.4 0.0 copy-start.3
  2.4 29.5 %all_to_all.10 = bf16[64,2,16,128]{3,2,1,0:T(8,128)(2,1)S(1)} all-to-all(bf16[64,2,16,128]{3,2,1,0:T(8,128)(2,1)S(1)} %bitcast.23), channel_id=1, replica_groups={{0,1,2,3,4,5,6,7,32,33,34,35,36,37,38,39,64,65,66,67,68,69,70,71,96,97,..., dimensions={0} | all-to-all | bytes 1048576 | tf_op jit(solution)/shard_map/all_to_all | solution.py:234
  31.9 3.0 %collective-permute-start = (bf16[8,8,2,16,128]{4,3,2,1,0:T(8,128)(2,1)S(1)}, bf16[8,8,2,16,128]{4,3,2,1,0:T(8,128)(2,1)S(1)}, u32[]{:S(2)}, u32[]{:S(2)}) collective-permute-start(bf16[8,8,2,16,128]{4,3,2,1,0:T(8,128)(2,1)S(1)} %bitcast.16), channel_id=1, source_target_pairs={{0,24},{8,0},{16,8},{24,16},{32,56},{40,32},{48,40},{56,48},{64,88... | collective-permute-start | bytes 1572872 | tf_op jit(solution)/shard_map/ppermute | solution.py:248
  34.9 0.0 collective-permute-start.1
  34.9 0.0 copy-start.5
  34.9 0.0 copy-start.6
  34.9 0.0 copy-done
  34.9 0.0 copy-done.2
  34.9 0.0 copy-done.3
  35.0 0.6 copy-done.5
  35.6 0.0 copy-done.6
  35.6 0.0 copy-start.1
  35.6 1.2 %copy-done.1 = bf16[512,1024]{1,0:T(8,128)(2,1)S(1)} copy-done((bf16[512,1024]{1,0:T(8,128)(2,1)S(1)}, bf16[512,1024]{1,0:T(8,128)(2,1)}, u32[]{:S(2)}) %copy-start.1) | copy-done | bytes 1048600
  36.8 4.5 %shard_map.128 = (bf16[8,2,256,128]{3,2,1,0:T(8,128)(2,1)S(1)}, bf16[8,2,256,128]{3,2,1,0:T(8,128)(2,1)S(1)}, bf16[8,2,256,128]{3,2,1,0:T(8,128)(2,1)S(1)}, bf16...) custom-call(s32[1]{0:T(128)} %bitcast.own_y.refs_0_, ...), custom_call_target="tpu_custom_call" | custom-call | flops 1000000000 | bytes 8388608 | tf_op jit(solution)/shard_map/pallas_call | solution.py:182
  41.4 4.9 %collective-permute-done.refs_5_ = bf16[8,8,2,16,128]{4,3,2,1,0:T(8,128)(2,1)S(1)} collective-permute-done((bf16[8,8,2,16,128]{4,3,2,1,0:T(8,128)(2,1)S(1)}, bf16[8,8,2,16,128]{4,3,2,1,0:T(8,128)(2,1)S(1)}, u32[]{:S(2)}, u32[]{:S(2)}) %collective-permute-start) | collective-permute-done | bytes 524320 | tf_op jit(solution)/shard_map/ppermute | solution.py:248
  46.3 3.8 %collective-permute-start.2 = (bf16[4,8,2,16,128]{4,3,2,1,0:T(8,128)(2,1)S(1)}, bf16[4,8,2,16,128]{4,3,2,1,0:T(8,128)(2,1)S(1)}, u32[]{:S(2)}, u32[]{:S(2)}) collective-permute-start(bf16[4,8,2,16,128]{4,3,2,1,0:T(8,128)(2,1)S(1)} %slice.16), channel_id=1, source_target_pairs={{0,24},{8,0},{16,8},{24,16},{32,56},{40,32},{48,40},{56,48},{64,88... | collective-permute-start | bytes 786440 | tf_op jit(solution)/shard_map/ppermute | solution.py:252
  50.1 0.0 collective-permute-done.1.refs_5_
  50.1 0.1 collective-permute-start.3
  50.2 0.0 copy-start.4
  50.2 0.6 copy-done.4
  50.9 3.9 %shard_map.131 = (bf16[8,256,128]{2,1,0:T(8,128)(2,1)S(1)}, bf16[8,2,32,128]{3,2,1,0:T(8,128)(2,1)S(1)}, bf16[8,128,256]{2,1,0:T(8,128)(2,1)S(1)}) custom-call(s32[1]{0:T(128)} %bitcast.own_y.refs_0_, s32[1,32]{1,0:T(1,128)S(1)} %copy-done.6, s32[1,32]{1,0:T(1,128)S(1)} %bitcast.19, bf16[8,2,256,128]{3,2,1,0:T(8,128)(2,1)S(1)} %get-tuple-element.34.refs_3_, ...), custom_call_target="tpu_custom_call" | custom-call | flops 3000000000 | bytes 4194304 | tf_op jit(solution)/shard_map/pallas_call | solution.py:201
  54.8 3.3 %collective-permute-start.5 = (bf16[8,128,256]{2,1,0:T(8,128)(2,1)S(1)}, bf16[8,128,256]{2,1,0:T(8,128)(2,1)S(1)}, u32[]{:S(2)}, u32[]{:S(2)}) collective-permute-start(bf16[8,128,256]{2,1,0:T(8,128)(2,1)S(1)} %get-tuple-element.49), channel_id=1, source_target_pairs={{0,24},{8,0},{16,8},{24,16},{32,56},{40,32},{48,40},{56,48},{64,88... | collective-permute-start | bytes 1572872 | tf_op jit(solution)/shard_map/ppermute | solution.py:260
  58.1 3.9 %shard_map.130 = (bf16[8,256,128]{2,1,0:T(8,128)(2,1)S(1)}, bf16[8,2,32,128]{3,2,1,0:T(8,128)(2,1)S(1)}, bf16[8,128,256]{2,1,0:T(8,128)(2,1)S(1)}) custom-call(s32[1]{0:T(128)} %bitcast.own_y.refs_0_, s32[1,32]{1,0:T(1,128)S(1)} %copy-done.6, s32[1,32]{1,0:T(1,128)S(1)} %bitcast.20, bf16[8,2,256,128]{3,2,1,0:T(8,128)(2,1)S(1)} %get-tuple-element.31.refs_3_, ...), custom_call_target="tpu_custom_call" | custom-call | flops 3000000000 | bytes 4194304 | tf_op jit(solution)/shard_map/pallas_call | solution.py:201
  62.0 0.1 collective-permute-start.4
  62.1 0.0 collective-permute-done.2.refs_5_
  62.1 0.0 collective-permute-done.3.refs_6_
  62.1 3.9 %shard_map.132 = (bf16[8,256,128]{2,1,0:T(8,128)(2,1)S(1)}, bf16[8,2,32,128]{3,2,1,0:T(8,128)(2,1)S(1)}, bf16[8,128,256]{2,1,0:T(8,128)(2,1)S(1)}) custom-call(s32[1]{0:T(128)} %bitcast.own_y.refs_0_, s32[1,32]{1,0:T(1,128)S(1)} %copy-done.6, s32[1,32]{1,0:T(1,128)S(1)} %bitcast.21, bf16[8,2,256,128]{3,2,1,0:T(8,128)(2,1)S(1)} %get-tuple-element.37.refs_3_, ...), custom_call_target="tpu_custom_call" | custom-call | flops 3000000000 | bytes 4194304 | tf_op jit(solution)/shard_map/pallas_call | solution.py:201
  66.1 1.5 %collective-permute-start.6 = (bf16[8,128,256]{2,1,0:T(8,128)(2,1)S(1)}, bf16[8,128,256]{2,1,0:T(8,128)(2,1)S(1)}, u32[]{:S(2)}, u32[]{:S(2)}) collective-permute-start(bf16[8,128,256]{2,1,0:T(8,128)(2,1)S(1)} %get-tuple-element.50), channel_id=1, source_target_pairs={{0,16},{8,24},{16,0},{24,8},{32,48},{40,56},{48,32},{56,40},{64,80... | collective-permute-start | bytes 1572872 | tf_op jit(solution)/shard_map/ppermute | solution.py:260
  67.6 3.9 %shard_map.129 = (bf16[8,256,128]{2,1,0:T(8,128)(2,1)S(1)}, bf16[8,2,32,128]{3,2,1,0:T(8,128)(2,1)S(1)}, bf16[8,128,256]{2,1,0:T(8,128)(2,1)S(1)}) custom-call(s32[1]{0:T(128)} %bitcast.own_y.refs_0_, s32[1,32]{1,0:T(1,128)S(1)} %copy-done.6, s32[1,32]{1,0:T(1,128)S(1)} %bitcast.22, bf16[8,2,256,128]{3,2,1,0:T(8,128)(2,1)S(1)} %get-tuple-element.28.refs_3_, ...), custom_call_target="tpu_custom_call" | custom-call | flops 3000000000 | bytes 4194304 | tf_op jit(solution)/shard_map/pallas_call | solution.py:201
  71.5 0.0 collective-permute-done.5
  71.5 15.2 %collective-permute-done.4 = bf16[8,128,256]{2,1,0:T(8,128)(2,1)S(1)} collective-permute-done((bf16[8,128,256]{2,1,0:T(8,128)(2,1)S(1)}, bf16[8,128,256]{2,1,0:T(8,128)(2,1)S(1)}, u32[]{:S(2)}, u32[]{:S(2)}) %collective-permute-start.4) | collective-permute-done | bytes 524320 | tf_op jit(solution)/shard_map/ppermute | solution.py:260
  86.7 0.0 collective-permute-done.6
  86.7 1.1 %add_convert_fusion = bf16[8,128,256]{2,1,0:T(8,128)(2,1)} fusion(bf16[8,128,256]{2,1,0:T(8,128)(2,1)S(1)} %collective-permute-done.6, bf16[8,128,256]{2,1,0:T(8,128)(2,1)S(1)} %collective-permute-done.5, bf16[8,128,256]{2,1,0:T(8,128)(2,1)S(1)} %collective-permute-done.4, bf16[8,128,256]{2,1,0:T(8,128)(2,1)S(1)} %get-tuple-element.47), kind=kLoop, calls=%fused_computation | loop fusion | flops 2097152 | bytes 2621440 | tf_op jit(solution)/shard_map/convert_element_type | solution.py:262
  87.8 3.5 %all-to-all-start.1 = ((bf16[8,128,256]{2,1,0:T(8,128)(2,1)}), bf16[8,128,256]{2,1,0:T(8,128)(2,1)S(1)}, u32[]{:S(2)}, u32[]{:S(2)}) async-start(bf16[8,128,256]{2,1,0:T(8,128)(2,1)} %add_convert_fusion), calls=%async_computation.1 | async-start | bytes 1048576 | tf_op jit(solution)/shard_map/all_to_all | solution.py:263
  91.3 5.4 %shard_map.133 = (bf16[512,1024]{1,0:T(8,128)(2,1)}, bf16[512,128]{1,0:T(8,128)(2,1)}, bf16[512,128]{1,0:T(8,128)(2,1)}) custom-call(s32[1]{0:T(128)} %bitcast.own_y.refs_0_, s32[1,32]{1,0:T(1,128)S(1)} %copy-done.5, s32[1,32]{1,0:T(1,128)S(1)} %copy-done.6, bf16[8,256,128]{2,1,0:T(8,128)(2,1)S(1)} %get-tuple-element.30.refs_0_, ...), custom_call_target="tpu_custom_call" | custom-call | flops 1000000000 | bytes 4194304 | tf_op jit(solution)/shard_map/pallas_call | solution.py:189
  96.7 8.7 %all-to-all-done.1 = bf16[8,128,256]{2,1,0:T(8,128)(2,1)S(1)} async-done(((bf16[8,128,256]{2,1,0:T(8,128)(2,1)}), bf16[8,128,256]{2,1,0:T(8,128)(2,1)S(1)}, u32[]{:S(2)}, u32[]{:S(2)}) %all-to-all-start.1) | async-done | bytes 524320 | tf_op jit(solution)/shard_map/all_to_all | solution.py:263
  105.4 0.1 reduce_sum.12
  105.5 0.6 fusion
  (4 shorter events, 0.1 us)
Async XLA Ops:
  0.6 34.3 %copy-start = (bf16[512,1024]{1,0:T(8,128)(2,1)S(1)}, bf16[512,1024]{1,0:T(8,128)(2,1)}, u32[]{:S(2)}) copy-start(bf16[512,1024]{1,0:T(8,128)(2,1)} %query.1) | copy-start | bytes 3145732
  2.4 32.6 %copy-start.2 = (bf16[512,128]{1,0:T(8,128)(2,1)S(1)}, bf16[512,128]{1,0:T(8,128)(2,1)}, u32[]{:S(2)}) copy-start(bf16[512,128]{1,0:T(8,128)(2,1)} %key.1) | copy-start | bytes 393220
  2.4 32.6 %copy-start.3 = (bf16[512,128]{1,0:T(8,128)(2,1)S(1)}, bf16[512,128]{1,0:T(8,128)(2,1)}, u32[]{:S(2)}) copy-start(bf16[512,128]{1,0:T(8,128)(2,1)} %value.1) | copy-start | bytes 393220
  31.9 14.4 %collective-permute-start = (bf16[8,8,2,16,128]{4,3,2,1,0:T(8,128)(2,1)S(1)}, bf16[8,8,2,16,128]{4,3,2,1,0:T(8,128)(2,1)S(1)}, u32[]{:S(2)}, u32[]{:S(2)}) collective-permute-start(bf16[8,8,2,16,128]{4,3,2,1,0:T(8,128)(2,1)S(1)} %bitcast.16), channel_id=1, source_target_pairs={{0,24},{8,0},{16,8},{24,16},{32,56},{40,32},{48,40},{56,48},{64,88... | collective-permute-start | bytes 1572872 | tf_op jit(solution)/shard_map/ppermute | solution.py:248
  34.9 15.2 %collective-permute-start.1 = (bf16[8,8,2,16,128]{4,3,2,1,0:T(8,128)(2,1)S(1)}, bf16[8,8,2,16,128]{4,3,2,1,0:T(8,128)(2,1)S(1)}, u32[]{:S(2)}, u32[]{:S(2)}) collective-permute-start(bf16[8,8,2,16,128]{4,3,2,1,0:T(8,128)(2,1)S(1)} %bitcast.17), channel_id=1, source_target_pairs={{0,8},{8,16},{16,24},{24,0},{32,40},{40,48},{48,56},{56,32},{64,72... | collective-permute-start | bytes 1572872 | tf_op jit(solution)/shard_map/ppermute | solution.py:249
  34.9 0.7 copy-start.5
  34.9 0.7 copy-start.6
  35.6 1.2 %copy-start.1 = (bf16[512,1024]{1,0:T(8,128)(2,1)S(1)}, bf16[512,1024]{1,0:T(8,128)(2,1)}, u32[]{:S(2)}) copy-start(bf16[512,1024]{1,0:T(8,128)(2,1)} %cotangent.1) | copy-start | bytes 3145732
  46.3 15.8 %collective-permute-start.2 = (bf16[4,8,2,16,128]{4,3,2,1,0:T(8,128)(2,1)S(1)}, bf16[4,8,2,16,128]{4,3,2,1,0:T(8,128)(2,1)S(1)}, u32[]{:S(2)}, u32[]{:S(2)}) collective-permute-start(bf16[4,8,2,16,128]{4,3,2,1,0:T(8,128)(2,1)S(1)} %slice.16), channel_id=1, source_target_pairs={{0,24},{8,0},{16,8},{24,16},{32,56},{40,32},{48,40},{56,48},{64,88... | collective-permute-start | bytes 786440 | tf_op jit(solution)/shard_map/ppermute | solution.py:252
  50.1 12.0 %collective-permute-start.3 = (bf16[4,8,2,16,128]{4,3,2,1,0:T(8,128)(2,1)S(1)}, bf16[4,8,2,16,128]{4,3,2,1,0:T(8,128)(2,1)S(1)}, u32[]{:S(2)}, u32[]{:S(2)}) collective-permute-start(bf16[4,8,2,16,128]{4,3,2,1,0:T(8,128)(2,1)S(1)} %slice.17), channel_id=1, source_target_pairs={{0,8},{8,16},{16,24},{24,0},{32,40},{40,48},{48,56},{56,32},{64,72... | collective-permute-start | bytes 786440 | tf_op jit(solution)/shard_map/ppermute | solution.py:253
  50.2 0.7 copy-start.4
  54.8 16.8 %collective-permute-start.5 = (bf16[8,128,256]{2,1,0:T(8,128)(2,1)S(1)}, bf16[8,128,256]{2,1,0:T(8,128)(2,1)S(1)}, u32[]{:S(2)}, u32[]{:S(2)}) collective-permute-start(bf16[8,128,256]{2,1,0:T(8,128)(2,1)S(1)} %get-tuple-element.49), channel_id=1, source_target_pairs={{0,24},{8,0},{16,8},{24,16},{32,56},{40,32},{48,40},{56,48},{64,88... | collective-permute-start | bytes 1572872 | tf_op jit(solution)/shard_map/ppermute | solution.py:260
  62.0 24.7 %collective-permute-start.4 = (bf16[8,128,256]{2,1,0:T(8,128)(2,1)S(1)}, bf16[8,128,256]{2,1,0:T(8,128)(2,1)S(1)}, u32[]{:S(2)}, u32[]{:S(2)}) collective-permute-start(bf16[8,128,256]{2,1,0:T(8,128)(2,1)S(1)} %get-tuple-element.48), channel_id=1, source_target_pairs={{0,8},{8,16},{16,24},{24,0},{32,40},{40,48},{48,56},{56,32},{64,72... | collective-permute-start | bytes 1572872 | tf_op jit(solution)/shard_map/ppermute | solution.py:260
  66.1 20.6 %collective-permute-start.6 = (bf16[8,128,256]{2,1,0:T(8,128)(2,1)S(1)}, bf16[8,128,256]{2,1,0:T(8,128)(2,1)S(1)}, u32[]{:S(2)}, u32[]{:S(2)}) collective-permute-start(bf16[8,128,256]{2,1,0:T(8,128)(2,1)S(1)} %get-tuple-element.50), channel_id=1, source_target_pairs={{0,16},{8,24},{16,0},{24,8},{32,48},{40,56},{48,32},{56,40},{64,80... | collective-permute-start | bytes 1572872 | tf_op jit(solution)/shard_map/ppermute | solution.py:260
  87.8 17.6 %all-to-all-start.1 = ((bf16[8,128,256]{2,1,0:T(8,128)(2,1)}), bf16[8,128,256]{2,1,0:T(8,128)(2,1)S(1)}, u32[]{:S(2)}, u32[]{:S(2)}) async-start(bf16[8,128,256]{2,1,0:T(8,128)(2,1)} %add_convert_fusion), calls=%async_computation.1 | async-start | bytes 1048576 | tf_op jit(solution)/shard_map/all_to_all | solution.py:263

commit v3 on v2

--- a/solution.py
+++ b/solution.py
@@ -79,8 +79,8 @@
         lax.fori_loop(0, NZ, one, 0, unroll=2)
 
 
-def unpack(turns, own_y, lengths, owners, *refs):
-    n = len(turns)
+def unpack(pieces, own_y, lengths, owners, *refs):
+    n = len(pieces)
     wide, near = refs[:n], refs[n : 2 * n]
     dq, dk, dv, first_of, count_of = refs[2 * n :]
     locate(lengths, owners, None, first_of, count_of, None)
@@ -88,43 +88,41 @@
     dq[...] = jnp.zeros_like(dq)
     dk[...] = jnp.zeros_like(dk)
     dv[...] = jnp.zeros_like(dv)
-    for turn, wide_ref, near_ref in zip(turns, wide, near):
+    for (turn, first), wide_ref, near_ref in zip(pieces, wide, near):
         y = lax.rem(own_y[0] + turn, NY)
 
-        def one(z, carry):
-            prompt = z * NY + y
+        def one(i, carry):
+            prompt = (first + i) * NY + y
             window, offset = window_of(first_of[prompt], rows)
             put = one_hot((WINDOW, SPAN), 1, offset, count_of[prompt])
             grads = jnp.concatenate(
-                [wide_ref[z, h * SPAN : (h + 1) * SPAN, :] for h in range(GROUP)], axis=1
+                [wide_ref[i, h * SPAN : (h + 1) * SPAN, :] for h in range(GROUP)], axis=1
             )
             dq[window, :] = dq[window, :] + dot(put, grads).astype(jnp.bfloat16)
             for j, ref in enumerate((dk, dv)):
-                ref[window, :] = ref[window, :] + dot(put, near_ref[z, j]).astype(jnp.bfloat16)
+                ref[window, :] = ref[window, :] + dot(put, near_ref[i, j]).astype(jnp.bfloat16)
             return carry
 
-        lax.fori_loop(0, NZ, one, 0, unroll=2)
-
-
-def attend(turn, n_parts, *refs):
-    own_y, owners, masks, wide, near = refs[:5]
-    prompts = refs[5 : 5 + n_parts]
-    dq, dnear, dprompt, mask_of = refs[5 + n_parts :]
+        lax.fori_loop(0, wide_ref.shape[0], one, 0, unroll=2)
+
+
+def attend(turn, first, *refs):
+    own_y, owners, masks, wide, near, prompts, dq, dnear, dprompt, mask_of = refs
     y = lax.rem(own_y[0] + turn, NY)
 
     def place(s, carry):
         mask_of[owners[0, s]] = masks[0, s]
         return carry
 
-    lax.fori_loop(0, NY * NZ, place, 0)
+    lax.fori_loop(0, NY * NZ, place, 0, unroll=4)
     key_at = lax.broadcasted_iota(jnp.int32, (SPAN, GROUP * SPAN), 0)
     token_at = lax.broadcasted_iota(jnp.int32, (SPAN, GROUP * SPAN), 1) % SPAN
     near_bias = jnp.where(key_at <= token_at, 0.0, far_below)
-
-    def response(z, prompt_ref, z_in):
+    for i in range(prompts.shape[0]):
+        z = first + i
         q, g = wide[z, 0], wide[z, 1]
-        k = jnp.concatenate([prompt_ref[z_in, :, 0].reshape(PROMPT, HEAD_DIMENSION), near[z, 0]])
-        v = jnp.concatenate([prompt_ref[z_in, :, 1].reshape(PROMPT, HEAD_DIMENSION), near[z, 1]])
+        k = jnp.concatenate([prompts[i, :, 0].reshape(PROMPT, HEAD_DIMENSION), near[z, 0]])
+        v = jnp.concatenate([prompts[i, :, 1].reshape(PROMPT, HEAD_DIMENSION), near[z, 1]])
         scores = dot(k, q, ((1,), (1,)))
         dots = dot(v, g, ((1,), (1,)))
         far_bias = jnp.where(mask_of[z * NY + y] > 0, 0.0, far_below).astype(jnp.float32)
@@ -138,21 +136,20 @@
         probs = probs.astype(jnp.bfloat16)
         k_grad = (dot(slopes, q) * scale).astype(jnp.bfloat16)
         v_grad = dot(probs, g).astype(jnp.bfloat16)
-        dq[z] = (dot(slopes, k, ((0,), (0,))) * scale).astype(jnp.bfloat16)
-        dprompt[z, :, :HEAD_DIMENSION] = k_grad[:PROMPT]
-        dprompt[z, :, HEAD_DIMENSION:] = v_grad[:PROMPT]
-        dnear[z, 0] = k_grad[PROMPT:]
-        dnear[z, 1] = v_grad[PROMPT:]
-
-    per_part = NZ // n_parts
-    for part, prompt_ref in enumerate(prompts):
-
-        def pair(i, carry):
-            for j in range(2):
-                response(part * per_part + 2 * i + j, prompt_ref, 2 * i + j)
-            return carry
-
-        lax.fori_loop(0, per_part // 2, pair, 0)
+        dq[i] = (dot(slopes, k, ((0,), (0,))) * scale).astype(jnp.bfloat16)
+        dprompt[i, :, :HEAD_DIMENSION] = k_grad[:PROMPT]
+        dprompt[i, :, HEAD_DIMENSION:] = v_grad[:PROMPT]
+        dnear[i, 0] = k_grad[PROMPT:]
+        dnear[i, 1] = v_grad[PROMPT:]
+
+
+def spread(keys, values, out):
+    part = keys.shape[0]
+    for h in range(HEADS):
+        for j, ref in enumerate((keys, values)):
+            rows = ref[:, h * HEAD_DIMENSION : (h + 1) * HEAD_DIMENSION]
+            for z in range(NZ):
+                out[z * HEADS + h, j] = rows
 
 
 smem = pl.BlockSpec(memory_space=pltpu.SMEM)
@@ -183,24 +180,30 @@
     return got[:n], got[n:]
 
 
-def unpack_call(turns, own_y, lengths, owners, wide, near, rows):
+def unpack_call(pieces, own_y, lengths, owners, wide, near, rows):
     outs = [shaped(rows, GROUP * HEAD_DIMENSION)] + [shaped(rows, HEAD_DIMENSION)] * 2
-    body = functools.partial(unpack, turns)
-    return call(body, outs, 3, 2 * len(turns), 2, 10**9, 4 * 2**20)(
+    body = functools.partial(unpack, pieces)
+    return call(body, outs, 3, 2 * len(pieces), 2, 10**9, 4 * 2**20)(
         own_y, lengths, owners, *wide, *near
     )
 
 
-def attend_call(turn, own_y, owners, masks, wide, near, prompts):
+def attend_call(turn, first, own_y, owners, masks, wide, near, prompts):
+    n = prompts.shape[0]
     outs = [
-        shaped(NZ, GROUP * SPAN, HEAD_DIMENSION),
-        shaped(NZ, 2, SPAN, HEAD_DIMENSION),
-        shaped(NZ, PROMPT, 2 * HEAD_DIMENSION),
+        shaped(n, GROUP * SPAN, HEAD_DIMENSION),
+        shaped(n, 2, SPAN, HEAD_DIMENSION),
+        shaped(n, PROMPT, 2 * HEAD_DIMENSION),
     ]
-    body = functools.partial(attend, turn, len(prompts))
-    return call(body, outs, 3, 2 + len(prompts), 1, 3 * 10**9, 4 * 2**20)(
-        own_y, owners, masks, wide, near, *prompts
-    )
+    body = functools.partial(attend, turn, first)
+    return call(body, outs, 3, 3, 1, 4 * 10**8 * n, 2**19 * n)(
+        own_y, owners, masks, wide, near, prompts
+    )
+
+
+def spread_call(keys, values):
+    out = shaped(NZ * HEADS, 2, keys.shape[0], HEAD_DIMENSION)
+    return call(spread, [out], 0, 2, 0, 0, 2**19)(keys, values)[0]
 
 
 def along_y(turn):
@@ -223,16 +226,9 @@
     block_mask,
 ):
     part = prompt_key_rows.shape[0]
-    mine = jnp.stack(
-        [
-            a.reshape(part, HEADS, HEAD_DIMENSION).transpose(1, 0, 2)
-            for a in (prompt_key_rows, prompt_value_rows)
-        ],
-        axis=1,
-    )
-    mine = jnp.broadcast_to(mine[None], (NZ,) + mine.shape).reshape((NZ * HEADS,) + mine.shape[1:])
+    half = NZ // 2
     column = lax.all_to_all(
-        mine,
+        spread_call(prompt_key_rows, prompt_value_rows),
         ("dp", "head"),
         split_axis=0,
         concat_axis=0,
@@ -245,21 +241,38 @@
     wide, near = pack_call(
         turns, own_y, resp_len, resp_owner, queries, output_cotangent, response_keys, response_values
     )
-    after = lax.ppermute(column, "dp", along_y(-1))
-    before = lax.ppermute(column, "dp", along_y(1))
-    half = NZ // 2
+    halves = (column[:half], column[half:])
+    after = [lax.ppermute(a, "dp", along_y(-1)) for a in halves]
+    before = [lax.ppermute(a, "dp", along_y(1)) for a in halves]
+    after, before = lax.optimization_barrier((after, before))
     across = [
-        lax.ppermute(after[:half], "dp", along_y(-1)),
-        lax.ppermute(before[half:], "dp", along_y(1)),
+        lax.ppermute(after[0], "dp", along_y(-1)),
+        lax.ppermute(before[1], "dp", along_y(1)),
     ]
-    dq, dnear, parts = [], [], []
-    for turn, a, b, prompts in zip(turns, wide, near, ([column], [after], [before], across)):
-        q_part, near_part, prompt_part = attend_call(turn, own_y, resp_owner, masks, a, b, prompts)
+    pieces = (
+        [(1, 0, after[0]), (3, 0, before[0]), (1, half, after[1]), (3, half, before[1])]
+        + [(2, 0, across[0]), (2, half, across[1])]
+        + [(0, 0, column)]
+    )
+    place = {turn: i for i, turn in enumerate(turns)}
+    dq, dnear, sums = [], [], [[], []]
+    for turn, first, prompts in pieces:
+        i = place[turn]
+        q_part, near_part, prompt_part = attend_call(
+            turn, first, own_y, resp_owner, masks, wide[i], near[i], prompts
+        )
         dq.append(q_part)
         dnear.append(near_part)
-        parts.append(lax.ppermute(prompt_part, "dp", along_y(turn)) if turn else prompt_part)
-    dq, dk, dv = unpack_call(turns, own_y, resp_len, resp_owner, dq, dnear, queries.shape[0])
-    summed = sum(a.astype(jnp.float32) for a in parts).astype(jnp.bfloat16)
+        if turn:
+            sums[first // half].append(lax.ppermute(prompt_part, "dp", along_y(turn)))
+        else:
+            sums[0].append(prompt_part[:half])
+            sums[1].append(prompt_part[half:])
+    dq, dk, dv = unpack_call(
+        [piece[:2] for piece in pieces], own_y, resp_len, resp_owner, dq, dnear, queries.shape[0]
+    )
+    summed = jnp.concatenate([sum(a.astype(jnp.float32) for a in part) for part in sums], axis=0)
+    summed, dq, dk, dv = lax.optimization_barrier((summed.astype(jnp.bfloat16), dq, dk, dv))
     shares = lax.all_to_all(
         summed, "dp", split_axis=0, concat_axis=0, axis_index_groups=same_y, tiled=True
     )

time: 106 us -> 105 us (level)
  the two profiles are of different devices: /device:TPU:2 before, /device:TPU:8 now
where the time goes in v3:
time: 105 us
  blocking collectives  48.6 us (46%)
  Pallas kernels  25.8 us (25%)
  starting transfers between devices  15.4 us (15%)
  waiting for transfers between devices  8.52 us (8%)
  local copies, waits for them, and re-layouts  5.19 us (5%)
    all_to_all x1, blocking collectives, per_device(): lax.all_to_all(spread_call(prompt_key_rows, prompt_value_rows), ('dp', 'h...  29.5 us
    all_to_all x1, blocking collectives, per_device(): lax.all_to_all(summed, 'dp', split_axis=0, concat_axis=0, axis_index_grou...  19.1 us
    pallas_call x7, Pallas kernels, attend_call(): call(body, outs, 3, 3, 1, 4 * 10 ** 8 * n, 2 ** 19 * n)  15.7 us
    ppermute x6, starting transfers between devices, per_device(): sums[first // half].append(lax.ppermute(prompt_part, 'dp', along_y(turn)))  9.37 us
    pallas_call x1, Pallas kernels, unpack_call(): call(body, outs, 3, 2 * len(pieces), 2, 10 ** 9, 4 * 2 ** 20)  5.46 us
    pallas_call x1, Pallas kernels, pack_call(): call(functools.partial(pack, turns), outs, 3, 4, 2, 10 ** 9, 8 * 2 ** 20)  4.52 us
    unnamed x18, local copies, waits for them, and re-layouts  3.73 us
    ppermute x2, waiting for transfers between devices, per_device(): before = [lax.ppermute(a, 'dp', along_y(1)) for a in halves]  3.18 us
  transfers between devices with their start and end apart: 12, of which 4 were waited for; matrix products, arithmetic and copies ran while one was open for 0% of the time, Pallas kernels for 25%

profile of v3, /device:TPU:8, one launch (start us, length us, event | category | flops | bytes accessed | tf_op | source)
XLA Modules:
  0.0 104.7 jit_solution(14403352034706783535)
XLA Ops:
  0.6 0.7 copy-done
  1.4 0.8 copy-done.1
  2.2 0.1 shard_map.129
  2.2 0.0 copy-start.2
  2.2 0.0 copy-start.3
  2.2 29.5 %all_to_all.10 = bf16[64,2,16,128]{3,2,1,0:T(8,128)(2,1)S(1)} all-to-all(bf16[64,2,16,128]{3,2,1,0:T(8,128)(2,1)S(1)} %shard_map.129), channel_id=1, replica_groups={{0,1,2,3,4,5,6,7,32,33,34,35,36,37,38,39,64,65,66,67,68,69,70,71,96,97,..., dimensions={0} | all-to-all | bytes 1048576 | tf_op jit(solution)/shard_map/all_to_all | solution.py:230
  31.8 0.8 fusion
  32.6 1.6 %collective-permute-start.2 = (bf16[4,8,2,16,128]{4,3,2,1,0:T(8,128)(2,1)}, bf16[4,8,2,16,128]{4,3,2,1,0:T(8,128)(2,1)S(1)}, u32[]{:S(2)}, u32[]{:S(2)}) collective-permute-start(bf16[4,8,2,16,128]{4,3,2,1,0:T(8,128)(2,1)} %bitcast.2), channel_id=1, source_target_pairs={{0,8},{8,16},{16,24},{24,0},{32,40},{40,48},{48,56},{56,32},{64,72... | collective-permute-start | bytes 786440 | tf_op jit(solution)/shard_map/ppermute | solution.py:246
  34.2 0.4 collective-permute-start
  34.6 1.6 %collective-permute-start.3 = (bf16[4,8,2,16,128]{4,3,2,1,0:T(8,128)(2,1)}, bf16[4,8,2,16,128]{4,3,2,1,0:T(8,128)(2,1)S(1)}, u32[]{:S(2)}, u32[]{:S(2)}) collective-permute-start(bf16[4,8,2,16,128]{4,3,2,1,0:T(8,128)(2,1)} %bitcast.3), channel_id=1, source_target_pairs={{0,8},{8,16},{16,24},{24,0},{32,40},{40,48},{48,56},{56,32},{64,72... | collective-permute-start | bytes 786440 | tf_op jit(solution)/shard_map/ppermute | solution.py:246
  36.2 0.4 collective-permute-start.1
  36.7 0.6 copy-done.7
  37.3 0.0 copy-done.8
  37.3 0.9 copy-done.5
  38.2 4.5 %shard_map.128 = (bf16[8,2,256,128]{3,2,1,0:T(8,128)(2,1)S(1)}, bf16[8,2,256,128]{3,2,1,0:T(8,128)(2,1)S(1)}, bf16[8,2,256,128]{3,2,1,0:T(8,128)(2,1)S(1)}, bf16...) custom-call(s32[1]{0:T(128)} %bitcast.own_y.refs_0_, ...), custom_call_target="tpu_custom_call" | custom-call | flops 1000000000 | bytes 8388608 | tf_op jit(solution)/shard_map/pallas_call | solution.py:179
  42.8 0.0 collective-permute-done.2.refs_5_
  42.8 0.8 collective-permute-done.refs_5_
  43.6 3.2 %collective-permute-done.3.refs_5_ = bf16[4,8,2,16,128]{4,3,2,1,0:T(8,128)(2,1)S(1)} collective-permute-done((bf16[4,8,2,16,128]{4,3,2,1,0:T(8,128)(2,1)}, bf16[4,8,2,16,128]{4,3,2,1,0:T(8,128)(2,1)S(1)}, u32[]{:S(2)}, u32[]{:S(2)}) %collective-permute-start.3) | collective-permute-done | bytes 262176 | tf_op jit(solution)/shard_map/ppermute | solution.py:246
  46.8 1.4 %collective-permute-done.1.refs_5_ = bf16[4,8,2,16,128]{4,3,2,1,0:T(8,128)(2,1)} collective-permute-done((bf16[4,8,2,16,128]{4,3,2,1,0:T(8,128)(2,1)}, bf16[4,8,2,16,128]{4,3,2,1,0:T(8,128)(2,1)}, u32[]{:S(2)}, u32[]{:S(2)}) %collective-permute-start.1) | collective-permute-done | bytes 262176 | tf_op jit(solution)/shard_map/ppermute | solution.py:245
  48.2 0.4 collective-permute-start.6
  48.6 1.6 %collective-permute-start.10 = (bf16[4,8,2,16,128]{4,3,2,1,0:T(8,128)(2,1)S(1)}, bf16[4,8,2,16,128]{4,3,2,1,0:T(8,128)(2,1)S(1)}, u32[]{:S(2)}, u32[]{:S(2)}) collective-permute-start(bf16[4,8,2,16,128]{4,3,2,1,0:T(8,128)(2,1)S(1)} %collective-permute-done.3.refs_5_), channel_id=1, source_target_pairs={{0,8},{8,16},{16,24},{24,0},{32,40},{40,48},{48,56},{56,32},{64,72... | collective-permute-start | bytes 786440 | tf_op jit(solution)/shard_map/ppermute | solution.py:250
  50.2 0.7 copy-done.6
  50.8 2.0 %shard_map.130 = (bf16[4,256,128]{2,1,0:T(8,128)(2,1)S(1)}, bf16[4,2,32,128]{3,2,1,0:T(8,128)(2,1)S(1)}, bf16[4,128,256]{2,1,0:T(8,128)(2,1)S(1)}) custom-call(s32[1]{0:T(128)} %bitcast.own_y.refs_0_, s32[1,32]{1,0:T(1,128)S(1)} %copy-done.8, s32[1,32]{1,0:T(1,128)S(1)} %bitcast.6, bf16[8,2,256,128]{3,2,1,0:T(8,128)(2,1)S(1)} %get-tuple-element.45.refs_3_, ...), custom_call_target="tpu_custom_call" | custom-call | flops 1600000000 | bytes 2097152 | tf_op jit(solution)/shard_map/pallas_call | solution.py:199
  52.8 2.4 %shard_map.134 = (bf16[4,256,128]{2,1,0:T(8,128)(2,1)S(1)}, bf16[4,2,32,128]{3,2,1,0:T(8,128)(2,1)S(1)}, bf16[4,128,256]{2,1,0:T(8,128)(2,1)S(1)}) custom-call(s32[1]{0:T(128)} %bitcast.own_y.refs_0_, s32[1,32]{1,0:T(1,128)S(1)} %copy-done.8, s32[1,32]{1,0:T(1,128)S(1)} %bitcast.7, bf16[8,2,256,128]{3,2,1,0:T(8,128)(2,1)S(1)} %get-tuple-element.45.refs_3_, ...), custom_call_target="tpu_custom_call" | custom-call | flops 1600000000 | bytes 2097152 | tf_op jit(solution)/shard_map/pallas_call | solution.py:199
  55.3 1.4 %collective-permute-start.8 = (bf16[4,128,256]{2,1,0:T(8,128)(2,1)S(1)}, bf16[4,128,256]{2,1,0:T(8,128)(2,1)S(1)}, u32[]{:S(2)}, u32[]{:S(2)}) collective-permute-start(bf16[4,128,256]{2,1,0:T(8,128)(2,1)S(1)} %get-tuple-element.60), channel_id=1, source_target_pairs={{0,8},{8,16},{16,24},{24,0},{32,40},{40,48},{48,56},{56,32},{64,72... | collective-permute-start | bytes 786440 | tf_op jit(solution)/shard_map/ppermute | solution.py:267
  56.6 2.7 %collective-permute-start.4 = (bf16[4,128,256]{2,1,0:T(8,128)(2,1)S(1)}, bf16[4,128,256]{2,1,0:T(8,128)(2,1)S(1)}, u32[]{:S(2)}, u32[]{:S(2)}) collective-permute-start(bf16[4,128,256]{2,1,0:T(8,128)(2,1)S(1)} %get-tuple-element.48), channel_id=1, source_target_pairs={{0,8},{8,16},{16,24},{24,0},{32,40},{40,48},{48,56},{56,32},{64,72... | collective-permute-start | bytes 786440 | tf_op jit(solution)/shard_map/ppermute | solution.py:267
  59.3 2.0 %shard_map.135 = (bf16[4,256,128]{2,1,0:T(8,128)(2,1)S(1)}, bf16[4,2,32,128]{3,2,1,0:T(8,128)(2,1)S(1)}, bf16[4,128,256]{2,1,0:T(8,128)(2,1)S(1)}) custom-call(s32[1]{0:T(128)} %bitcast.own_y.refs_0_, s32[1,32]{1,0:T(1,128)S(1)} %copy-done.8, s32[1,32]{1,0:T(1,128)S(1)} %bitcast.8, bf16[8,2,256,128]{3,2,1,0:T(8,128)(2,1)S(1)} %get-tuple-element.49.refs_3_, ...), custom_call_target="tpu_custom_call" | custom-call | flops 1600000000 | bytes 2097152 | tf_op jit(solution)/shard_map/pallas_call | solution.py:199
  61.4 0.3 collective-permute-start.9
  61.6 2.0 %shard_map.131 = (bf16[4,256,128]{2,1,0:T(8,128)(2,1)S(1)}, bf16[4,2,32,128]{3,2,1,0:T(8,128)(2,1)S(1)}, bf16[4,128,256]{2,1,0:T(8,128)(2,1)S(1)}) custom-call(s32[1]{0:T(128)} %bitcast.own_y.refs_0_, s32[1,32]{1,0:T(1,128)S(1)} %copy-done.8, s32[1,32]{1,0:T(1,128)S(1)} %bitcast.9, bf16[8,2,256,128]{3,2,1,0:T(8,128)(2,1)S(1)} %get-tuple-element.49.refs_3_, ...), custom_call_target="tpu_custom_call" | custom-call | flops 1600000000 | bytes 2097152 | tf_op jit(solution)/shard_map/pallas_call | solution.py:199
  63.6 0.0 collective-permute-done.10.refs_5_
  63.7 1.3 %collective-permute-start.5 = (bf16[4,128,256]{2,1,0:T(8,128)(2,1)S(1)}, bf16[4,128,256]{2,1,0:T(8,128)(2,1)S(1)}, u32[]{:S(2)}, u32[]{:S(2)}) collective-permute-start(bf16[4,128,256]{2,1,0:T(8,128)(2,1)S(1)} %get-tuple-element.52), channel_id=1, source_target_pairs={{0,24},{8,0},{16,8},{24,16},{32,56},{40,32},{48,40},{56,48},{64,88... | collective-permute-start | bytes 786440 | tf_op jit(solution)/shard_map/ppermute | solution.py:267
  65.0 2.0 %shard_map.136 = (bf16[4,256,128]{2,1,0:T(8,128)(2,1)S(1)}, bf16[4,2,32,128]{3,2,1,0:T(8,128)(2,1)S(1)}, bf16[4,128,256]{2,1,0:T(8,128)(2,1)S(1)}) custom-call(s32[1]{0:T(128)} %bitcast.own_y.refs_0_, s32[1,32]{1,0:T(1,128)S(1)} %copy-done.8, s32[1,32]{1,0:T(1,128)S(1)} %bitcast.10, bf16[8,2,256,128]{3,2,1,0:T(8,128)(2,1)S(1)} %get-tuple-element.53.refs_3_, ...), custom_call_target="tpu_custom_call" | custom-call | flops 1600000000 | bytes 2097152 | tf_op jit(solution)/shard_map/pallas_call | solution.py:199
  67.0 0.0 collective-permute-done.6.refs_5_
  67.0 2.3 %collective-permute-start.11 = (bf16[4,128,256]{2,1,0:T(8,128)(2,1)S(1)}, bf16[4,128,256]{2,1,0:T(8,128)(2,1)S(1)}, u32[]{:S(2)}, u32[]{:S(2)}) collective-permute-start(bf16[4,128,256]{2,1,0:T(8,128)(2,1)S(1)} %get-tuple-element.63), channel_id=1, source_target_pairs={{0,16},{8,24},{16,0},{24,8},{32,48},{40,56},{48,32},{56,40},{64,80... | collective-permute-start | bytes 786440 | tf_op jit(solution)/shard_map/ppermute | solution.py:267
  69.3 2.0 %shard_map.132 = (bf16[4,256,128]{2,1,0:T(8,128)(2,1)S(1)}, bf16[4,2,32,128]{3,2,1,0:T(8,128)(2,1)S(1)}, bf16[4,128,256]{2,1,0:T(8,128)(2,1)S(1)}) custom-call(s32[1]{0:T(128)} %bitcast.own_y.refs_0_, s32[1,32]{1,0:T(1,128)S(1)} %copy-done.8, s32[1,32]{1,0:T(1,128)S(1)} %bitcast.11, bf16[8,2,256,128]{3,2,1,0:T(8,128)(2,1)S(1)} %get-tuple-element.53.refs_3_, ...), custom_call_target="tpu_custom_call" | custom-call | flops 1600000000 | bytes 2097152 | tf_op jit(solution)/shard_map/pallas_call | solution.py:199
  71.3 0.0 collective-permute-done.8
  71.3 1.4 %collective-permute-start.7 = (bf16[4,128,256]{2,1,0:T(8,128)(2,1)S(1)}, bf16[4,128,256]{2,1,0:T(8,128)(2,1)S(1)}, u32[]{:S(2)}, u32[]{:S(2)}) collective-permute-start(bf16[4,128,256]{2,1,0:T(8,128)(2,1)S(1)} %get-tuple-element.55), channel_id=1, source_target_pairs={{0,16},{8,24},{16,0},{24,8},{32,48},{40,56},{48,32},{56,40},{64,80... | collective-permute-start | bytes 786440 | tf_op jit(solution)/shard_map/ppermute | solution.py:267
  72.7 3.3 %shard_map.133 = (bf16[8,256,128]{2,1,0:T(8,128)(2,1)S(1)}, bf16[8,2,32,128]{3,2,1,0:T(8,128)(2,1)S(1)}, bf16[8,128,256]{2,1,0:T(8,128)(2,1)S(1)}) custom-call(s32[1]{0:T(128)} %bitcast.own_y.refs_0_, s32[1,32]{1,0:T(1,128)S(1)} %copy-done.8, s32[1,32]{1,0:T(1,128)S(1)} %bitcast.12, bf16[8,2,256,128]{3,2,1,0:T(8,128)(2,1)S(1)} %get-tuple-element.56.refs_3_, ...), custom_call_target="tpu_custom_call" | custom-call | flops 3200000000 | bytes 4194304 | tf_op jit(solution)/shard_map/pallas_call | solution.py:199
  76.0 5.5 %shard_map.137 = (bf16[512,1024]{1,0:T(8,128)(2,1)}, bf16[512,128]{1,0:T(8,128)(2,1)}, bf16[512,128]{1,0:T(8,128)(2,1)}) custom-call(s32[1]{0:T(128)} %bitcast.own_y.refs_0_, s32[1,32]{1,0:T(1,128)S(1)} %copy-done.7, s32[1,32]{1,0:T(1,128)S(1)} %copy-done.8, bf16[4,256,128]{2,1,0:T(8,128)(2,1)S(1)} %get-tuple-element.64.refs_0_, ...), custom_call_target="tpu_custom_call" | custom-call | flops 1000000000 | bytes 4194304 | tf_op jit(solution)/shard_map/pallas_call | solution.py:186
  81.5 0.0 collective-permute-done.4
  81.5 0.0 collective-permute-done.9
  81.5 3.1 %collective-permute-done.5 = bf16[4,128,256]{2,1,0:T(8,128)(2,1)S(1)} collective-permute-done((bf16[4,128,256]{2,1,0:T(8,128)(2,1)S(1)}, bf16[4,128,256]{2,1,0:T(8,128)(2,1)S(1)}, u32[]{:S(2)}, u32[]{:S(2)}) %collective-permute-start.5) | collective-permute-done | bytes 262176 | tf_op jit(solution)/shard_map/ppermute | solution.py:267
  84.6 0.0 collective-permute-done.11
  84.6 0.0 collective-permute-done.7
  84.6 0.3 add_convert_fusion.1
  84.9 19.1 %all_to_all.11 = bf16[8,128,256]{2,1,0:T(8,128)(2,1)S(1)} all-to-all(bf16[8,128,256]{2,1,0:T(8,128)(2,1)S(1)} %pad_maximum_fusion), channel_id=1, replica_groups={{0,32,64,96,128,160,192,224},{8,40,72,104,136,168,200,232},{16,48,80,11..., dimensions={0} | all-to-all | bytes 1048576 | tf_op jit(solution)/shard_map/all_to_all | solution.py:276
  104.0 0.1 reduce_sum.12
  104.1 0.6 fusion.1
  (11 shorter events, 0.1 us)
Async XLA Ops:
  0.6 0.8 copy-start
  1.4 0.8 copy-start.1
  2.1 34.5 %copy-start.4 = (bf16[512,128]{1,0:T(8,128)(2,1)S(1)}, bf16[512,128]{1,0:T(8,128)(2,1)}, u32[]{:S(2)}) copy-start(bf16[512,128]{1,0:T(8,128)(2,1)} %key.1) | copy-start | bytes 393220
  2.2 34.4 %copy-start.2 = (bf16[512,1024]{1,0:T(8,128)(2,1)S(1)}, bf16[512,1024]{1,0:T(8,128)(2,1)}, u32[]{:S(2)}) copy-start(bf16[512,1024]{1,0:T(8,128)(2,1)} %query.1) | copy-start | bytes 3145732
  2.2 34.4 %copy-start.3 = (bf16[512,1024]{1,0:T(8,128)(2,1)S(1)}, bf16[512,1024]{1,0:T(8,128)(2,1)}, u32[]{:S(2)}) copy-start(bf16[512,1024]{1,0:T(8,128)(2,1)} %cotangent.1) | copy-start | bytes 3145732
  32.6 10.2 %collective-permute-start.2 = (bf16[4,8,2,16,128]{4,3,2,1,0:T(8,128)(2,1)}, bf16[4,8,2,16,128]{4,3,2,1,0:T(8,128)(2,1)S(1)}, u32[]{:S(2)}, u32[]{:S(2)}) collective-permute-start(bf16[4,8,2,16,128]{4,3,2,1,0:T(8,128)(2,1)} %bitcast.2), channel_id=1, source_target_pairs={{0,8},{8,16},{16,24},{24,0},{32,40},{40,48},{48,56},{56,32},{64,72... | collective-permute-start | bytes 786440 | tf_op jit(solution)/shard_map/ppermute | solution.py:246
  34.2 9.4 %collective-permute-start = (bf16[4,8,2,16,128]{4,3,2,1,0:T(8,128)(2,1)}, bf16[4,8,2,16,128]{4,3,2,1,0:T(8,128)(2,1)S(1)}, u32[]{:S(2)}, u32[]{:S(2)}) collective-permute-start(bf16[4,8,2,16,128]{4,3,2,1,0:T(8,128)(2,1)} %bitcast.2), channel_id=1, source_target_pairs={{0,24},{8,0},{16,8},{24,16},{32,56},{40,32},{48,40},{56,48},{64,88... | collective-permute-start | bytes 786440 | tf_op jit(solution)/shard_map/ppermute | solution.py:245
  34.6 12.1 %collective-permute-start.3 = (bf16[4,8,2,16,128]{4,3,2,1,0:T(8,128)(2,1)}, bf16[4,8,2,16,128]{4,3,2,1,0:T(8,128)(2,1)S(1)}, u32[]{:S(2)}, u32[]{:S(2)}) collective-permute-start(bf16[4,8,2,16,128]{4,3,2,1,0:T(8,128)(2,1)} %bitcast.3), channel_id=1, source_target_pairs={{0,8},{8,16},{16,24},{24,0},{32,40},{40,48},{48,56},{56,32},{64,72... | collective-permute-start | bytes 786440 | tf_op jit(solution)/shard_map/ppermute | solution.py:246
  36.2 12.0 %collective-permute-start.1 = (bf16[4,8,2,16,128]{4,3,2,1,0:T(8,128)(2,1)}, bf16[4,8,2,16,128]{4,3,2,1,0:T(8,128)(2,1)}, u32[]{:S(2)}, u32[]{:S(2)}) collective-permute-start(bf16[4,8,2,16,128]{4,3,2,1,0:T(8,128)(2,1)} %bitcast.3), channel_id=1, source_target_pairs={{0,24},{8,0},{16,8},{24,16},{32,56},{40,32},{48,40},{56,48},{64,88... | collective-permute-start | bytes 786440 | tf_op jit(solution)/shard_map/ppermute | solution.py:245
  36.6 0.7 copy-start.7
  36.6 0.7 copy-start.8
  37.3 0.9 copy-start.5
  48.2 18.8 %collective-permute-start.6 = (bf16[4,8,2,16,128]{4,3,2,1,0:T(8,128)(2,1)S(1)}, bf16[4,8,2,16,128]{4,3,2,1,0:T(8,128)(2,1)S(1)}, u32[]{:S(2)}, u32[]{:S(2)}) collective-permute-start(bf16[4,8,2,16,128]{4,3,2,1,0:T(8,128)(2,1)S(1)} %collective-permute-done.refs_5_), channel_id=1, source_target_pairs={{0,24},{8,0},{16,8},{24,16},{32,56},{40,32},{48,40},{56,48},{64,88... | collective-permute-start | bytes 786440 | tf_op jit(solution)/shard_map/ppermute | solution.py:249
  48.6 15.0 %collective-permute-start.10 = (bf16[4,8,2,16,128]{4,3,2,1,0:T(8,128)(2,1)S(1)}, bf16[4,8,2,16,128]{4,3,2,1,0:T(8,128)(2,1)S(1)}, u32[]{:S(2)}, u32[]{:S(2)}) collective-permute-start(bf16[4,8,2,16,128]{4,3,2,1,0:T(8,128)(2,1)S(1)} %collective-permute-done.3.refs_5_), channel_id=1, source_target_pairs={{0,8},{8,16},{16,24},{24,0},{32,40},{40,48},{48,56},{56,32},{64,72... | collective-permute-start | bytes 786440 | tf_op jit(solution)/shard_map/ppermute | solution.py:250
  50.2 0.7 copy-start.6
  55.3 16.1 %collective-permute-start.8 = (bf16[4,128,256]{2,1,0:T(8,128)(2,1)S(1)}, bf16[4,128,256]{2,1,0:T(8,128)(2,1)S(1)}, u32[]{:S(2)}, u32[]{:S(2)}) collective-permute-start(bf16[4,128,256]{2,1,0:T(8,128)(2,1)S(1)} %get-tuple-element.60), channel_id=1, source_target_pairs={{0,8},{8,16},{16,24},{24,0},{32,40},{40,48},{48,56},{56,32},{64,72... | collective-permute-start | bytes 786440 | tf_op jit(solution)/shard_map/ppermute | solution.py:267
  56.6 24.8 %collective-permute-start.4 = (bf16[4,128,256]{2,1,0:T(8,128)(2,1)S(1)}, bf16[4,128,256]{2,1,0:T(8,128)(2,1)S(1)}, u32[]{:S(2)}, u32[]{:S(2)}) collective-permute-start(bf16[4,128,256]{2,1,0:T(8,128)(2,1)S(1)} %get-tuple-element.48), channel_id=1, source_target_pairs={{0,8},{8,16},{16,24},{24,0},{32,40},{40,48},{48,56},{56,32},{64,72... | collective-permute-start | bytes 786440 | tf_op jit(solution)/shard_map/ppermute | solution.py:267
  61.4 20.1 %collective-permute-start.9 = (bf16[4,128,256]{2,1,0:T(8,128)(2,1)S(1)}, bf16[4,128,256]{2,1,0:T(8,128)(2,1)S(1)}, u32[]{:S(2)}, u32[]{:S(2)}) collective-permute-start(bf16[4,128,256]{2,1,0:T(8,128)(2,1)S(1)} %get-tuple-element.62), channel_id=1, source_target_pairs={{0,24},{8,0},{16,8},{24,16},{32,56},{40,32},{48,40},{56,48},{64,88... | collective-permute-start | bytes 786440 | tf_op jit(solution)/shard_map/ppermute | solution.py:267
  63.7 20.9 %collective-permute-start.5 = (bf16[4,128,256]{2,1,0:T(8,128)(2,1)S(1)}, bf16[4,128,256]{2,1,0:T(8,128)(2,1)S(1)}, u32[]{:S(2)}, u32[]{:S(2)}) collective-permute-start(bf16[4,128,256]{2,1,0:T(8,128)(2,1)S(1)} %get-tuple-element.52), channel_id=1, source_target_pairs={{0,24},{8,0},{16,8},{24,16},{32,56},{40,32},{48,40},{56,48},{64,88... | collective-permute-start | bytes 786440 | tf_op jit(solution)/shard_map/ppermute | solution.py:267
  67.0 17.6 %collective-permute-start.11 = (bf16[4,128,256]{2,1,0:T(8,128)(2,1)S(1)}, bf16[4,128,256]{2,1,0:T(8,128)(2,1)S(1)}, u32[]{:S(2)}, u32[]{:S(2)}) collective-permute-start(bf16[4,128,256]{2,1,0:T(8,128)(2,1)S(1)} %get-tuple-element.63), channel_id=1, source_target_pairs={{0,16},{8,24},{16,0},{24,8},{32,48},{40,56},{48,32},{56,40},{64,80... | collective-permute-start | bytes 786440 | tf_op jit(solution)/shard_map/ppermute | solution.py:267
  71.3 13.3 %collective-permute-start.7 = (bf16[4,128,256]{2,1,0:T(8,128)(2,1)S(1)}, bf16[4,128,256]{2,1,0:T(8,128)(2,1)S(1)}, u32[]{:S(2)}, u32[]{:S(2)}) collective-permute-start(bf16[4,128,256]{2,1,0:T(8,128)(2,1)S(1)} %get-tuple-element.55), channel_id=1, source_target_pairs={{0,16},{8,24},{16,0},{24,8},{32,48},{40,56},{48,32},{56,40},{64,80... | collective-permute-start | bytes 786440 | tf_op jit(solution)/shard_map/ppermute | solution.py:267

commit v4 on v2

--- a/solution.py
+++ b/solution.py
@@ -52,13 +52,13 @@
     return pl.ds(base, WINDOW), start - base
 
 
-def pack(turns, own_y, lengths, owners, query, cotangent, key, value, *refs):
+def pack(turns, own_y, lengths, owners, masks, query, cotangent, key, value, *refs):
     n = len(turns)
-    wide, near = refs[:n], refs[n : 2 * n]
-    first_of, count_of = refs[2 * n :]
-    locate(lengths, owners, None, first_of, count_of, None)
+    wide, near, bias = refs[:n], refs[n : 2 * n], refs[2 * n : 3 * n]
+    first_of, count_of, mask_of = refs[3 * n :]
+    locate(lengths, owners, masks, first_of, count_of, mask_of)
     rows = query.shape[0]
-    for turn, wide_ref, near_ref in zip(turns, wide, near):
+    for turn, wide_ref, near_ref, bias_ref in zip(turns, wide, near, bias):
         y = lax.rem(own_y[0] + turn, NY)
 
         def one(z, carry):
@@ -74,6 +74,8 @@
                     ]
             for j, ref in enumerate((key, value)):
                 near_ref[z, j] = dot(pick, ref[window, :]).astype(jnp.bfloat16)
+            hidden = jnp.where(mask_of[prompt] > 0, 0.0, far_below).astype(jnp.float32)
+            bias_ref[z] = jnp.full(bias_ref.shape[1:], hidden, jnp.float32)
             return carry
 
         lax.fori_loop(0, NZ, one, 0, unroll=2)
@@ -91,46 +93,44 @@
     for turn, wide_ref, near_ref in zip(turns, wide, near):
         y = lax.rem(own_y[0] + turn, NY)
 
-        def one(z, carry):
-            prompt = z * NY + y
+        def one(i, carry):
+            prompt = i * NY + y
             window, offset = window_of(first_of[prompt], rows)
             put = one_hot((WINDOW, SPAN), 1, offset, count_of[prompt])
             grads = jnp.concatenate(
-                [wide_ref[z, h * SPAN : (h + 1) * SPAN, :] for h in range(GROUP)], axis=1
+                [wide_ref[i, h * SPAN : (h + 1) * SPAN, :] for h in range(GROUP)], axis=1
             )
             dq[window, :] = dq[window, :] + dot(put, grads).astype(jnp.bfloat16)
             for j, ref in enumerate((dk, dv)):
-                ref[window, :] = ref[window, :] + dot(put, near_ref[z, j]).astype(jnp.bfloat16)
+                ref[window, :] = ref[window, :] + dot(put, near_ref[i, j]).astype(jnp.bfloat16)
             return carry
 
         lax.fori_loop(0, NZ, one, 0, unroll=2)
 
 
-def attend(turn, n_parts, *refs):
-    own_y, owners, masks, wide, near = refs[:5]
-    prompts = refs[5 : 5 + n_parts]
-    dq, dnear, dprompt, mask_of = refs[5 + n_parts :]
-    y = lax.rem(own_y[0] + turn, NY)
-
-    def place(s, carry):
-        mask_of[owners[0, s]] = masks[0, s]
-        return carry
-
-    lax.fori_loop(0, NY * NZ, place, 0)
+def attend(n_parts, wide, near, bias, *refs):
+    parts = refs[:n_parts]
+    dq, dnear, dprompt = refs[n_parts:]
     key_at = lax.broadcasted_iota(jnp.int32, (SPAN, GROUP * SPAN), 0)
     token_at = lax.broadcasted_iota(jnp.int32, (SPAN, GROUP * SPAN), 1) % SPAN
     near_bias = jnp.where(key_at <= token_at, 0.0, far_below)
-
-    def response(z, prompt_ref, z_in):
+    per_part = NZ // n_parts
+    for z in range(NZ):
+        prompt = parts[z // per_part]
+        i = z % per_part
         q, g = wide[z, 0], wide[z, 1]
-        k = jnp.concatenate([prompt_ref[z_in, :, 0].reshape(PROMPT, HEAD_DIMENSION), near[z, 0]])
-        v = jnp.concatenate([prompt_ref[z_in, :, 1].reshape(PROMPT, HEAD_DIMENSION), near[z, 1]])
+        k = jnp.concatenate([prompt[i, :, 0].reshape(PROMPT, HEAD_DIMENSION), near[z, 0]])
+        v = jnp.concatenate([prompt[i, :, 1].reshape(PROMPT, HEAD_DIMENSION), near[z, 1]])
         scores = dot(k, q, ((1,), (1,)))
         dots = dot(v, g, ((1,), (1,)))
-        far_bias = jnp.where(mask_of[z * NY + y] > 0, 0.0, far_below).astype(jnp.float32)
-        scores = jnp.concatenate([scores[:PROMPT] + far_bias, scores[PROMPT:] + near_bias], axis=0)
-        highest = jnp.max(scores, axis=0, keepdims=True)
-        weights = jnp.exp2((scores - highest) * exp2_scale)
+        far, own = scores[:PROMPT], scores[PROMPT:] + near_bias
+        hidden = bias[z]
+        highest = jnp.maximum(
+            jnp.max(far, axis=0, keepdims=True) + hidden, jnp.max(own, axis=0, keepdims=True)
+        )
+        weights = jnp.exp2(
+            jnp.concatenate([far - (highest - hidden), own - highest], axis=0) * exp2_scale
+        )
         inverse = 1.0 / jnp.sum(weights, axis=0, keepdims=True)
         delta = jnp.sum(weights * dots, axis=0, keepdims=True) * inverse
         probs = weights * inverse
@@ -144,15 +144,19 @@
         dnear[z, 0] = k_grad[PROMPT:]
         dnear[z, 1] = v_grad[PROMPT:]
 
-    per_part = NZ // n_parts
-    for part, prompt_ref in enumerate(prompts):
-
-        def pair(i, carry):
-            for j in range(2):
-                response(part * per_part + 2 * i + j, prompt_ref, 2 * i + j)
-            return carry
-
-        lax.fori_loop(0, per_part // 2, pair, 0)
+
+def spread(keys, values, out, held, sems):
+    copies = [
+        pltpu.make_async_copy(ref, held.at[j], sems.at[j]) for j, ref in enumerate((keys, values))
+    ]
+    for copy in copies:
+        copy.start()
+    for j, copy in enumerate(copies):
+        copy.wait()
+        for h in range(HEADS):
+            rows = held[j, :, h * HEAD_DIMENSION : (h + 1) * HEAD_DIMENSION]
+            for z in range(NZ):
+                out[z * HEADS + h, j] = rows
 
 
 smem = pl.BlockSpec(memory_space=pltpu.SMEM)
@@ -179,8 +183,9 @@
     n = len(turns)
     outs = [shaped(NZ, 2, GROUP * SPAN, HEAD_DIMENSION)] * n
     outs += [shaped(NZ, 2, SPAN, HEAD_DIMENSION)] * n
-    got = call(functools.partial(pack, turns), outs, 3, 4, 2, 10**9, 8 * 2**20)(*args)
-    return got[:n], got[n:]
+    outs += [jax.ShapeDtypeStruct((NZ, 1, GROUP * SPAN), jnp.float32)] * n
+    got = call(functools.partial(pack, turns), outs, 4, 4, 3, 10**9, 8 * 2**20)(*args)
+    return [got[i::n] for i in range(n)]
 
 
 def unpack_call(turns, own_y, lengths, owners, wide, near, rows):
@@ -191,16 +196,29 @@
     )
 
 
-def attend_call(turn, own_y, owners, masks, wide, near, prompts):
+def attend_call(packed, parts):
     outs = [
         shaped(NZ, GROUP * SPAN, HEAD_DIMENSION),
         shaped(NZ, 2, SPAN, HEAD_DIMENSION),
         shaped(NZ, PROMPT, 2 * HEAD_DIMENSION),
     ]
-    body = functools.partial(attend, turn, len(prompts))
-    return call(body, outs, 3, 2 + len(prompts), 1, 3 * 10**9, 4 * 2**20)(
-        own_y, owners, masks, wide, near, *prompts
-    )
+    body = functools.partial(attend, len(parts))
+    return call(body, outs, 0, 3 + len(parts), 0, 4 * 10**9, 2**22)(*packed, *parts)
+
+
+def spread_call(keys, values):
+    anywhere = pl.BlockSpec(memory_space=pl.ANY)
+    return pl.pallas_call(
+        spread,
+        out_shape=shaped(NZ * HEADS, 2, keys.shape[0], HEAD_DIMENSION),
+        in_specs=[anywhere] * 2,
+        out_specs=vmem,
+        scratch_shapes=[
+            pltpu.VMEM((2,) + keys.shape, jnp.bfloat16),
+            pltpu.SemaphoreType.DMA((2,)),
+        ],
+        compiler_params=pltpu.CompilerParams(vmem_limit_bytes=60 * 1024 * 1024),
+    )(keys, values)
 
 
 def along_y(turn):
@@ -223,16 +241,9 @@
     block_mask,
 ):
     part = prompt_key_rows.shape[0]
-    mine = jnp.stack(
-        [
-            a.reshape(part, HEADS, HEAD_DIMENSION).transpose(1, 0, 2)
-            for a in (prompt_key_rows, prompt_value_rows)
-        ],
-        axis=1,
-    )
-    mine = jnp.broadcast_to(mine[None], (NZ,) + mine.shape).reshape((NZ * HEADS,) + mine.shape[1:])
+    half = NZ // 2
     column = lax.all_to_all(
-        mine,
+        spread_call(prompt_key_rows, prompt_value_rows),
         ("dp", "head"),
         split_axis=0,
         concat_axis=0,
@@ -242,24 +253,41 @@
     turns = (0, 1, 3, 2)
     own_y = lax.rem(lax.axis_index("dp"), NY).reshape(1).astype(jnp.int32)
     masks = block_mask.reshape(block_mask.shape[:2])
-    wide, near = pack_call(
-        turns, own_y, resp_len, resp_owner, queries, output_cotangent, response_keys, response_values
-    )
-    after = lax.ppermute(column, "dp", along_y(-1))
-    before = lax.ppermute(column, "dp", along_y(1))
-    half = NZ // 2
+    own, next_one, last_one, far = pack_call(
+        turns,
+        own_y,
+        resp_len,
+        resp_owner,
+        masks,
+        queries,
+        output_cotangent,
+        response_keys,
+        response_values,
+    )
+    halves = (column[:half], lax.optimization_barrier(column)[half:])
+    after = [lax.ppermute(a, "dp", along_y(-1)) for a in halves]
+    before = [lax.ppermute(a, "dp", along_y(1)) for a in halves]
+    after, before = lax.optimization_barrier((after, before))
     across = [
-        lax.ppermute(after[:half], "dp", along_y(-1)),
-        lax.ppermute(before[half:], "dp", along_y(1)),
+        lax.ppermute(after[0], "dp", along_y(-1)),
+        lax.ppermute(before[1], "dp", along_y(1)),
     ]
-    dq, dnear, parts = [], [], []
-    for turn, a, b, prompts in zip(turns, wide, near, ([column], [after], [before], across)):
-        q_part, near_part, prompt_part = attend_call(turn, own_y, resp_owner, masks, a, b, prompts)
+    dq, dnear, sums = [], [], []
+    for turn, packed, prompts in (
+        (1, next_one, after),
+        (3, last_one, before),
+        (2, far, across),
+        (0, own, [column]),
+    ):
+        q_part, near_part, prompt_part = attend_call(packed, prompts)
         dq.append(q_part)
         dnear.append(near_part)
-        parts.append(lax.ppermute(prompt_part, "dp", along_y(turn)) if turn else prompt_part)
-    dq, dk, dv = unpack_call(turns, own_y, resp_len, resp_owner, dq, dnear, queries.shape[0])
-    summed = sum(a.astype(jnp.float32) for a in parts).astype(jnp.bfloat16)
+        sums.append(lax.ppermute(prompt_part, "dp", along_y(turn)) if turn else prompt_part)
+    dq, dk, dv = unpack_call(
+        (1, 3, 2, 0), own_y, resp_len, resp_owner, dq, dnear, queries.shape[0]
+    )
+    summed = sum(a.astype(jnp.float32) for a in sums).astype(jnp.bfloat16)
+    summed, dq, dk, dv = lax.optimization_barrier((summed, dq, dk, dv))
     shares = lax.all_to_all(
         summed, "dp", split_axis=0, concat_axis=0, axis_index_groups=same_y, tiled=True
     )

time: 106 us -> 104 us (0.981)
  blocking collectives: 29.5 us -> 46.4 us
  waiting for transfers between devices: 28.8 us -> 19.2 us
  starting transfers between devices: 15.3 us -> 10.2 us
  Pallas kernels: 25.7 us -> 23.2 us
  local copies, waits for them, and re-layouts: 4.91 us -> 3.65 us
    all_to_all x1 -> x2, blocking collectives: 29.5 us -> 46.4 us  [the longest x1 29.7 us: per_device(): lax.all_to_all(spread_call(prompt_key_rows, prompt_value_rows), ('dp', 'h...]
    all_to_all x1 -> x0, waiting for transfers between devices: 8.68 us -> none  [per_device(): lax.all_to_all(summed, 'dp', split_axis=0, concat_axis=0, axis_index_grou...]
    all_to_all x1 -> x0, starting transfers between devices: 3.49 us -> none  [per_device(): lax.all_to_all(summed, 'dp', split_axis=0, concat_axis=0, axis_index_grou...]
    ppermute x3, waiting for transfers between devices: 15.2 us -> 12 us  [per_device(): lax.ppermute(prompt_part, 'dp', along_y(turn))]
    unnamed x16 -> x14, local copies, waits for them, and re-layouts: 4.15 us -> 1.58 us
    pallas_call x5 -> x6, Pallas kernels: 20.2 us -> 17.8 us  [the longest x4 11.5 us: attend_call(): call(body, outs, 0, 3 + len(parts), 0, 4 * 10 ** 9, 2 ** 22)]
    ppermute x4 -> x6, waiting for transfers between devices: 4.93 us -> 7.24 us  [the longest x2 4.49 us: per_device(): before = [lax.ppermute(a, 'dp', along_y(1)) for a in halves]]
    ppermute x3, starting transfers between devices: 4.92 us -> 3.12 us  [per_device(): lax.ppermute(prompt_part, 'dp', along_y(turn))]
  transfers between devices with their start and end apart: 8 -> 9, of which waited for: 3 -> 4; matrix products, arithmetic and copies ran while one was open for 0% -> 1% of each run, Pallas kernels for 24% -> 21%
where the time goes in v4:
time: 104 us
  blocking collectives  46.4 us (45%)
  Pallas kernels  23.2 us (22%)
  waiting for transfers between devices  19.2 us (18%)
  starting transfers between devices  10.2 us (10%)
  local copies, waits for them, and re-layouts  3.65 us (4%)
    all_to_all x1, blocking collectives, per_device(): lax.all_to_all(spread_call(prompt_key_rows, prompt_value_rows), ('dp', 'h...  29.7 us
    all_to_all x1, blocking collectives, per_device(): lax.all_to_all(summed, 'dp', split_axis=0, concat_axis=0, axis_index_grou...  16.7 us
    ppermute x3, waiting for transfers between devices, per_device(): lax.ppermute(prompt_part, 'dp', along_y(turn))  12 us
    pallas_call x4, Pallas kernels, attend_call(): call(body, outs, 0, 3 + len(parts), 0, 4 * 10 ** 9, 2 ** 22)  11.5 us
    pallas_call x1, Pallas kernels, unpack_call(): call(body, outs, 3, 2 * len(turns), 2, 10 ** 9, 4 * 2 ** 20)  5.41 us
    pallas_call x1, Pallas kernels, pack_call(): call(functools.partial(pack, turns), outs, 4, 4, 3, 10 ** 9, 8 * 2 ** 20)  4.55 us
    ppermute x2, waiting for transfers between devices, per_device(): before = [lax.ppermute(a, 'dp', along_y(1)) for a in halves]  4.49 us
    ppermute x2, starting transfers between devices, per_device(): after = [lax.ppermute(a, 'dp', along_y(-1)) for a in halves]  3.76 us
  transfers between devices with their start and end apart: 9, of which 4 were waited for; matrix products, arithmetic and copies ran while one was open for 1% of the time, Pallas kernels for 21%

profile of v4, /device:TPU:2, one launch (start us, length us, event | category | flops | bytes accessed | tf_op | source)
XLA Modules:
  0.0 103.8 jit_solution(10664862153500291145)
XLA Ops:
  0.6 0.0 copy-start.2
  0.6 1.7 %shard_map.129 = bf16[64,2,16,128]{3,2,1,0:T(8,128)(2,1)} custom-call(bf16[16,1024]{1,0:T(8,128)(2,1)} %keys.1, bf16[16,1024]{1,0:T(8,128)(2,1)} %values.1), custom_call_target="tpu_custom_call" | custom-call | tf_op jit(solution)/shard_map/pallas_call | solution.py:211
  2.3 0.0 copy-start
  2.3 0.0 copy-start.1
  2.3 29.7 %all_to_all.10 = bf16[64,2,16,128]{3,2,1,0:T(8,128)(2,1)S(1)} all-to-all(bf16[64,2,16,128]{3,2,1,0:T(8,128)(2,1)} %shard_map.129), channel_id=1, replica_groups={{0,1,2,3,4,5,6,7,32,33,34,35,36,37,38,39,64,65,66,67,68,69,70,71,96,97,..., dimensions={0} | all-to-all | bytes 1048576 | tf_op jit(solution)/shard_map/all_to_all | solution.py:245
  32.1 0.7 slice.20
  32.8 3.0 %collective-permute-start = (bf16[4,8,2,16,128]{4,3,2,1,0:T(8,128)(2,1)}, bf16[4,8,2,16,128]{4,3,2,1,0:T(8,128)(2,1)S(1)}, u32[]{:S(2)}, u32[]{:S(2)}) collective-permute-start(bf16[4,8,2,16,128]{4,3,2,1,0:T(8,128)(2,1)} %bitcast.2), channel_id=1, source_target_pairs={{0,24},{8,0},{16,8},{24,16},{32,56},{40,32},{48,40},{56,48},{64,88... | collective-permute-start | bytes 786440 | tf_op jit(solution)/shard_map/ppermute | solution.py:268
  35.8 0.7 slice.21
  36.5 0.7 collective-permute-start.1
  37.3 1.3 %collective-permute-start.2 = (bf16[4,8,2,16,128]{4,3,2,1,0:T(8,128)(2,1)}, bf16[4,8,2,16,128]{4,3,2,1,0:T(8,128)(2,1)}, u32[]{:S(2)}, u32[]{:S(2)}) collective-permute-start(bf16[4,8,2,16,128]{4,3,2,1,0:T(8,128)(2,1)} %bitcast.2), channel_id=1, source_target_pairs={{0,8},{8,16},{16,24},{24,0},{32,40},{40,48},{48,56},{56,32},{64,72... | collective-permute-start | bytes 786440 | tf_op jit(solution)/shard_map/ppermute | solution.py:269
  38.5 0.0 collective-permute-start.3
  38.6 0.0 copy-start.4
  38.6 0.0 copy-start.5
  38.6 0.0 copy-start.6
  38.6 0.0 copy-done.2
  38.6 0.0 copy-done
  38.6 0.0 copy-done.1
  38.6 0.6 copy-done.4
  39.2 0.0 copy-done.5
  39.2 0.0 copy-done.6
  39.3 0.0 copy-start.3
  39.3 0.9 copy-done.3
  40.2 4.6 %shard_map.128 = (bf16[8,2,256,128]{3,2,1,0:T(8,128)(2,1)S(1)}, bf16[8,2,256,128]{3,2,1,0:T(8,128)(2,1)S(1)}, bf16[8,2,256,128]{3,2,1,0:T(8,128)(2,1)S(1)}, bf16...) custom-call(s32[1]{0:T(128)} %bitcast.own_y, ...), custom_call_target="tpu_custom_call" | custom-call | flops 1000000000 | bytes 8388608 | tf_op jit(solution)/shard_map/pallas_call | solution.py:187
  44.7 0.0 collective-permute-done.refs_0_
  44.7 2.7 %collective-permute-done.1.refs_1_ = bf16[4,8,2,16,128]{4,3,2,1,0:T(8,128)(2,1)S(1)} collective-permute-done((bf16[4,8,2,16,128]{4,3,2,1,0:T(8,128)(2,1)}, bf16[4,8,2,16,128]{4,3,2,1,0:T(8,128)(2,1)S(1)}, u32[]{:S(2)}, u32[]{:S(2)}) %collective-permute-start.1) | collective-permute-done | bytes 262176 | tf_op jit(solution)/shard_map/ppermute | solution.py:268
  47.5 0.6 collective-permute-done.2.refs_0_
  48.0 3.9 %collective-permute-done.3.refs_1_ = bf16[4,8,2,16,128]{4,3,2,1,0:T(8,128)(2,1)S(1)} collective-permute-done((bf16[4,8,2,16,128]{4,3,2,1,0:T(8,128)(2,1)}, bf16[4,8,2,16,128]{4,3,2,1,0:T(8,128)(2,1)S(1)}, u32[]{:S(2)}, u32[]{:S(2)}) %collective-permute-start.3) | collective-permute-done | bytes 262176 | tf_op jit(solution)/shard_map/ppermute | solution.py:269
  52.0 0.0 collective-permute-start.6
  52.0 2.0 %collective-permute-start.7 = (bf16[4,8,2,16,128]{4,3,2,1,0:T(8,128)(2,1)S(1)}, bf16[4,8,2,16,128]{4,3,2,1,0:T(8,128)(2,1)S(1)}, u32[]{:S(2)}, u32[]{:S(2)}) collective-permute-start(bf16[4,8,2,16,128]{4,3,2,1,0:T(8,128)(2,1)S(1)} %collective-permute-done.3.refs_1_), channel_id=1, source_target_pairs={{0,8},{8,16},{16,24},{24,0},{32,40},{40,48},{48,56},{56,32},{64,72... | collective-permute-start | bytes 786440 | tf_op jit(solution)/shard_map/ppermute | solution.py:273
  54.0 3.6 %shard_map.131 = (bf16[8,256,128]{2,1,0:T(8,128)(2,1)S(1)}, bf16[8,2,32,128]{3,2,1,0:T(8,128)(2,1)S(1)}, bf16[8,128,256]{2,1,0:T(8,128)(2,1)S(1)}) custom-call(bf16[8,2,256,128]{3,2,1,0:T(8,128)(2,1)S(1)} %get-tuple-element.46.wide, bf16[8,2,32,128]{3,2,1,0:T(8,128)(2,1)S(1)} %get-tuple-element.47.near, f32[8,1,256]{2,1,0:T(1,128)S(1)} %get-tuple-element.48.bias, ...), custom_call_target="tpu_custom_call" | custom-call | flops 4000000000 | bytes 4194304 | tf_op jit(solution)/shard_map/pallas_call | solution.py:206
  57.6 1.3 %collective-permute-start.5 = (bf16[8,128,256]{2,1,0:T(8,128)(2,1)S(1)}, bf16[8,128,256]{2,1,0:T(8,128)(2,1)S(1)}, u32[]{:S(2)}, u32[]{:S(2)}) collective-permute-start(bf16[8,128,256]{2,1,0:T(8,128)(2,1)S(1)} %get-tuple-element.51), channel_id=1, source_target_pairs={{0,24},{8,0},{16,8},{24,16},{32,56},{40,32},{48,40},{56,48},{64,88... | collective-permute-start | bytes 1572872 | tf_op jit(solution)/shard_map/ppermute | solution.py:285
  58.9 2.6 %shard_map.130 = (bf16[8,256,128]{2,1,0:T(8,128)(2,1)S(1)}, bf16[8,2,32,128]{3,2,1,0:T(8,128)(2,1)S(1)}, bf16[8,128,256]{2,1,0:T(8,128)(2,1)S(1)}) custom-call(bf16[8,2,256,128]{3,2,1,0:T(8,128)(2,1)S(1)} %get-tuple-element.40.wide, bf16[8,2,32,128]{3,2,1,0:T(8,128)(2,1)S(1)} %get-tuple-element.41.near, f32[8,1,256]{2,1,0:T(1,128)S(1)} %get-tuple-element.42.bias, ...), custom_call_target="tpu_custom_call" | custom-call | flops 4000000000 | bytes 4194304 | tf_op jit(solution)/shard_map/pallas_call | solution.py:206
  61.6 1.1 %collective-permute-start.4 = (bf16[8,128,256]{2,1,0:T(8,128)(2,1)S(1)}, bf16[8,128,256]{2,1,0:T(8,128)(2,1)S(1)}, u32[]{:S(2)}, u32[]{:S(2)}) collective-permute-start(bf16[8,128,256]{2,1,0:T(8,128)(2,1)S(1)} %get-tuple-element.45), channel_id=1, source_target_pairs={{0,8},{8,16},{16,24},{24,0},{32,40},{40,48},{48,56},{56,32},{64,72... | collective-permute-start | bytes 1572872 | tf_op jit(solution)/shard_map/ppermute | solution.py:285
  62.6 0.0 collective-permute-done.6.refs_0_
  62.6 0.0 collective-permute-done.7.refs_1_
  62.6 2.6 %shard_map.132 = (bf16[8,256,128]{2,1,0:T(8,128)(2,1)S(1)}, bf16[8,2,32,128]{3,2,1,0:T(8,128)(2,1)S(1)}, bf16[8,128,256]{2,1,0:T(8,128)(2,1)S(1)}) custom-call(bf16[8,2,256,128]{3,2,1,0:T(8,128)(2,1)S(1)} %get-tuple-element.52.wide, bf16[8,2,32,128]{3,2,1,0:T(8,128)(2,1)S(1)} %get-tuple-element.53.near, f32[8,1,256]{2,1,0:T(1,128)S(1)} %get-tuple-element.54.bias, ...), custom_call_target="tpu_custom_call" | custom-call | flops 4000000000 | bytes 4194304 | tf_op jit(solution)/shard_map/pallas_call | solution.py:206
  65.3 0.8 collective-permute-start.8
  66.0 2.7 %shard_map.133 = (bf16[8,256,128]{2,1,0:T(8,128)(2,1)S(1)}, bf16[8,2,32,128]{3,2,1,0:T(8,128)(2,1)S(1)}, bf16[8,128,256]{2,1,0:T(8,128)(2,1)S(1)}) custom-call(bf16[8,2,256,128]{3,2,1,0:T(8,128)(2,1)S(1)} %get-tuple-element.56.wide, bf16[8,2,32,128]{3,2,1,0:T(8,128)(2,1)S(1)} %get-tuple-element.57.near, f32[8,1,256]{2,1,0:T(1,128)S(1)} %get-tuple-element.58.bias, ...), custom_call_target="tpu_custom_call" | custom-call | flops 4000000000 | bytes 4194304 | tf_op jit(solution)/shard_map/pallas_call | solution.py:206
  68.7 5.4 %shard_map.134 = (bf16[512,1024]{1,0:T(8,128)(2,1)}, bf16[512,128]{1,0:T(8,128)(2,1)}, bf16[512,128]{1,0:T(8,128)(2,1)}) custom-call(s32[1]{0:T(128)} %bitcast.own_y, s32[1,32]{1,0:T(1,128)S(1)} %copy-done.5, s32[1,32]{1,0:T(1,128)S(1)} %copy-done.6, bf16[8,256,128]{2,1,0:T(8,128)(2,1)S(1)} %get-tuple-element.60.refs_0_, ...), custom_call_target="tpu_custom_call" | custom-call | flops 1000000000 | bytes 4194304 | tf_op jit(solution)/shard_map/pallas_call | solution.py:194
  74.1 0.0 collective-permute-done.5
  74.1 11.9 %collective-permute-done.4 = bf16[8,128,256]{2,1,0:T(8,128)(2,1)S(1)} collective-permute-done((bf16[8,128,256]{2,1,0:T(8,128)(2,1)S(1)}, bf16[8,128,256]{2,1,0:T(8,128)(2,1)S(1)}, u32[]{:S(2)}, u32[]{:S(2)}) %collective-permute-start.4) | collective-permute-done | bytes 524320 | tf_op jit(solution)/shard_map/ppermute | solution.py:285
  86.1 0.0 collective-permute-done.8
  86.1 0.3 add_convert_fusion
  86.4 16.7 %all_to_all.11 = bf16[8,128,256]{2,1,0:T(8,128)(2,1)S(1)} all-to-all(bf16[8,128,256]{2,1,0:T(8,128)(2,1)S(1)} %add_convert_fusion), channel_id=1, replica_groups={{0,32,64,96,128,160,192,224},{8,40,72,104,136,168,200,232},{16,48,80,11..., dimensions={0} | all-to-all | bytes 1048576 | tf_op jit(solution)/shard_map/all_to_all | solution.py:291
  103.1 0.1 reduce_sum.12
  103.1 0.6 fusion
Async XLA Ops:
  0.6 38.0 %copy-start.2 = (bf16[512,128]{1,0:T(8,128)(2,1)S(1)}, bf16[512,128]{1,0:T(8,128)(2,1)}, u32[]{:S(2)}) copy-start(bf16[512,128]{1,0:T(8,128)(2,1)} %key.1) | copy-start | bytes 393220
  2.3 36.3 %copy-start = (bf16[512,1024]{1,0:T(8,128)(2,1)S(1)}, bf16[512,1024]{1,0:T(8,128)(2,1)}, u32[]{:S(2)}) copy-start(bf16[512,1024]{1,0:T(8,128)(2,1)} %query.1) | copy-start | bytes 3145732
  2.3 36.3 %copy-start.1 = (bf16[512,1024]{1,0:T(8,128)(2,1)S(1)}, bf16[512,1024]{1,0:T(8,128)(2,1)}, u32[]{:S(2)}) copy-start(bf16[512,1024]{1,0:T(8,128)(2,1)} %cotangent.1) | copy-start | bytes 3145732
  32.8 11.9 %collective-permute-start = (bf16[4,8,2,16,128]{4,3,2,1,0:T(8,128)(2,1)}, bf16[4,8,2,16,128]{4,3,2,1,0:T(8,128)(2,1)S(1)}, u32[]{:S(2)}, u32[]{:S(2)}) collective-permute-start(bf16[4,8,2,16,128]{4,3,2,1,0:T(8,128)(2,1)} %bitcast.2), channel_id=1, source_target_pairs={{0,24},{8,0},{16,8},{24,16},{32,56},{40,32},{48,40},{56,48},{64,88... | collective-permute-start | bytes 786440 | tf_op jit(solution)/shard_map/ppermute | solution.py:268
  36.5 11.0 %collective-permute-start.1 = (bf16[4,8,2,16,128]{4,3,2,1,0:T(8,128)(2,1)}, bf16[4,8,2,16,128]{4,3,2,1,0:T(8,128)(2,1)S(1)}, u32[]{:S(2)}, u32[]{:S(2)}) collective-permute-start(bf16[4,8,2,16,128]{4,3,2,1,0:T(8,128)(2,1)} %slice.21), channel_id=1, source_target_pairs={{0,24},{8,0},{16,8},{24,16},{32,56},{40,32},{48,40},{56,48},{64,88... | collective-permute-start | bytes 786440 | tf_op jit(solution)/shard_map/ppermute | solution.py:268
  37.3 10.8 %collective-permute-start.2 = (bf16[4,8,2,16,128]{4,3,2,1,0:T(8,128)(2,1)}, bf16[4,8,2,16,128]{4,3,2,1,0:T(8,128)(2,1)}, u32[]{:S(2)}, u32[]{:S(2)}) collective-permute-start(bf16[4,8,2,16,128]{4,3,2,1,0:T(8,128)(2,1)} %bitcast.2), channel_id=1, source_target_pairs={{0,8},{8,16},{16,24},{24,0},{32,40},{40,48},{48,56},{56,32},{64,72... | collective-permute-start | bytes 786440 | tf_op jit(solution)/shard_map/ppermute | solution.py:269
  38.5 13.4 %collective-permute-start.3 = (bf16[4,8,2,16,128]{4,3,2,1,0:T(8,128)(2,1)}, bf16[4,8,2,16,128]{4,3,2,1,0:T(8,128)(2,1)S(1)}, u32[]{:S(2)}, u32[]{:S(2)}) collective-permute-start(bf16[4,8,2,16,128]{4,3,2,1,0:T(8,128)(2,1)} %slice.21), channel_id=1, source_target_pairs={{0,8},{8,16},{16,24},{24,0},{32,40},{40,48},{48,56},{56,32},{64,72... | collective-permute-start | bytes 786440 | tf_op jit(solution)/shard_map/ppermute | solution.py:269
  38.6 0.7 copy-start.4
  38.6 0.7 copy-start.5
  38.6 0.7 copy-start.6
  39.3 0.9 copy-start.3
  52.0 10.7 %collective-permute-start.6 = (bf16[4,8,2,16,128]{4,3,2,1,0:T(8,128)(2,1)S(1)}, bf16[4,8,2,16,128]{4,3,2,1,0:T(8,128)(2,1)S(1)}, u32[]{:S(2)}, u32[]{:S(2)}) collective-permute-start(bf16[4,8,2,16,128]{4,3,2,1,0:T(8,128)(2,1)S(1)} %collective-permute-done.refs_0_), channel_id=1, source_target_pairs={{0,24},{8,0},{16,8},{24,16},{32,56},{40,32},{48,40},{56,48},{64,88... | collective-permute-start | bytes 786440 | tf_op jit(solution)/shard_map/ppermute | solution.py:272
  52.0 10.7 %collective-permute-start.7 = (bf16[4,8,2,16,128]{4,3,2,1,0:T(8,128)(2,1)S(1)}, bf16[4,8,2,16,128]{4,3,2,1,0:T(8,128)(2,1)S(1)}, u32[]{:S(2)}, u32[]{:S(2)}) collective-permute-start(bf16[4,8,2,16,128]{4,3,2,1,0:T(8,128)(2,1)S(1)} %collective-permute-done.3.refs_1_), channel_id=1, source_target_pairs={{0,8},{8,16},{16,24},{24,0},{32,40},{40,48},{48,56},{56,32},{64,72... | collective-permute-start | bytes 786440 | tf_op jit(solution)/shard_map/ppermute | solution.py:273
  57.6 16.5 %collective-permute-start.5 = (bf16[8,128,256]{2,1,0:T(8,128)(2,1)S(1)}, bf16[8,128,256]{2,1,0:T(8,128)(2,1)S(1)}, u32[]{:S(2)}, u32[]{:S(2)}) collective-permute-start(bf16[8,128,256]{2,1,0:T(8,128)(2,1)S(1)} %get-tuple-element.51), channel_id=1, source_target_pairs={{0,24},{8,0},{16,8},{24,16},{32,56},{40,32},{48,40},{56,48},{64,88... | collective-permute-start | bytes 1572872 | tf_op jit(solution)/shard_map/ppermute | solution.py:285
  61.6 24.5 %collective-permute-start.4 = (bf16[8,128,256]{2,1,0:T(8,128)(2,1)S(1)}, bf16[8,128,256]{2,1,0:T(8,128)(2,1)S(1)}, u32[]{:S(2)}, u32[]{:S(2)}) collective-permute-start(bf16[8,128,256]{2,1,0:T(8,128)(2,1)S(1)} %get-tuple-element.45), channel_id=1, source_target_pairs={{0,8},{8,16},{16,24},{24,0},{32,40},{40,48},{48,56},{56,32},{64,72... | collective-permute-start | bytes 1572872 | tf_op jit(solution)/shard_map/ppermute | solution.py:285
  65.3 20.8 %collective-permute-start.8 = (bf16[8,128,256]{2,1,0:T(8,128)(2,1)S(1)}, bf16[8,128,256]{2,1,0:T(8,128)(2,1)S(1)}, u32[]{:S(2)}, u32[]{:S(2)}) collective-permute-start(bf16[8,128,256]{2,1,0:T(8,128)(2,1)S(1)} %get-tuple-element.55), channel_id=1, source_target_pairs={{0,16},{8,24},{16,0},{24,8},{32,48},{40,56},{48,32},{56,40},{64,80... | collective-permute-start | bytes 1572872 | tf_op jit(solution)/shard_map/ppermute | solution.py:285

commit v5 on v4

--- a/solution.py
+++ b/solution.py
@@ -184,14 +184,14 @@
     outs = [shaped(NZ, 2, GROUP * SPAN, HEAD_DIMENSION)] * n
     outs += [shaped(NZ, 2, SPAN, HEAD_DIMENSION)] * n
     outs += [jax.ShapeDtypeStruct((NZ, 1, GROUP * SPAN), jnp.float32)] * n
-    got = call(functools.partial(pack, turns), outs, 4, 4, 3, 10**9, 8 * 2**20)(*args)
+    got = call(functools.partial(pack, turns), outs, 4, 4, 3, 10**8, 2**10)(*args)
     return [got[i::n] for i in range(n)]
 
 
 def unpack_call(turns, own_y, lengths, owners, wide, near, rows):
     outs = [shaped(rows, GROUP * HEAD_DIMENSION)] + [shaped(rows, HEAD_DIMENSION)] * 2
     body = functools.partial(unpack, turns)
-    return call(body, outs, 3, 2 * len(turns), 2, 10**9, 4 * 2**20)(
+    return call(body, outs, 3, 2 * len(turns), 2, 10**6, 2**10)(
         own_y, lengths, owners, *wide, *near
     )
 
@@ -203,7 +203,18 @@
         shaped(NZ, PROMPT, 2 * HEAD_DIMENSION),
     ]
     body = functools.partial(attend, len(parts))
-    return call(body, outs, 0, 3 + len(parts), 0, 4 * 10**9, 2**22)(*packed, *parts)
+    return call(body, outs, 0, 3 + len(parts), 0, 10**6, 2**10)(*packed, *parts)
+
+
+def split_call(column):
+    half = NZ // 2
+
+    def split(column, low, high):
+        low[...] = column[:half]
+        high[...] = column[half:]
+
+    outs = [shaped(half, *column.shape[1:])] * 2
+    return call(split, outs, 0, 1, 0, 0, 2**20)(column)
 
 
 def spread_call(keys, values):
@@ -264,19 +275,23 @@
         response_keys,
         response_values,
     )
-    halves = (column[:half], lax.optimization_barrier(column)[half:])
-    after = [lax.ppermute(a, "dp", along_y(-1)) for a in halves]
-    before = [lax.ppermute(a, "dp", along_y(1)) for a in halves]
+    column, own = lax.optimization_barrier((column, own))
+    low, high = split_call(column)
+    after_low = lax.ppermute(low, "dp", along_y(-1))
+    before_high = lax.ppermute(high, "dp", along_y(1))
+    across = [
+        lax.ppermute(after_low, "dp", along_y(-1)),
+        lax.ppermute(before_high, "dp", along_y(1)),
+    ]
+    after = [after_low, lax.ppermute(high, "dp", along_y(-1))]
+    before = [lax.ppermute(low, "dp", along_y(1)), before_high]
     after, before = lax.optimization_barrier((after, before))
-    across = [
-        lax.ppermute(after[0], "dp", along_y(-1)),
-        lax.ppermute(before[1], "dp", along_y(1)),
-    ]
     dq, dnear, sums = [], [], []
+    order = (1, 2, 3, 0)
     for turn, packed, prompts in (
         (1, next_one, after),
+        (2, far, across),
         (3, last_one, before),
-        (2, far, across),
         (0, own, [column]),
     ):
         q_part, near_part, prompt_part = attend_call(packed, prompts)
@@ -284,7 +299,7 @@
         dnear.append(near_part)
         sums.append(lax.ppermute(prompt_part, "dp", along_y(turn)) if turn else prompt_part)
     dq, dk, dv = unpack_call(
-        (1, 3, 2, 0), own_y, resp_len, resp_owner, dq, dnear, queries.shape[0]
+        order, own_y, resp_len, resp_owner, dq, dnear, queries.shape[0]
     )
     summed = sum(a.astype(jnp.float32) for a in sums).astype(jnp.bfloat16)
     summed, dq, dk, dv = lax.optimization_barrier((summed, dq, dk, dv))

time: 104 us -> 101 us (0.971)
  blocking collectives: 46.4 us -> 17.2 us
  starting transfers between devices: 10.2 us -> 24.6 us
  waiting for transfers between devices: 19.2 us -> 28.3 us
  local copies, waits for them, and re-layouts: 3.65 us -> 6.94 us
    all_to_all x1 -> x0, blocking collectives: 29.7 us -> none  [per_device(): lax.all_to_all(spread_call(prompt_key_rows, prompt_value_rows), ('dp', 'h...]
    all_to_all x0 -> x1, starting transfers between devices: none -> 12.2 us  [per_device(): lax.all_to_all(spread_call(prompt_key_rows, prompt_value_rows), ('dp', 'h...]
    all_to_all x0 -> x1, waiting for transfers between devices: none -> 7.86 us  [per_device(): lax.all_to_all(spread_call(prompt_key_rows, prompt_value_rows), ('dp', 'h...]
    unnamed x14 -> x22, local copies, waits for them, and re-layouts: 1.58 us -> 6.31 us
    ppermute x6, starting transfers between devices: 7.1 us -> 10 us  [the longest x1 3.69 us: per_device(): lax.ppermute(after_low, 'dp', along_y(-1))]
    ppermute x6, waiting for transfers between devices: 7.24 us -> 9.1 us  [the longest x1 3.73 us: per_device(): before = [lax.ppermute(low, 'dp', along_y(1)), before_high]]
    slice x2 -> x0, local copies, waits for them, and re-layouts: 1.44 us -> none  [per_device(): halves = (column[:half], lax.optimization_barrier(column)[half:])]
    pallas_call x6 -> x7, Pallas kernels: 21.5 us -> 20.6 us  [the longest x4 10.6 us: attend_call(): call(body, outs, 0, 3 + len(parts), 0, 10 ** 6, 2 ** 10)(*packed, *parts)]
  transfers between devices with their start and end apart: 9 -> 10, of which waited for: 4 -> 5; matrix products, arithmetic and copies ran while one was open for 1% -> 0% of each run, Pallas kernels for 21% -> 20%
where the time goes in v5:
time: 101 us; the launch traced here: 100 us
  waiting for transfers between devices  28.3 us (28%)
  starting transfers between devices  24.6 us (24%)
  Pallas kernels  22.3 us (22%)
  blocking collectives  17.2 us (17%)
  local copies, waits for them, and re-layouts  6.94 us (7%)
    all_to_all x1, blocking collectives, per_device(): lax.all_to_all(summed, 'dp', split_axis=0, concat_axis=0, axis_index_grou...  17.2 us
    all_to_all x1, starting transfers between devices, per_device(): lax.all_to_all(spread_call(prompt_key_rows, prompt_value_rows), ('dp', 'h...  12.2 us
    ppermute x3, waiting for transfers between devices, per_device(): lax.ppermute(prompt_part, 'dp', along_y(turn))  11.3 us
    pallas_call x4, Pallas kernels, attend_call(): call(body, outs, 0, 3 + len(parts), 0, 10 ** 6, 2 ** 10)(*packed, *parts)  10.6 us
    all_to_all x1, waiting for transfers between devices, per_device(): lax.all_to_all(spread_call(prompt_key_rows, prompt_value_rows), ('dp', 'h...  7.86 us
    unnamed x22, local copies, waits for them, and re-layouts  6.31 us
    pallas_call x1, Pallas kernels, unpack_call(): call(body, outs, 3, 2 * len(turns), 2, 10 ** 6, 2 ** 10)  5.42 us
    pallas_call x1, Pallas kernels, pack_call(): call(functools.partial(pack, turns), outs, 4, 4, 3, 10 ** 8, 2 ** 10)(*args)  4.56 us
  transfers between devices with their start and end apart: 10, of which 5 were waited for; matrix products, arithmetic and copies ran while one was open for 0% of the time, Pallas kernels for 20%

profile of v5, /device:TPU:2, one launch (start us, length us, event | category | flops | bytes accessed | tf_op | source)
XLA Modules:
  0.0 100.5 jit_solution(1626256939820175571)
XLA Ops:
  0.6 1.6 %shard_map.129 = bf16[64,2,16,128]{3,2,1,0:T(8,128)(2,1)} custom-call(bf16[16,1024]{1,0:T(8,128)(2,1)} %keys.1, bf16[16,1024]{1,0:T(8,128)(2,1)} %values.1), custom_call_target="tpu_custom_call" | custom-call | tf_op jit(solution)/shard_map/pallas_call | solution.py:222
  2.3 0.0 copy-start.6
  2.3 0.0 copy-start.7
  2.3 12.2 %all-to-all-start = ((bf16[64,2,16,128]{3,2,1,0:T(8,128)(2,1)}), bf16[64,2,16,128]{3,2,1,0:T(8,128)(2,1)S(1)}, u32[]{:S(2)}, u32[]{:S(2)}) async-start(bf16[64,2,16,128]{3,2,1,0:T(8,128)(2,1)} %shard_map.129), calls=%async_computation | async-start | bytes 1048576 | tf_op jit(solution)/shard_map/all_to_all | solution.py:256
  14.5 0.0 copy-start.8
  14.5 0.0 copy-start.9
  14.5 0.0 copy-start.10
  14.5 0.0 copy-done.6
  14.5 0.0 copy-done.7
  14.5 0.6 copy-done.8
  15.1 0.0 copy-done.9
  15.2 0.0 copy-done.10
  15.2 1.2 %copy-done.4 = bf16[512,1024]{1,0:T(8,128)(2,1)S(1)} copy-done((bf16[512,1024]{1,0:T(8,128)(2,1)S(1)}, bf16[512,1024]{1,0:T(8,128)(2,1)}, u32[]{:S(2)}) %copy-start.4) | copy-done | bytes 1048600
  16.4 1.2 %copy-done.5 = bf16[512,1024]{1,0:T(8,128)(2,1)S(1)} copy-done((bf16[512,1024]{1,0:T(8,128)(2,1)S(1)}, bf16[512,1024]{1,0:T(8,128)(2,1)}, u32[]{:S(2)}) %copy-start.5) | copy-done | bytes 1048600
  17.6 4.6 %shard_map.128 = (bf16[8,2,256,128]{3,2,1,0:T(8,128)(2,1)S(1)}, bf16[8,2,256,128]{3,2,1,0:T(8,128)(2,1)S(1)}, bf16[8,2,256,128]{3,2,1,0:T(8,128)(2,1)S(1)}, bf16...) custom-call(s32[1]{0:T(128)} %bitcast.own_y, ...), custom_call_target="tpu_custom_call" | custom-call | flops 100000000 | bytes 1024 | tf_op jit(solution)/shard_map/pallas_call | solution.py:187
  22.2 0.0 copy-start
  22.2 1.0 copy-done
  23.2 1.0 %copy-done.2 = bf16[8,2,256,128]{3,2,1,0:T(8,128)(2,1)} copy-done((bf16[8,2,256,128]{3,2,1,0:T(8,128)(2,1)}, bf16[8,2,256,128]{3,2,1,0:T(8,128)(2,1)S(1)}, u32[]{:S(2)}) %copy-start.2) | copy-done | bytes 1048600
  24.2 7.9 %all-to-all-done = bf16[64,2,16,128]{3,2,1,0:T(8,128)(2,1)S(1)} async-done(((bf16[64,2,16,128]{3,2,1,0:T(8,128)(2,1)}), bf16[64,2,16,128]{3,2,1,0:T(8,128)(2,1)S(1)}, u32[]{:S(2)}, u32[]{:S(2)}) %all-to-all-start) | async-done | bytes 524320 | tf_op jit(solution)/shard_map/all_to_all | solution.py:256
  32.1 3.1 %collective-permute-start = (bf16[4,8,2,16,128]{4,3,2,1,0:T(8,128)(2,1)S(1)}, bf16[4,8,2,16,128]{4,3,2,1,0:T(8,128)(2,1)S(1)}, u32[]{:S(2)}, u32[]{:S(2)}) collective-permute-start(bf16[4,8,2,16,128]{4,3,2,1,0:T(8,128)(2,1)S(1)} %get-tuple-element.53), channel_id=1, source_target_pairs={{0,24},{8,0},{16,8},{24,16},{32,56},{40,32},{48,40},{56,48},{64,88... | collective-permute-start | bytes 786440 | tf_op jit(solution)/shard_map/ppermute | solution.py:280
  35.2 0.0 collective-permute-start.3
  35.2 3.2 %collective-permute-start.1 = (bf16[4,8,2,16,128]{4,3,2,1,0:T(8,128)(2,1)S(1)}, bf16[4,8,2,16,128]{4,3,2,1,0:T(8,128)(2,1)S(1)}, u32[]{:S(2)}, u32[]{:S(2)}) collective-permute-start(bf16[4,8,2,16,128]{4,3,2,1,0:T(8,128)(2,1)S(1)} %get-tuple-element.54), channel_id=1, source_target_pairs={{0,24},{8,0},{16,8},{24,16},{32,56},{40,32},{48,40},{56,48},{64,88... | collective-permute-start | bytes 786440 | tf_op jit(solution)/shard_map/ppermute | solution.py:286
  38.4 0.0 collective-permute-start.2
  38.4 3.4 %collective-permute-done.refs_0_ = bf16[4,8,2,16,128]{4,3,2,1,0:T(8,128)(2,1)S(1)} collective-permute-done((bf16[4,8,2,16,128]{4,3,2,1,0:T(8,128)(2,1)S(1)}, bf16[4,8,2,16,128]{4,3,2,1,0:T(8,128)(2,1)S(1)}, u32[]{:S(2)}, u32[]{:S(2)}) %collective-permute-start) | collective-permute-done | bytes 262176 | tf_op jit(solution)/shard_map/ppermute | solution.py:280
  41.9 3.7 %collective-permute-start.5 = (bf16[4,8,2,16,128]{4,3,2,1,0:T(8,128)(2,1)S(1)}, bf16[4,8,2,16,128]{4,3,2,1,0:T(8,128)(2,1)S(1)}, u32[]{:S(2)}, u32[]{:S(2)}) collective-permute-start(bf16[4,8,2,16,128]{4,3,2,1,0:T(8,128)(2,1)S(1)} %collective-permute-done.refs_0_), channel_id=1, source_target_pairs={{0,24},{8,0},{16,8},{24,16},{32,56},{40,32},{48,40},{56,48},{64,88... | collective-permute-start | bytes 786440 | tf_op jit(solution)/shard_map/ppermute | solution.py:283
  45.5 0.0 collective-permute-done.3.refs_1_
  45.6 0.0 collective-permute-start.6
  45.6 1.9 %collective-permute-done.1.refs_1_ = bf16[4,8,2,16,128]{4,3,2,1,0:T(8,128)(2,1)S(1)} collective-permute-done((bf16[4,8,2,16,128]{4,3,2,1,0:T(8,128)(2,1)S(1)}, bf16[4,8,2,16,128]{4,3,2,1,0:T(8,128)(2,1)S(1)}, u32[]{:S(2)}, u32[]{:S(2)}) %collective-permute-start.1) | collective-permute-done | bytes 262176 | tf_op jit(solution)/shard_map/ppermute | solution.py:286
  47.5 3.7 %collective-permute-done.2.refs_0_ = bf16[4,8,2,16,128]{4,3,2,1,0:T(8,128)(2,1)S(1)} collective-permute-done((bf16[4,8,2,16,128]{4,3,2,1,0:T(8,128)(2,1)S(1)}, bf16[4,8,2,16,128]{4,3,2,1,0:T(8,128)(2,1)S(1)}, u32[]{:S(2)}, u32[]{:S(2)}) %collective-permute-start.2) | collective-permute-done | bytes 262176 | tf_op jit(solution)/shard_map/ppermute | solution.py:287
  51.2 1.2 %copy-done.3 = bf16[8,2,256,128]{3,2,1,0:T(8,128)(2,1)S(1)} copy-done((bf16[8,2,256,128]{3,2,1,0:T(8,128)(2,1)S(1)}, bf16[8,2,256,128]{3,2,1,0:T(8,128)(2,1)}, u32[]{:S(2)}) %copy-start.3) | copy-done | bytes 1048600
  52.4 2.6 %shard_map.133 = (bf16[8,256,128]{2,1,0:T(8,128)(2,1)S(1)}, bf16[8,2,32,128]{3,2,1,0:T(8,128)(2,1)S(1)}, bf16[8,128,256]{2,1,0:T(8,128)(2,1)S(1)}) custom-call(bf16[8,2,256,128]{3,2,1,0:T(8,128)(2,1)S(1)} %copy-done.3, bf16[8,2,32,128]{3,2,1,0:T(8,128)(2,1)S(1)} %get-tuple-element.63.near, f32[8,1,256]{2,1,0:T(1,128)S(1)} %get-tuple-element.64.bias, ...), custom_call_target="tpu_custom_call" | custom-call | flops 1000000 | bytes 1024 | tf_op jit(solution)/shard_map/pallas_call | solution.py:206
  55.1 0.1 collective-permute-start.8
  55.2 0.0 copy-done.1
  55.2 2.6 %shard_map.131 = (bf16[8,256,128]{2,1,0:T(8,128)(2,1)S(1)}, bf16[8,2,32,128]{3,2,1,0:T(8,128)(2,1)S(1)}, bf16[8,128,256]{2,1,0:T(8,128)(2,1)S(1)}) custom-call(bf16[8,2,256,128]{3,2,1,0:T(8,128)(2,1)S(1)} %copy-done.1, bf16[8,2,32,128]{3,2,1,0:T(8,128)(2,1)S(1)} %get-tuple-element.47.near, f32[8,1,256]{2,1,0:T(1,128)S(1)} %get-tuple-element.48.bias, ...), custom_call_target="tpu_custom_call" | custom-call | flops 1000000 | bytes 1024 | tf_op jit(solution)/shard_map/pallas_call | solution.py:206
  57.8 2.3 %collective-permute-start.4 = (bf16[8,128,256]{2,1,0:T(8,128)(2,1)S(1)}, bf16[8,128,256]{2,1,0:T(8,128)(2,1)S(1)}, u32[]{:S(2)}, u32[]{:S(2)}) collective-permute-start(bf16[8,128,256]{2,1,0:T(8,128)(2,1)S(1)} %get-tuple-element.57), channel_id=1, source_target_pairs={{0,8},{8,16},{16,24},{24,0},{32,40},{40,48},{48,56},{56,32},{64,72... | collective-permute-start | bytes 1572872 | tf_op jit(solution)/shard_map/ppermute | solution.py:300
  60.1 0.0 collective-permute-done.5.refs_0_
  60.1 0.0 collective-permute-done.6.refs_1_
  60.1 2.6 %shard_map.132 = (bf16[8,256,128]{2,1,0:T(8,128)(2,1)S(1)}, bf16[8,2,32,128]{3,2,1,0:T(8,128)(2,1)S(1)}, bf16[8,128,256]{2,1,0:T(8,128)(2,1)S(1)}) custom-call(bf16[8,2,256,128]{3,2,1,0:T(8,128)(2,1)S(1)} %get-tuple-element.58.wide, bf16[8,2,32,128]{3,2,1,0:T(8,128)(2,1)S(1)} %get-tuple-element.59.near, f32[8,1,256]{2,1,0:T(1,128)S(1)} %get-tuple-element.60.bias, ...), custom_call_target="tpu_custom_call" | custom-call | flops 1000000 | bytes 1024 | tf_op jit(solution)/shard_map/pallas_call | solution.py:206
  62.8 0.1 collective-permute-start.7
  62.9 2.7 %shard_map.134 = (bf16[8,256,128]{2,1,0:T(8,128)(2,1)S(1)}, bf16[8,2,32,128]{3,2,1,0:T(8,128)(2,1)S(1)}, bf16[8,128,256]{2,1,0:T(8,128)(2,1)S(1)}) custom-call(bf16[8,2,256,128]{3,2,1,0:T(8,128)(2,1)S(1)} %get-tuple-element.68.wide, bf16[8,2,32,128]{3,2,1,0:T(8,128)(2,1)S(1)} %get-tuple-element.69.near, f32[8,1,256]{2,1,0:T(1,128)S(1)} %get-tuple-element.70.bias, ...), custom_call_target="tpu_custom_call" | custom-call | flops 1000000 | bytes 1024 | tf_op jit(solution)/shard_map/pallas_call | solution.py:206
  65.5 5.4 %shard_map.135 = (bf16[512,1024]{1,0:T(8,128)(2,1)}, bf16[512,128]{1,0:T(8,128)(2,1)}, bf16[512,128]{1,0:T(8,128)(2,1)}) custom-call(s32[1]{0:T(128)} %bitcast.own_y, s32[1,32]{1,0:T(1,128)S(1)} %copy-done.8, s32[1,32]{1,0:T(1,128)S(1)} %copy-done.9, bf16[8,256,128]{2,1,0:T(8,128)(2,1)S(1)} %get-tuple-element.72.refs_0_, ...), custom_call_target="tpu_custom_call" | custom-call | flops 1000000 | bytes 1024 | tf_op jit(solution)/shard_map/pallas_call | solution.py:194
  71.0 0.0 collective-permute-done.8
  71.0 11.3 %collective-permute-done.4 = bf16[8,128,256]{2,1,0:T(8,128)(2,1)S(1)} collective-permute-done((bf16[8,128,256]{2,1,0:T(8,128)(2,1)S(1)}, bf16[8,128,256]{2,1,0:T(8,128)(2,1)S(1)}, u32[]{:S(2)}, u32[]{:S(2)}) %collective-permute-start.4) | collective-permute-done | bytes 524320 | tf_op jit(solution)/shard_map/ppermute | solution.py:300
  82.3 0.0 collective-permute-done.7
  82.3 0.3 add_convert_fusion
  82.6 17.2 %all_to_all.10 = bf16[8,128,256]{2,1,0:T(8,128)(2,1)S(1)} all-to-all(bf16[8,128,256]{2,1,0:T(8,128)(2,1)S(1)} %add_convert_fusion), channel_id=1, replica_groups={{0,32,64,96,128,160,192,224},{8,40,72,104,136,168,200,232},{16,48,80,11..., dimensions={0} | all-to-all | bytes 1048576 | tf_op jit(solution)/shard_map/all_to_all | solution.py:306
  99.8 0.1 reduce_sum.12
  99.8 0.6 fusion
  (6 shorter events, 0.0 us)
Async XLA Ops:
  2.3 12.2 %copy-start.6 = (bf16[512,128]{1,0:T(8,128)(2,1)S(1)}, bf16[512,128]{1,0:T(8,128)(2,1)}, u32[]{:S(2)}) copy-start(bf16[512,128]{1,0:T(8,128)(2,1)} %key.1) | copy-start | bytes 393220
  2.3 12.2 %copy-start.7 = (bf16[512,128]{1,0:T(8,128)(2,1)S(1)}, bf16[512,128]{1,0:T(8,128)(2,1)}, u32[]{:S(2)}) copy-start(bf16[512,128]{1,0:T(8,128)(2,1)} %value.1) | copy-start | bytes 393220
  2.3 29.7 %all-to-all-start = ((bf16[64,2,16,128]{3,2,1,0:T(8,128)(2,1)}), bf16[64,2,16,128]{3,2,1,0:T(8,128)(2,1)S(1)}, u32[]{:S(2)}, u32[]{:S(2)}) async-start(bf16[64,2,16,128]{3,2,1,0:T(8,128)(2,1)} %shard_map.129), calls=%async_computation | async-start | bytes 1048576 | tf_op jit(solution)/shard_map/all_to_all | solution.py:256
  14.5 0.7 copy-start.8
  14.5 0.7 copy-start.9
  14.5 0.7 copy-start.10
  15.2 1.2 %copy-start.4 = (bf16[512,1024]{1,0:T(8,128)(2,1)S(1)}, bf16[512,1024]{1,0:T(8,128)(2,1)}, u32[]{:S(2)}) copy-start(bf16[512,1024]{1,0:T(8,128)(2,1)} %query.1) | copy-start | bytes 3145732
  16.4 1.2 %copy-start.5 = (bf16[512,1024]{1,0:T(8,128)(2,1)S(1)}, bf16[512,1024]{1,0:T(8,128)(2,1)}, u32[]{:S(2)}) copy-start(bf16[512,1024]{1,0:T(8,128)(2,1)} %cotangent.1) | copy-start | bytes 3145732
  22.2 1.0 copy-start
  23.2 1.0 %copy-start.2 = (bf16[8,2,256,128]{3,2,1,0:T(8,128)(2,1)}, bf16[8,2,256,128]{3,2,1,0:T(8,128)(2,1)S(1)}, u32[]{:S(2)}) copy-start(bf16[8,2,256,128]{3,2,1,0:T(8,128)(2,1)S(1)} %get-tuple-element.62.wide) | copy-start | bytes 3145732
  32.0 23.1 %copy-start.1 = (bf16[8,2,256,128]{3,2,1,0:T(8,128)(2,1)S(1)}, bf16[8,2,256,128]{3,2,1,0:T(8,128)(2,1)}, u32[]{:S(2)}) copy-start(bf16[8,2,256,128]{3,2,1,0:T(8,128)(2,1)} %copy-done) | copy-start | bytes 3145732
  32.1 9.8 %collective-permute-start = (bf16[4,8,2,16,128]{4,3,2,1,0:T(8,128)(2,1)S(1)}, bf16[4,8,2,16,128]{4,3,2,1,0:T(8,128)(2,1)S(1)}, u32[]{:S(2)}, u32[]{:S(2)}) collective-permute-start(bf16[4,8,2,16,128]{4,3,2,1,0:T(8,128)(2,1)S(1)} %get-tuple-element.53), channel_id=1, source_target_pairs={{0,24},{8,0},{16,8},{24,16},{32,56},{40,32},{48,40},{56,48},{64,88... | collective-permute-start | bytes 786440 | tf_op jit(solution)/shard_map/ppermute | solution.py:280
  35.2 10.4 %collective-permute-start.3 = (bf16[4,8,2,16,128]{4,3,2,1,0:T(8,128)(2,1)S(1)}, bf16[4,8,2,16,128]{4,3,2,1,0:T(8,128)(2,1)S(1)}, u32[]{:S(2)}, u32[]{:S(2)}) collective-permute-start(bf16[4,8,2,16,128]{4,3,2,1,0:T(8,128)(2,1)S(1)} %get-tuple-element.54), channel_id=1, source_target_pairs={{0,8},{8,16},{16,24},{24,0},{32,40},{40,48},{48,56},{56,32},{64,72... | collective-permute-start | bytes 786440 | tf_op jit(solution)/shard_map/ppermute | solution.py:281
  35.2 12.3 %collective-permute-start.1 = (bf16[4,8,2,16,128]{4,3,2,1,0:T(8,128)(2,1)S(1)}, bf16[4,8,2,16,128]{4,3,2,1,0:T(8,128)(2,1)S(1)}, u32[]{:S(2)}, u32[]{:S(2)}) collective-permute-start(bf16[4,8,2,16,128]{4,3,2,1,0:T(8,128)(2,1)S(1)} %get-tuple-element.54), channel_id=1, source_target_pairs={{0,24},{8,0},{16,8},{24,16},{32,56},{40,32},{48,40},{56,48},{64,88... | collective-permute-start | bytes 786440 | tf_op jit(solution)/shard_map/ppermute | solution.py:286
  38.4 12.8 %collective-permute-start.2 = (bf16[4,8,2,16,128]{4,3,2,1,0:T(8,128)(2,1)S(1)}, bf16[4,8,2,16,128]{4,3,2,1,0:T(8,128)(2,1)S(1)}, u32[]{:S(2)}, u32[]{:S(2)}) collective-permute-start(bf16[4,8,2,16,128]{4,3,2,1,0:T(8,128)(2,1)S(1)} %get-tuple-element.53), channel_id=1, source_target_pairs={{0,8},{8,16},{16,24},{24,0},{32,40},{40,48},{48,56},{56,32},{64,72... | collective-permute-start | bytes 786440 | tf_op jit(solution)/shard_map/ppermute | solution.py:287
  41.9 18.3 %collective-permute-start.5 = (bf16[4,8,2,16,128]{4,3,2,1,0:T(8,128)(2,1)S(1)}, bf16[4,8,2,16,128]{4,3,2,1,0:T(8,128)(2,1)S(1)}, u32[]{:S(2)}, u32[]{:S(2)}) collective-permute-start(bf16[4,8,2,16,128]{4,3,2,1,0:T(8,128)(2,1)S(1)} %collective-permute-done.refs_0_), channel_id=1, source_target_pairs={{0,24},{8,0},{16,8},{24,16},{32,56},{40,32},{48,40},{56,48},{64,88... | collective-permute-start | bytes 786440 | tf_op jit(solution)/shard_map/ppermute | solution.py:283
  45.6 14.5 %collective-permute-start.6 = (bf16[4,8,2,16,128]{4,3,2,1,0:T(8,128)(2,1)S(1)}, bf16[4,8,2,16,128]{4,3,2,1,0:T(8,128)(2,1)S(1)}, u32[]{:S(2)}, u32[]{:S(2)}) collective-permute-start(bf16[4,8,2,16,128]{4,3,2,1,0:T(8,128)(2,1)S(1)} %collective-permute-done.3.refs_1_), channel_id=1, source_target_pairs={{0,8},{8,16},{16,24},{24,0},{32,40},{40,48},{48,56},{56,32},{64,72... | collective-permute-start | bytes 786440 | tf_op jit(solution)/shard_map/ppermute | solution.py:284
  51.2 1.2 %copy-start.3 = (bf16[8,2,256,128]{3,2,1,0:T(8,128)(2,1)S(1)}, bf16[8,2,256,128]{3,2,1,0:T(8,128)(2,1)}, u32[]{:S(2)}) copy-start(bf16[8,2,256,128]{3,2,1,0:T(8,128)(2,1)} %copy-done.2) | copy-start | bytes 3145732
  55.1 15.9 %collective-permute-start.8 = (bf16[8,128,256]{2,1,0:T(8,128)(2,1)S(1)}, bf16[8,128,256]{2,1,0:T(8,128)(2,1)S(1)}, u32[]{:S(2)}, u32[]{:S(2)}) collective-permute-start(bf16[8,128,256]{2,1,0:T(8,128)(2,1)S(1)} %get-tuple-element.67), channel_id=1, source_target_pairs={{0,24},{8,0},{16,8},{24,16},{32,56},{40,32},{48,40},{56,48},{64,88... | collective-permute-start | bytes 1572872 | tf_op jit(solution)/shard_map/ppermute | solution.py:300
  57.8 24.4 %collective-permute-start.4 = (bf16[8,128,256]{2,1,0:T(8,128)(2,1)S(1)}, bf16[8,128,256]{2,1,0:T(8,128)(2,1)S(1)}, u32[]{:S(2)}, u32[]{:S(2)}) collective-permute-start(bf16[8,128,256]{2,1,0:T(8,128)(2,1)S(1)} %get-tuple-element.57), channel_id=1, source_target_pairs={{0,8},{8,16},{16,24},{24,0},{32,40},{40,48},{48,56},{56,32},{64,72... | collective-permute-start | bytes 1572872 | tf_op jit(solution)/shard_map/ppermute | solution.py:300
  62.8 19.5 %collective-permute-start.7 = (bf16[8,128,256]{2,1,0:T(8,128)(2,1)S(1)}, bf16[8,128,256]{2,1,0:T(8,128)(2,1)S(1)}, u32[]{:S(2)}, u32[]{:S(2)}) collective-permute-start(bf16[8,128,256]{2,1,0:T(8,128)(2,1)S(1)} %get-tuple-element.61), channel_id=1, source_target_pairs={{0,16},{8,24},{16,0},{24,8},{32,48},{40,56},{48,32},{56,40},{64,80... | collective-permute-start | bytes 1572872 | tf_op jit(solution)/shard_map/ppermute | solution.py:300

commit v6 on v5

--- a/solution.py
+++ b/solution.py
@@ -97,8 +97,9 @@
             prompt = i * NY + y
             window, offset = window_of(first_of[prompt], rows)
             put = one_hot((WINDOW, SPAN), 1, offset, count_of[prompt])
+            turned = wide_ref[i].T
             grads = jnp.concatenate(
-                [wide_ref[i, h * SPAN : (h + 1) * SPAN, :] for h in range(GROUP)], axis=1
+                [turned[h * SPAN : (h + 1) * SPAN] for h in range(GROUP)], axis=1
             )
             dq[window, :] = dq[window, :] + dot(put, grads).astype(jnp.bfloat16)
             for j, ref in enumerate((dk, dv)):
@@ -138,7 +139,7 @@
         probs = probs.astype(jnp.bfloat16)
         k_grad = (dot(slopes, q) * scale).astype(jnp.bfloat16)
         v_grad = dot(probs, g).astype(jnp.bfloat16)
-        dq[z] = (dot(slopes, k, ((0,), (0,))) * scale).astype(jnp.bfloat16)
+        dq[z] = (dot(k, slopes, ((0,), (0,))) * scale).astype(jnp.bfloat16)
         dprompt[z, :, :HEAD_DIMENSION] = k_grad[:PROMPT]
         dprompt[z, :, HEAD_DIMENSION:] = v_grad[:PROMPT]
         dnear[z, 0] = k_grad[PROMPT:]
@@ -198,7 +199,7 @@
 
 def attend_call(packed, parts):
     outs = [
-        shaped(NZ, GROUP * SPAN, HEAD_DIMENSION),
+        shaped(NZ, HEAD_DIMENSION, GROUP * SPAN),
         shaped(NZ, 2, SPAN, HEAD_DIMENSION),
         shaped(NZ, PROMPT, 2 * HEAD_DIMENSION),
     ]
@@ -261,21 +262,13 @@
         axis_index_groups=same_y_head,
         tiled=True,
     ).reshape(NZ, HEADS, 2, part, HEAD_DIMENSION)
-    turns = (0, 1, 3, 2)
     own_y = lax.rem(lax.axis_index("dp"), NY).reshape(1).astype(jnp.int32)
     masks = block_mask.reshape(block_mask.shape[:2])
-    own, next_one, last_one, far = pack_call(
-        turns,
-        own_y,
-        resp_len,
-        resp_owner,
-        masks,
-        queries,
-        output_cotangent,
-        response_keys,
-        response_values,
-    )
-    column, own = lax.optimization_barrier((column, own))
+    scalars = (own_y, resp_len, resp_owner, masks)
+    rows_of = (queries, output_cotangent, response_keys, response_values)
+    next_one, last_one = pack_call((1, 3), *scalars, *rows_of)
+    far, own = pack_call((2, 0), *scalars, *rows_of)
+    column, next_one = lax.optimization_barrier((column, next_one))
     low, high = split_call(column)
     after_low = lax.ppermute(low, "dp", along_y(-1))
     before_high = lax.ppermute(high, "dp", along_y(1))

time: 101 us -> 99.1 us (0.981)
  local copies, waits for them, and re-layouts: 6.94 us -> 4.48 us
  Pallas kernels: 22.3 us -> 23.4 us
    all_to_all x1, waiting for transfers between devices: 7.86 us -> 11 us  [per_device(): lax.all_to_all(spread_call(prompt_key_rows, prompt_value_rows), ('dp', 'h...]
    unnamed x22 -> x24, local copies, waits for them, and re-layouts: 6.31 us -> 3.84 us
    ppermute x1, waiting for transfers between devices: 1.88 us -> 0.01 us  [per_device(): after = [after_low, lax.ppermute(high, 'dp', along_y(-1))]]
    pallas_call x1, Pallas kernels: 5.42 us -> 6.43 us  [unpack_call(): call(body, outs, 3, 2 * len(turns), 2, 10 ** 6, 2 ** 10)]
    pallas_call x1 -> x2, Pallas kernels: 4.56 us -> 5.38 us  [pack_call(): call(functools.partial(pack, turns), outs, 4, 4, 3, 10 ** 8, 2 ** 10)(*args)]
  transfers between devices with their start and end apart: 10 -> 10, of which waited for: 5 -> 4; matrix products, arithmetic and copies ran while one was open for 0% -> 0% of each run, Pallas kernels for 20% -> 22%
where the time goes in v6:
time: 99.1 us; the launch traced here: 98.6 us
  waiting for transfers between devices  28.1 us (28%)
  starting transfers between devices  24.6 us (25%)
  Pallas kernels  23.4 us (24%)
  blocking collectives  16.8 us (17%)
  local copies, waits for them, and re-layouts  4.48 us (5%)
    all_to_all x1, blocking collectives, per_device(): lax.all_to_all(summed, 'dp', split_axis=0, concat_axis=0, axis_index_grou...  16.8 us
    all_to_all x1, starting transfers between devices, per_device(): lax.all_to_all(spread_call(prompt_key_rows, prompt_value_rows), ('dp', 'h...  12.2 us
    all_to_all x1, waiting for transfers between devices, per_device(): lax.all_to_all(spread_call(prompt_key_rows, prompt_value_rows), ('dp', 'h...  11 us
    ppermute x3, waiting for transfers between devices, per_device(): lax.ppermute(prompt_part, 'dp', along_y(turn))  10.7 us
    pallas_call x4, Pallas kernels, attend_call(): call(body, outs, 0, 3 + len(parts), 0, 10 ** 6, 2 ** 10)(*packed, *parts)  9.79 us
    pallas_call x1, Pallas kernels, unpack_call(): call(body, outs, 3, 2 * len(turns), 2, 10 ** 6, 2 ** 10)  6.43 us
    pallas_call x2, Pallas kernels, pack_call(): call(functools.partial(pack, turns), outs, 4, 4, 3, 10 ** 8, 2 ** 10)(*args)  5.38 us
    unnamed x24, local copies, waits for them, and re-layouts  3.84 us
  transfers between devices with their start and end apart: 10, of which 4 were waited for; matrix products, arithmetic and copies ran while one was open for 0% of the time, Pallas kernels for 22%

profile of v6, /device:TPU:2, one launch (start us, length us, event | category | flops | bytes accessed | tf_op | source)
XLA Modules:
  0.0 98.6 jit_solution(18229034582341566121)
XLA Ops:
  0.6 1.7 %shard_map.128 = bf16[64,2,16,128]{3,2,1,0:T(8,128)(2,1)} custom-call(bf16[16,1024]{1,0:T(8,128)(2,1)} %keys.1, bf16[16,1024]{1,0:T(8,128)(2,1)} %values.1), custom_call_target="tpu_custom_call" | custom-call | tf_op jit(solution)/shard_map/pallas_call | solution.py:223
  2.4 0.0 copy-start.7
  2.4 0.0 copy-start.8
  2.4 12.2 %all-to-all-start = ((bf16[64,2,16,128]{3,2,1,0:T(8,128)(2,1)}), bf16[64,2,16,128]{3,2,1,0:T(8,128)(2,1)S(1)}, u32[]{:S(2)}, u32[]{:S(2)}) async-start(bf16[64,2,16,128]{3,2,1,0:T(8,128)(2,1)} %shard_map.128), calls=%async_computation | async-start | bytes 1048576 | tf_op jit(solution)/shard_map/all_to_all | solution.py:257
  14.6 0.0 copy-start.9
  14.6 0.0 copy-start.10
  14.6 0.0 copy-start.11
  14.6 0.0 copy-done
  14.6 0.0 copy-done.7
  14.6 0.0 copy-done.8
  14.6 0.6 copy-done.9
  15.2 0.0 copy-done.10
  15.3 0.0 copy-done.11
  15.3 1.2 %copy-done.1 = bf16[512,1024]{1,0:T(8,128)(2,1)S(1)} copy-done((bf16[512,1024]{1,0:T(8,128)(2,1)S(1)}, bf16[512,1024]{1,0:T(8,128)(2,1)}, u32[]{:S(2)}) %copy-start.1) | copy-done | bytes 1048600
  16.5 2.7 %shard_map.129 = (bf16[8,2,256,128]{3,2,1,0:T(8,128)(2,1)S(1)}, bf16[8,2,256,128]{3,2,1,0:T(8,128)(2,1)S(1)}, bf16[8,2,32,128]{3,2,1,0:T(8,128)(2,1)S(1)}, bf16[...) custom-call(s32[1]{0:T(128)} %bitcast.1.own_y, s32[1,32]{1,0:T(1,128)S(1)} %copy-done.9, ...), custom_call_target="tpu_custom_call" | custom-call | flops 100000000 | bytes 1024 | tf_op jit(solution)/shard_map/pallas_call | solution.py:188
  19.2 0.0 copy-start.3
  19.2 1.0 copy-done.3
  20.2 1.0 %copy-done.5 = bf16[8,2,256,128]{3,2,1,0:T(8,128)(2,1)} copy-done((bf16[8,2,256,128]{3,2,1,0:T(8,128)(2,1)}, bf16[8,2,256,128]{3,2,1,0:T(8,128)(2,1)S(1)}, u32[]{:S(2)}) %copy-start.5) | copy-done | bytes 1048600
  21.2 11.0 %all-to-all-done = bf16[64,2,16,128]{3,2,1,0:T(8,128)(2,1)S(1)} async-done(((bf16[64,2,16,128]{3,2,1,0:T(8,128)(2,1)}), bf16[64,2,16,128]{3,2,1,0:T(8,128)(2,1)S(1)}, u32[]{:S(2)}, u32[]{:S(2)}) %all-to-all-start) | async-done | bytes 524320 | tf_op jit(solution)/shard_map/all_to_all | solution.py:257
  32.2 3.1 %collective-permute-start = (bf16[4,8,2,16,128]{4,3,2,1,0:T(8,128)(2,1)S(1)}, bf16[4,8,2,16,128]{4,3,2,1,0:T(8,128)(2,1)S(1)}, u32[]{:S(2)}, u32[]{:S(2)}) collective-permute-start(bf16[4,8,2,16,128]{4,3,2,1,0:T(8,128)(2,1)S(1)} %get-tuple-element.53), channel_id=1, source_target_pairs={{0,24},{8,0},{16,8},{24,16},{32,56},{40,32},{48,40},{56,48},{64,88... | collective-permute-start | bytes 786440 | tf_op jit(solution)/shard_map/ppermute | solution.py:273
  35.3 0.0 collective-permute-start.3
  35.3 3.2 %collective-permute-start.1 = (bf16[4,8,2,16,128]{4,3,2,1,0:T(8,128)(2,1)S(1)}, bf16[4,8,2,16,128]{4,3,2,1,0:T(8,128)(2,1)S(1)}, u32[]{:S(2)}, u32[]{:S(2)}) collective-permute-start(bf16[4,8,2,16,128]{4,3,2,1,0:T(8,128)(2,1)S(1)} %get-tuple-element.54), channel_id=1, source_target_pairs={{0,24},{8,0},{16,8},{24,16},{32,56},{40,32},{48,40},{56,48},{64,88... | collective-permute-start | bytes 786440 | tf_op jit(solution)/shard_map/ppermute | solution.py:279
  38.5 0.0 collective-permute-start.2
  38.5 3.4 %collective-permute-done.refs_0_ = bf16[4,8,2,16,128]{4,3,2,1,0:T(8,128)(2,1)S(1)} collective-permute-done((bf16[4,8,2,16,128]{4,3,2,1,0:T(8,128)(2,1)S(1)}, bf16[4,8,2,16,128]{4,3,2,1,0:T(8,128)(2,1)S(1)}, u32[]{:S(2)}, u32[]{:S(2)}) %collective-permute-start) | collective-permute-done | bytes 262176 | tf_op jit(solution)/shard_map/ppermute | solution.py:273
  42.0 3.7 %collective-permute-start.5 = (bf16[4,8,2,16,128]{4,3,2,1,0:T(8,128)(2,1)S(1)}, bf16[4,8,2,16,128]{4,3,2,1,0:T(8,128)(2,1)S(1)}, u32[]{:S(2)}, u32[]{:S(2)}) collective-permute-start(bf16[4,8,2,16,128]{4,3,2,1,0:T(8,128)(2,1)S(1)} %collective-permute-done.refs_0_), channel_id=1, source_target_pairs={{0,24},{8,0},{16,8},{24,16},{32,56},{40,32},{48,40},{56,48},{64,88... | collective-permute-start | bytes 786440 | tf_op jit(solution)/shard_map/ppermute | solution.py:276
  45.6 0.0 collective-permute-done.3.refs_1_
  45.7 0.0 collective-permute-start.6
  45.7 2.7 %shard_map.132 = (bf16[8,2,256,128]{3,2,1,0:T(8,128)(2,1)S(1)}, bf16[8,2,256,128]{3,2,1,0:T(8,128)(2,1)S(1)}, bf16[8,2,32,128]{3,2,1,0:T(8,128)(2,1)S(1)}, bf16[...) custom-call(s32[1]{0:T(128)} %bitcast.1.own_y, s32[1,32]{1,0:T(1,128)S(1)} %copy-done.9, ...), custom_call_target="tpu_custom_call" | custom-call | flops 100000000 | bytes 1024 | tf_op jit(solution)/shard_map/pallas_call | solution.py:188
  48.4 0.0 copy-start.4
  48.4 0.0 collective-permute-done.1.refs_1_
  48.4 2.9 %collective-permute-done.2.refs_0_ = bf16[4,8,2,16,128]{4,3,2,1,0:T(8,128)(2,1)S(1)} collective-permute-done((bf16[4,8,2,16,128]{4,3,2,1,0:T(8,128)(2,1)S(1)}, bf16[4,8,2,16,128]{4,3,2,1,0:T(8,128)(2,1)S(1)}, u32[]{:S(2)}, u32[]{:S(2)}) %collective-permute-start.2) | collective-permute-done | bytes 262176 | tf_op jit(solution)/shard_map/ppermute | solution.py:280
  51.3 2.5 %shard_map.134 = (bf16[8,128,256]{2,1,0:T(8,128)(2,1)S(1)}, bf16[8,2,32,128]{3,2,1,0:T(8,128)(2,1)S(1)}, bf16[8,128,256]{2,1,0:T(8,128)(2,1)S(1)}) custom-call(bf16[8,2,256,128]{3,2,1,0:T(8,128)(2,1)S(1)} %copy-done.6, bf16[8,2,32,128]{3,2,1,0:T(8,128)(2,1)S(1)} %get-tuple-element.63.near, f32[8,1,256]{2,1,0:T(1,128)S(1)} %get-tuple-element.64.bias, ...), custom_call_target="tpu_custom_call" | custom-call | flops 1000000 | bytes 1024 | tf_op jit(solution)/shard_map/pallas_call | solution.py:207
  53.8 0.5 collective-permute-start.8
  54.2 2.5 %shard_map.131 = (bf16[8,128,256]{2,1,0:T(8,128)(2,1)S(1)}, bf16[8,2,32,128]{3,2,1,0:T(8,128)(2,1)S(1)}, bf16[8,128,256]{2,1,0:T(8,128)(2,1)S(1)}) custom-call(bf16[8,2,256,128]{3,2,1,0:T(8,128)(2,1)S(1)} %copy-done.4, bf16[8,2,32,128]{3,2,1,0:T(8,128)(2,1)S(1)} %get-tuple-element.50.near, f32[8,1,256]{2,1,0:T(1,128)S(1)} %get-tuple-element.51.bias, ...), custom_call_target="tpu_custom_call" | custom-call | flops 1000000 | bytes 1024 | tf_op jit(solution)/shard_map/pallas_call | solution.py:207
  56.7 1.9 %collective-permute-start.4 = (bf16[8,128,256]{2,1,0:T(8,128)(2,1)S(1)}, bf16[8,128,256]{2,1,0:T(8,128)(2,1)S(1)}, u32[]{:S(2)}, u32[]{:S(2)}) collective-permute-start(bf16[8,128,256]{2,1,0:T(8,128)(2,1)S(1)} %get-tuple-element.57), channel_id=1, source_target_pairs={{0,8},{8,16},{16,24},{24,0},{32,40},{40,48},{48,56},{56,32},{64,72... | collective-permute-start | bytes 1572872 | tf_op jit(solution)/shard_map/ppermute | solution.py:293
  58.6 0.0 collective-permute-done.5.refs_0_
  58.6 0.0 collective-permute-done.6.refs_1_
  58.6 2.4 %shard_map.133 = (bf16[8,128,256]{2,1,0:T(8,128)(2,1)S(1)}, bf16[8,2,32,128]{3,2,1,0:T(8,128)(2,1)S(1)}, bf16[8,128,256]{2,1,0:T(8,128)(2,1)S(1)}) custom-call(bf16[8,2,256,128]{3,2,1,0:T(8,128)(2,1)S(1)} %get-tuple-element.58.wide, bf16[8,2,32,128]{3,2,1,0:T(8,128)(2,1)S(1)} %get-tuple-element.59.near, f32[8,1,256]{2,1,0:T(1,128)S(1)} %get-tuple-element.60.bias, ...), custom_call_target="tpu_custom_call" | custom-call | flops 1000000 | bytes 1024 | tf_op jit(solution)/shard_map/pallas_call | solution.py:207
  61.0 0.1 collective-permute-start.7
  61.1 2.4 %shard_map.135 = (bf16[8,128,256]{2,1,0:T(8,128)(2,1)S(1)}, bf16[8,2,32,128]{3,2,1,0:T(8,128)(2,1)S(1)}, bf16[8,128,256]{2,1,0:T(8,128)(2,1)S(1)}) custom-call(bf16[8,2,256,128]{3,2,1,0:T(8,128)(2,1)S(1)} %get-tuple-element.68.wide, bf16[8,2,32,128]{3,2,1,0:T(8,128)(2,1)S(1)} %get-tuple-element.69.near, f32[8,1,256]{2,1,0:T(1,128)S(1)} %get-tuple-element.70.bias, ...), custom_call_target="tpu_custom_call" | custom-call | flops 1000000 | bytes 1024 | tf_op jit(solution)/shard_map/pallas_call | solution.py:207
  63.6 6.4 %shard_map.136 = (bf16[512,1024]{1,0:T(8,128)(2,1)}, bf16[512,128]{1,0:T(8,128)(2,1)}, bf16[512,128]{1,0:T(8,128)(2,1)}) custom-call(s32[1]{0:T(128)} %bitcast.1.own_y, s32[1,32]{1,0:T(1,128)S(1)} %copy-done.9, s32[1,32]{1,0:T(1,128)S(1)} %copy-done.10, bf16[8,128,256]{2,1,0:T(8,128)(2,1)S(1)} %get-tuple-element.72.refs_0_, ...), custom_call_target="tpu_custom_call" | custom-call | flops 1000000 | bytes 1024 | tf_op jit(solution)/shard_map/pallas_call | solution.py:195
  70.0 0.0 collective-permute-done.8
  70.0 10.7 %collective-permute-done.4 = bf16[8,128,256]{2,1,0:T(8,128)(2,1)S(1)} collective-permute-done((bf16[8,128,256]{2,1,0:T(8,128)(2,1)S(1)}, bf16[8,128,256]{2,1,0:T(8,128)(2,1)S(1)}, u32[]{:S(2)}, u32[]{:S(2)}) %collective-permute-start.4) | collective-permute-done | bytes 524320 | tf_op jit(solution)/shard_map/ppermute | solution.py:293
  80.8 0.0 collective-permute-done.7
  80.8 0.3 add_convert_fusion
  81.1 16.8 %all_to_all.10 = bf16[8,128,256]{2,1,0:T(8,128)(2,1)S(1)} all-to-all(bf16[8,128,256]{2,1,0:T(8,128)(2,1)S(1)} %add_convert_fusion), channel_id=1, replica_groups={{0,32,64,96,128,160,192,224},{8,40,72,104,136,168,200,232},{16,48,80,11..., dimensions={0} | all-to-all | bytes 1048576 | tf_op jit(solution)/shard_map/all_to_all | solution.py:299
  97.8 0.1 reduce_sum.12
  97.9 0.6 fusion
  (9 shorter events, 0.0 us)
Async XLA Ops:
  0.6 14.0 %copy-start = (bf16[512,1024]{1,0:T(8,128)(2,1)S(1)}, bf16[512,1024]{1,0:T(8,128)(2,1)}, u32[]{:S(2)}) copy-start(bf16[512,1024]{1,0:T(8,128)(2,1)} %query.3) | copy-start | bytes 3145732
  2.4 12.2 %copy-start.7 = (bf16[512,128]{1,0:T(8,128)(2,1)S(1)}, bf16[512,128]{1,0:T(8,128)(2,1)}, u32[]{:S(2)}) copy-start(bf16[512,128]{1,0:T(8,128)(2,1)} %key.3) | copy-start | bytes 393220
  2.4 12.2 %copy-start.8 = (bf16[512,128]{1,0:T(8,128)(2,1)S(1)}, bf16[512,128]{1,0:T(8,128)(2,1)}, u32[]{:S(2)}) copy-start(bf16[512,128]{1,0:T(8,128)(2,1)} %value.3) | copy-start | bytes 393220
  2.4 29.7 %all-to-all-start = ((bf16[64,2,16,128]{3,2,1,0:T(8,128)(2,1)}), bf16[64,2,16,128]{3,2,1,0:T(8,128)(2,1)S(1)}, u32[]{:S(2)}, u32[]{:S(2)}) async-start(bf16[64,2,16,128]{3,2,1,0:T(8,128)(2,1)} %shard_map.128), calls=%async_computation | async-start | bytes 1048576 | tf_op jit(solution)/shard_map/all_to_all | solution.py:257
  14.6 0.7 copy-start.9
  14.6 0.7 copy-start.10
  14.6 0.7 copy-start.11
  15.3 1.2 %copy-start.1 = (bf16[512,1024]{1,0:T(8,128)(2,1)S(1)}, bf16[512,1024]{1,0:T(8,128)(2,1)}, u32[]{:S(2)}) copy-start(bf16[512,1024]{1,0:T(8,128)(2,1)} %cotangent.3) | copy-start | bytes 3145732
  16.5 29.2 %copy-start.2 = (bf16[512,1024]{1,0:T(8,128)(2,1)S(1)}, bf16[512,1024]{1,0:T(8,128)(2,1)}, u32[]{:S(2)}) copy-start(bf16[512,1024]{1,0:T(8,128)(2,1)} %cotangent.3) | copy-start | bytes 3145732
  19.2 1.0 copy-start.3
  20.2 1.0 %copy-start.5 = (bf16[8,2,256,128]{3,2,1,0:T(8,128)(2,1)}, bf16[8,2,256,128]{3,2,1,0:T(8,128)(2,1)S(1)}, u32[]{:S(2)}) copy-start(bf16[8,2,256,128]{3,2,1,0:T(8,128)(2,1)S(1)} %get-tuple-element.62.wide) | copy-start | bytes 3145732
  32.2 9.8 %collective-permute-start = (bf16[4,8,2,16,128]{4,3,2,1,0:T(8,128)(2,1)S(1)}, bf16[4,8,2,16,128]{4,3,2,1,0:T(8,128)(2,1)S(1)}, u32[]{:S(2)}, u32[]{:S(2)}) collective-permute-start(bf16[4,8,2,16,128]{4,3,2,1,0:T(8,128)(2,1)S(1)} %get-tuple-element.53), channel_id=1, source_target_pairs={{0,24},{8,0},{16,8},{24,16},{32,56},{40,32},{48,40},{56,48},{64,88... | collective-permute-start | bytes 786440 | tf_op jit(solution)/shard_map/ppermute | solution.py:273
  35.3 16.0 %copy-start.6 = (bf16[8,2,256,128]{3,2,1,0:T(8,128)(2,1)S(1)}, bf16[8,2,256,128]{3,2,1,0:T(8,128)(2,1)}, u32[]{:S(2)}) copy-start(bf16[8,2,256,128]{3,2,1,0:T(8,128)(2,1)} %copy-done.5) | copy-start | bytes 3145732
  35.3 10.4 %collective-permute-start.3 = (bf16[4,8,2,16,128]{4,3,2,1,0:T(8,128)(2,1)S(1)}, bf16[4,8,2,16,128]{4,3,2,1,0:T(8,128)(2,1)S(1)}, u32[]{:S(2)}, u32[]{:S(2)}) collective-permute-start(bf16[4,8,2,16,128]{4,3,2,1,0:T(8,128)(2,1)S(1)} %get-tuple-element.54), channel_id=1, source_target_pairs={{0,8},{8,16},{16,24},{24,0},{32,40},{40,48},{48,56},{56,32},{64,72... | collective-permute-start | bytes 786440 | tf_op jit(solution)/shard_map/ppermute | solution.py:274
  35.3 13.1 %collective-permute-start.1 = (bf16[4,8,2,16,128]{4,3,2,1,0:T(8,128)(2,1)S(1)}, bf16[4,8,2,16,128]{4,3,2,1,0:T(8,128)(2,1)S(1)}, u32[]{:S(2)}, u32[]{:S(2)}) collective-permute-start(bf16[4,8,2,16,128]{4,3,2,1,0:T(8,128)(2,1)S(1)} %get-tuple-element.54), channel_id=1, source_target_pairs={{0,24},{8,0},{16,8},{24,16},{32,56},{40,32},{48,40},{56,48},{64,88... | collective-permute-start | bytes 786440 | tf_op jit(solution)/shard_map/ppermute | solution.py:279
  38.5 12.8 %collective-permute-start.2 = (bf16[4,8,2,16,128]{4,3,2,1,0:T(8,128)(2,1)S(1)}, bf16[4,8,2,16,128]{4,3,2,1,0:T(8,128)(2,1)S(1)}, u32[]{:S(2)}, u32[]{:S(2)}) collective-permute-start(bf16[4,8,2,16,128]{4,3,2,1,0:T(8,128)(2,1)S(1)} %get-tuple-element.53), channel_id=1, source_target_pairs={{0,8},{8,16},{16,24},{24,0},{32,40},{40,48},{48,56},{56,32},{64,72... | collective-permute-start | bytes 786440 | tf_op jit(solution)/shard_map/ppermute | solution.py:280
  42.0 16.6 %collective-permute-start.5 = (bf16[4,8,2,16,128]{4,3,2,1,0:T(8,128)(2,1)S(1)}, bf16[4,8,2,16,128]{4,3,2,1,0:T(8,128)(2,1)S(1)}, u32[]{:S(2)}, u32[]{:S(2)}) collective-permute-start(bf16[4,8,2,16,128]{4,3,2,1,0:T(8,128)(2,1)S(1)} %collective-permute-done.refs_0_), channel_id=1, source_target_pairs={{0,24},{8,0},{16,8},{24,16},{32,56},{40,32},{48,40},{56,48},{64,88... | collective-permute-start | bytes 786440 | tf_op jit(solution)/shard_map/ppermute | solution.py:276
  45.7 12.9 %collective-permute-start.6 = (bf16[4,8,2,16,128]{4,3,2,1,0:T(8,128)(2,1)S(1)}, bf16[4,8,2,16,128]{4,3,2,1,0:T(8,128)(2,1)S(1)}, u32[]{:S(2)}, u32[]{:S(2)}) collective-permute-start(bf16[4,8,2,16,128]{4,3,2,1,0:T(8,128)(2,1)S(1)} %collective-permute-done.3.refs_1_), channel_id=1, source_target_pairs={{0,8},{8,16},{16,24},{24,0},{32,40},{40,48},{48,56},{56,32},{64,72... | collective-permute-start | bytes 786440 | tf_op jit(solution)/shard_map/ppermute | solution.py:277
  48.4 5.8 %copy-start.4 = (bf16[8,2,256,128]{3,2,1,0:T(8,128)(2,1)S(1)}, bf16[8,2,256,128]{3,2,1,0:T(8,128)(2,1)}, u32[]{:S(2)}) copy-start(bf16[8,2,256,128]{3,2,1,0:T(8,128)(2,1)} %copy-done.3) | copy-start | bytes 3145732
  53.8 16.3 %collective-permute-start.8 = (bf16[8,128,256]{2,1,0:T(8,128)(2,1)S(1)}, bf16[8,128,256]{2,1,0:T(8,128)(2,1)S(1)}, u32[]{:S(2)}, u32[]{:S(2)}) collective-permute-start(bf16[8,128,256]{2,1,0:T(8,128)(2,1)S(1)} %get-tuple-element.67), channel_id=1, source_target_pairs={{0,24},{8,0},{16,8},{24,16},{32,56},{40,32},{48,40},{56,48},{64,88... | collective-permute-start | bytes 1572872 | tf_op jit(solution)/shard_map/ppermute | solution.py:293
  56.7 24.1 %collective-permute-start.4 = (bf16[8,128,256]{2,1,0:T(8,128)(2,1)S(1)}, bf16[8,128,256]{2,1,0:T(8,128)(2,1)S(1)}, u32[]{:S(2)}, u32[]{:S(2)}) collective-permute-start(bf16[8,128,256]{2,1,0:T(8,128)(2,1)S(1)} %get-tuple-element.57), channel_id=1, source_target_pairs={{0,8},{8,16},{16,24},{24,0},{32,40},{40,48},{48,56},{56,32},{64,72... | collective-permute-start | bytes 1572872 | tf_op jit(solution)/shard_map/ppermute | solution.py:293
  61.0 19.7 %collective-permute-start.7 = (bf16[8,128,256]{2,1,0:T(8,128)(2,1)S(1)}, bf16[8,128,256]{2,1,0:T(8,128)(2,1)S(1)}, u32[]{:S(2)}, u32[]{:S(2)}) collective-permute-start(bf16[8,128,256]{2,1,0:T(8,128)(2,1)S(1)} %get-tuple-element.61), channel_id=1, source_target_pairs={{0,16},{8,24},{16,0},{24,8},{32,48},{40,56},{48,32},{56,40},{64,80... | collective-permute-start | bytes 1572872 | tf_op jit(solution)/shard_map/ppermute | solution.py:293

commit v7 on v6

--- a/solution.py
+++ b/solution.py
@@ -59,9 +59,9 @@
     locate(lengths, owners, masks, first_of, count_of, mask_of)
     rows = query.shape[0]
     for turn, wide_ref, near_ref, bias_ref in zip(turns, wide, near, bias):
-        y = lax.rem(own_y[0] + turn, NY)
 
         def one(z, carry):
+            y = lax.rem(own_y[0] + jnp.where(z < NZ // 2, turn[0], turn[1]), NY)
             prompt = z * NY + y
             start = first_of[prompt]
             window, offset = window_of(start, rows)
@@ -91,9 +91,9 @@
     dk[...] = jnp.zeros_like(dk)
     dv[...] = jnp.zeros_like(dv)
     for turn, wide_ref, near_ref in zip(turns, wide, near):
-        y = lax.rem(own_y[0] + turn, NY)
 
         def one(i, carry):
+            y = lax.rem(own_y[0] + jnp.where(i < NZ // 2, turn[0], turn[1]), NY)
             prompt = i * NY + y
             window, offset = window_of(first_of[prompt], rows)
             put = one_hot((WINDOW, SPAN), 1, offset, count_of[prompt])
@@ -109,9 +109,13 @@
         lax.fori_loop(0, NZ, one, 0, unroll=2)
 
 
-def attend(n_parts, wide, near, bias, *refs):
-    parts = refs[:n_parts]
-    dq, dnear, dprompt = refs[n_parts:]
+def attend(n_parts, n_early, n_out, wide, near, bias, *refs):
+    parts, early = refs[:n_parts], refs[n_parts : n_parts + n_early]
+    dq, dnear, *dprompts = refs[n_parts + n_early :]
+    half = NZ // 2
+    if n_early:
+        dprompts[0][:half] = early[0][...]
+        dprompts[1][half:] = early[1][...]
     key_at = lax.broadcasted_iota(jnp.int32, (SPAN, GROUP * SPAN), 0)
     token_at = lax.broadcasted_iota(jnp.int32, (SPAN, GROUP * SPAN), 1) % SPAN
     near_bias = jnp.where(key_at <= token_at, 0.0, far_below)
@@ -140,8 +144,13 @@
         k_grad = (dot(slopes, q) * scale).astype(jnp.bfloat16)
         v_grad = dot(probs, g).astype(jnp.bfloat16)
         dq[z] = (dot(k, slopes, ((0,), (0,))) * scale).astype(jnp.bfloat16)
-        dprompt[z, :, :HEAD_DIMENSION] = k_grad[:PROMPT]
-        dprompt[z, :, HEAD_DIMENSION:] = v_grad[:PROMPT]
+        if n_early:
+            dprompt, j = dprompts[1 if z < half else 0], z
+        else:
+            dprompt = dprompts[z * n_out // NZ]
+            j = z % dprompt.shape[0]
+        dprompt[j, :, :HEAD_DIMENSION] = k_grad[:PROMPT]
+        dprompt[j, :, HEAD_DIMENSION:] = v_grad[:PROMPT]
         dnear[z, 0] = k_grad[PROMPT:]
         dnear[z, 1] = v_grad[PROMPT:]
 
@@ -197,14 +206,14 @@
     )
 
 
-def attend_call(packed, parts):
-    outs = [
-        shaped(NZ, HEAD_DIMENSION, GROUP * SPAN),
-        shaped(NZ, 2, SPAN, HEAD_DIMENSION),
-        shaped(NZ, PROMPT, 2 * HEAD_DIMENSION),
-    ]
-    body = functools.partial(attend, len(parts))
-    return call(body, outs, 0, 3 + len(parts), 0, 10**6, 2**10)(*packed, *parts)
+def attend_call(packed, parts, n_out=1, early=()):
+    whole = NZ if early else NZ // n_out
+    outs = [shaped(NZ, HEAD_DIMENSION, GROUP * SPAN), shaped(NZ, 2, SPAN, HEAD_DIMENSION)]
+    outs += [shaped(whole, PROMPT, 2 * HEAD_DIMENSION)] * n_out
+    body = functools.partial(attend, len(parts), len(early), n_out)
+    return call(body, outs, 0, 3 + len(parts) + len(early), 0, 10**6, 2**10)(
+        *packed, *parts, *early
+    )
 
 
 def split_call(column):
@@ -262,38 +271,34 @@
         axis_index_groups=same_y_head,
         tiled=True,
     ).reshape(NZ, HEADS, 2, part, HEAD_DIMENSION)
+    turns = ((1, 3), (3, 1), (2, 2), (0, 0))
     own_y = lax.rem(lax.axis_index("dp"), NY).reshape(1).astype(jnp.int32)
     masks = block_mask.reshape(block_mask.shape[:2])
     scalars = (own_y, resp_len, resp_owner, masks)
     rows_of = (queries, output_cotangent, response_keys, response_values)
-    next_one, last_one = pack_call((1, 3), *scalars, *rows_of)
-    far, own = pack_call((2, 0), *scalars, *rows_of)
-    column, next_one = lax.optimization_barrier((column, next_one))
+    first, second = pack_call(turns[:2], *scalars, *rows_of)
+    far, own = pack_call(turns[2:], *scalars, *rows_of)
+    column, first = lax.optimization_barrier((column, first))
     low, high = split_call(column)
     after_low = lax.ppermute(low, "dp", along_y(-1))
     before_high = lax.ppermute(high, "dp", along_y(1))
+    after_high = lax.ppermute(high, "dp", along_y(-1))
+    before_low = lax.ppermute(low, "dp", along_y(1))
+    after_low, before_high, far = lax.optimization_barrier((after_low, before_high, far))
     across = [
         lax.ppermute(after_low, "dp", along_y(-1)),
         lax.ppermute(before_high, "dp", along_y(1)),
     ]
-    after = [after_low, lax.ppermute(high, "dp", along_y(-1))]
-    before = [lax.ppermute(low, "dp", along_y(1)), before_high]
-    after, before = lax.optimization_barrier((after, before))
-    dq, dnear, sums = [], [], []
-    order = (1, 2, 3, 0)
-    for turn, packed, prompts in (
-        (1, next_one, after),
-        (2, far, across),
-        (3, last_one, before),
-        (0, own, [column]),
-    ):
-        q_part, near_part, prompt_part = attend_call(packed, prompts)
-        dq.append(q_part)
-        dnear.append(near_part)
-        sums.append(lax.ppermute(prompt_part, "dp", along_y(turn)) if turn else prompt_part)
-    dq, dk, dv = unpack_call(
-        order, own_y, resp_len, resp_owner, dq, dnear, queries.shape[0]
-    )
+    made = [attend_call(first, [after_low, before_high], 2)]
+    made.append(attend_call(second, [before_low, after_high], 2, made[0][2:]))
+    made.append(attend_call(far, across))
+    made.append(attend_call(own, [column]))
+    dq = [a[0] for a in made]
+    dnear = [a[1] for a in made]
+    sums = [made[3][2]]
+    for turn, part in zip((1, 3, 2), (*made[1][2:], made[2][2])):
+        sums.append(lax.ppermute(part, "dp", along_y(turn)))
+    dq, dk, dv = unpack_call(turns, own_y, resp_len, resp_owner, dq, dnear, queries.shape[0])
     summed = sum(a.astype(jnp.float32) for a in sums).astype(jnp.bfloat16)
     summed, dq, dk, dv = lax.optimization_barrier((summed, dq, dk, dv))
     shares = lax.all_to_all(

time: 99.1 us -> 97 us (0.979)
  waiting for transfers between devices: 28.1 us -> 26.1 us
    ppermute x1, waiting for transfers between devices: 0.04 us -> 3.73 us  [per_device(): before_high = lax.ppermute(high, 'dp', along_y(1))]
    ppermute x1, starting transfers between devices: 3.69 us -> 0.01 us  [per_device(): lax.ppermute(after_low, 'dp', along_y(-1))]
    ppermute x5, waiting for transfers between devices: 13.6 us -> 10.8 us  [the longest x3 9.62 us: per_device(): sums.append(lax.ppermute(part, 'dp', along_y(turn)))]
    ppermute x1, waiting for transfers between devices: 3.45 us -> 0.67 us  [per_device(): after_low = lax.ppermute(low, 'dp', along_y(-1))]
    ppermute x1, starting transfers between devices: 0.01 us -> 2.02 us  [per_device(): lax.ppermute(before_high, 'dp', along_y(1))]
  transfers between devices with their start and end apart: 10 -> 10, of which waited for: 4 -> 5; matrix products, arithmetic and copies ran while one was open for 0% -> 0% of each run, Pallas kernels for 22% -> 23%
where the time goes in v7:
time: 97 us; the launch traced here: 96.2 us
  waiting for transfers between devices  26.1 us (27%)
  starting transfers between devices  23.9 us (25%)
  Pallas kernels  23.5 us (24%)
  blocking collectives  17.1 us (18%)
  local copies, waits for them, and re-layouts  4.47 us (5%)
    all_to_all x1, blocking collectives, per_device(): lax.all_to_all(summed, 'dp', split_axis=0, concat_axis=0, axis_index_grou...  17.1 us
    all_to_all x1, starting transfers between devices, per_device(): lax.all_to_all(spread_call(prompt_key_rows, prompt_value_rows), ('dp', 'h...  12.2 us
    all_to_all x1, waiting for transfers between devices, per_device(): lax.all_to_all(spread_call(prompt_key_rows, prompt_value_rows), ('dp', 'h...  10.9 us
    pallas_call x4, Pallas kernels, attend_call(): call(body, outs, 0, 3 + len(parts) + len(early), 0, 10 ** 6, 2 ** 10)  9.78 us
    ppermute x3, waiting for transfers between devices, per_device(): sums.append(lax.ppermute(part, 'dp', along_y(turn)))  9.62 us
    pallas_call x1, Pallas kernels, unpack_call(): call(body, outs, 3, 2 * len(turns), 2, 10 ** 6, 2 ** 10)  6.43 us
    pallas_call x2, Pallas kernels, pack_call(): call(functools.partial(pack, turns), outs, 4, 4, 3, 10 ** 8, 2 ** 10)(*args)  5.47 us
    unnamed x24, local copies, waits for them, and re-layouts  3.84 us
  transfers between devices with their start and end apart: 10, of which 5 were waited for; matrix products, arithmetic and copies ran while one was open for 0% of the time, Pallas kernels for 23%

profile of v7, /device:TPU:2, one launch (start us, length us, event | category | flops | bytes accessed | tf_op | source)
XLA Modules:
  0.0 96.2 jit_solution(13456125676989761484)
XLA Ops:
  0.6 0.0 copy-start
  0.6 1.7 %shard_map.129 = bf16[64,2,16,128]{3,2,1,0:T(8,128)(2,1)} custom-call(bf16[16,1024]{1,0:T(8,128)(2,1)} %keys.1, bf16[16,1024]{1,0:T(8,128)(2,1)} %values.1), custom_call_target="tpu_custom_call" | custom-call | tf_op jit(solution)/shard_map/pallas_call | solution.py:232
  2.4 0.0 copy-start.7
  2.4 0.0 copy-start.8
  2.4 12.2 %all-to-all-start = ((bf16[64,2,16,128]{3,2,1,0:T(8,128)(2,1)}), bf16[64,2,16,128]{3,2,1,0:T(8,128)(2,1)S(1)}, u32[]{:S(2)}, u32[]{:S(2)}) async-start(bf16[64,2,16,128]{3,2,1,0:T(8,128)(2,1)} %shard_map.129), calls=%async_computation | async-start | bytes 1048576 | tf_op jit(solution)/shard_map/all_to_all | solution.py:266
  14.6 0.0 copy-start.9
  14.6 0.0 copy-start.10
  14.6 0.0 copy-start.11
  14.6 0.0 copy-done
  14.6 0.0 copy-done.7
  14.6 0.6 copy-done.9
  15.2 0.0 copy-done.10
  15.3 0.0 copy-done.11
  15.3 1.2 %copy-done.1 = bf16[512,1024]{1,0:T(8,128)(2,1)S(1)} copy-done((bf16[512,1024]{1,0:T(8,128)(2,1)S(1)}, bf16[512,1024]{1,0:T(8,128)(2,1)}, u32[]{:S(2)}) %copy-start.1) | copy-done | bytes 1048600
  16.5 2.7 %shard_map.130 = (bf16[8,2,256,128]{3,2,1,0:T(8,128)(2,1)S(1)}, bf16[8,2,256,128]{3,2,1,0:T(8,128)(2,1)S(1)}, bf16[8,2,32,128]{3,2,1,0:T(8,128)(2,1)S(1)}, bf16[...) custom-call(s32[1]{0:T(128)} %bitcast.own_y, s32[1,32]{1,0:T(1,128)S(1)} %copy-done.9, ...), custom_call_target="tpu_custom_call" | custom-call | flops 100000000 | bytes 1024 | tf_op jit(solution)/shard_map/pallas_call | solution.py:197
  19.3 1.0 %copy-done.3 = bf16[8,2,256,128]{3,2,1,0:T(8,128)(2,1)} copy-done((bf16[8,2,256,128]{3,2,1,0:T(8,128)(2,1)}, bf16[8,2,256,128]{3,2,1,0:T(8,128)(2,1)S(1)}, u32[]{:S(2)}) %copy-start.3) | copy-done | bytes 1048600
  20.2 1.0 %copy-done.5 = bf16[8,2,256,128]{3,2,1,0:T(8,128)(2,1)} copy-done((bf16[8,2,256,128]{3,2,1,0:T(8,128)(2,1)}, bf16[8,2,256,128]{3,2,1,0:T(8,128)(2,1)S(1)}, u32[]{:S(2)}) %copy-start.5) | copy-done | bytes 1048600
  21.2 10.9 %all-to-all-done = bf16[64,2,16,128]{3,2,1,0:T(8,128)(2,1)S(1)} async-done(((bf16[64,2,16,128]{3,2,1,0:T(8,128)(2,1)}), bf16[64,2,16,128]{3,2,1,0:T(8,128)(2,1)S(1)}, u32[]{:S(2)}, u32[]{:S(2)}) %all-to-all-start) | async-done | bytes 524320 | tf_op jit(solution)/shard_map/all_to_all | solution.py:266
  32.2 3.1 %collective-permute-start.2 = (bf16[4,8,2,16,128]{4,3,2,1,0:T(8,128)(2,1)S(1)}, bf16[4,8,2,16,128]{4,3,2,1,0:T(8,128)(2,1)S(1)}, u32[]{:S(2)}, u32[]{:S(2)}) collective-permute-start(bf16[4,8,2,16,128]{4,3,2,1,0:T(8,128)(2,1)S(1)} %get-tuple-element.60), channel_id=1, source_target_pairs={{0,24},{8,0},{16,8},{24,16},{32,56},{40,32},{48,40},{56,48},{64,88... | collective-permute-start | bytes 786440 | tf_op jit(solution)/shard_map/ppermute | solution.py:283
  35.3 0.0 collective-permute-start.3
  35.3 0.6 collective-permute-start
  35.9 2.7 %collective-permute-start.1 = (bf16[4,8,2,16,128]{4,3,2,1,0:T(8,128)(2,1)S(1)}, bf16[4,8,2,16,128]{4,3,2,1,0:T(8,128)(2,1)S(1)}, u32[]{:S(2)}, u32[]{:S(2)}) collective-permute-start(bf16[4,8,2,16,128]{4,3,2,1,0:T(8,128)(2,1)S(1)} %get-tuple-element.61), channel_id=1, source_target_pairs={{0,24},{8,0},{16,8},{24,16},{32,56},{40,32},{48,40},{56,48},{64,88... | collective-permute-start | bytes 786440 | tf_op jit(solution)/shard_map/ppermute | solution.py:285
  38.5 0.0 copy-done.2
  38.5 2.7 %shard_map.128 = (bf16[8,2,256,128]{3,2,1,0:T(8,128)(2,1)S(1)}, bf16[8,2,256,128]{3,2,1,0:T(8,128)(2,1)S(1)}, bf16[8,2,32,128]{3,2,1,0:T(8,128)(2,1)S(1)}, bf16[...) custom-call(s32[1]{0:T(128)} %bitcast.own_y, s32[1,32]{1,0:T(1,128)S(1)} %copy-done.9, ...), custom_call_target="tpu_custom_call" | custom-call | flops 100000000 | bytes 1024 | tf_op jit(solution)/shard_map/pallas_call | solution.py:197
  41.3 0.7 collective-permute-done.2.refs_0_
  42.0 3.7 %collective-permute-done.3.refs_1_ = bf16[4,8,2,16,128]{4,3,2,1,0:T(8,128)(2,1)S(1)} collective-permute-done((bf16[4,8,2,16,128]{4,3,2,1,0:T(8,128)(2,1)S(1)}, bf16[4,8,2,16,128]{4,3,2,1,0:T(8,128)(2,1)S(1)}, u32[]{:S(2)}, u32[]{:S(2)}) %collective-permute-start.3) | collective-permute-done | bytes 262176 | tf_op jit(solution)/shard_map/ppermute | solution.py:284
  45.7 0.0 collective-permute-start.6
  45.7 2.0 %collective-permute-start.7 = (bf16[4,8,2,16,128]{4,3,2,1,0:T(8,128)(2,1)S(1)}, bf16[4,8,2,16,128]{4,3,2,1,0:T(8,128)(2,1)S(1)}, u32[]{:S(2)}, u32[]{:S(2)}) collective-permute-start(bf16[4,8,2,16,128]{4,3,2,1,0:T(8,128)(2,1)S(1)} %collective-permute-done.3.refs_1_), channel_id=1, source_target_pairs={{0,8},{8,16},{16,24},{24,0},{32,40},{40,48},{48,56},{56,32},{64,72... | collective-permute-start | bytes 786440 | tf_op jit(solution)/shard_map/ppermute | solution.py:290
  47.7 2.4 %shard_map.133 = (bf16[8,128,256]{2,1,0:T(8,128)(2,1)S(1)}, bf16[8,2,32,128]{3,2,1,0:T(8,128)(2,1)S(1)}, bf16[4,128,256]{2,1,0:T(8,128)(2,1)S(1)}, bf16[4,128,256]{2,1,0:T(8,128)(2,1)S(1)}) custom-call(bf16[8,2,256,128]{3,2,1,0:T(8,128)(2,1)S(1)} %copy-done.6, bf16[8,2,32,128]{3,2,1,0:T(8,128)(2,1)S(1)} %get-tuple-element.63.near, ...), custom_call_target="tpu_custom_call" | custom-call | flops 1000000 | bytes 1024 | tf_op jit(solution)/shard_map/pallas_call | solution.py:214
  50.2 1.1 %collective-permute-done.refs_0_ = bf16[4,8,2,16,128]{4,3,2,1,0:T(8,128)(2,1)S(1)} collective-permute-done((bf16[4,8,2,16,128]{4,3,2,1,0:T(8,128)(2,1)S(1)}, bf16[4,8,2,16,128]{4,3,2,1,0:T(8,128)(2,1)S(1)}, u32[]{:S(2)}, u32[]{:S(2)}) %collective-permute-start) | collective-permute-done | bytes 262176 | tf_op jit(solution)/shard_map/ppermute | solution.py:286
  51.3 0.0 collective-permute-done.1.refs_1_
  51.3 0.0 copy-done.4
  51.3 2.4 %shard_map.134 = (bf16[8,128,256]{2,1,0:T(8,128)(2,1)S(1)}, bf16[8,2,32,128]{3,2,1,0:T(8,128)(2,1)S(1)}, bf16[8,128,256]{2,1,0:T(8,128)(2,1)S(1)}, bf16[8,128,256]{2,1,0:T(8,128)(2,1)S(1)}) custom-call(bf16[8,2,256,128]{3,2,1,0:T(8,128)(2,1)S(1)} %copy-done.4, bf16[8,2,32,128]{3,2,1,0:T(8,128)(2,1)S(1)} %get-tuple-element.58.near, ...), custom_call_target="tpu_custom_call" | custom-call | flops 1000000 | bytes 1024 | tf_op jit(solution)/shard_map/pallas_call | solution.py:214
  53.8 0.1 collective-permute-start.4
  53.9 3.2 %collective-permute-start.5 = (bf16[8,128,256]{2,1,0:T(8,128)(2,1)S(1)}, bf16[8,128,256]{2,1,0:T(8,128)(2,1)S(1)}, u32[]{:S(2)}, u32[]{:S(2)}) collective-permute-start(bf16[8,128,256]{2,1,0:T(8,128)(2,1)S(1)} %get-tuple-element.73), channel_id=1, source_target_pairs={{0,24},{8,0},{16,8},{24,16},{32,56},{40,32},{48,40},{56,48},{64,88... | collective-permute-start | bytes 1572872 | tf_op jit(solution)/shard_map/ppermute | solution.py:300
  57.1 0.0 collective-permute-done.6.refs_0_
  57.1 0.0 collective-permute-done.7.refs_1_
  57.1 2.5 %shard_map.135 = (bf16[8,128,256]{2,1,0:T(8,128)(2,1)S(1)}, bf16[8,2,32,128]{3,2,1,0:T(8,128)(2,1)S(1)}, bf16[8,128,256]{2,1,0:T(8,128)(2,1)S(1)}) custom-call(bf16[8,2,256,128]{3,2,1,0:T(8,128)(2,1)S(1)} %get-tuple-element.74.wide, bf16[8,2,32,128]{3,2,1,0:T(8,128)(2,1)S(1)} %get-tuple-element.75.near, f32[8,1,256]{2,1,0:T(1,128)S(1)} %get-tuple-element.76.bias, ...), custom_call_target="tpu_custom_call" | custom-call | flops 1000000 | bytes 1024 | tf_op jit(solution)/shard_map/pallas_call | solution.py:214
  59.5 0.1 collective-permute-start.8
  59.6 2.4 %shard_map.131 = (bf16[8,128,256]{2,1,0:T(8,128)(2,1)S(1)}, bf16[8,2,32,128]{3,2,1,0:T(8,128)(2,1)S(1)}, bf16[8,128,256]{2,1,0:T(8,128)(2,1)S(1)}) custom-call(bf16[8,2,256,128]{3,2,1,0:T(8,128)(2,1)S(1)} %get-tuple-element.49.wide, bf16[8,2,32,128]{3,2,1,0:T(8,128)(2,1)S(1)} %get-tuple-element.50.near, f32[8,1,256]{2,1,0:T(1,128)S(1)} %get-tuple-element.51.bias, ...), custom_call_target="tpu_custom_call" | custom-call | flops 1000000 | bytes 1024 | tf_op jit(solution)/shard_map/pallas_call | solution.py:214
  62.1 6.4 %shard_map.136 = (bf16[512,1024]{1,0:T(8,128)(2,1)}, bf16[512,128]{1,0:T(8,128)(2,1)}, bf16[512,128]{1,0:T(8,128)(2,1)}) custom-call(s32[1]{0:T(128)} %bitcast.own_y, s32[1,32]{1,0:T(1,128)S(1)} %copy-done.9, s32[1,32]{1,0:T(1,128)S(1)} %copy-done.10, bf16[8,128,256]{2,1,0:T(8,128)(2,1)S(1)} %get-tuple-element.78.refs_0_, ...), custom_call_target="tpu_custom_call" | custom-call | flops 1000000 | bytes 1024 | tf_op jit(solution)/shard_map/pallas_call | solution.py:204
  68.5 9.6 %collective-permute-done.4 = bf16[8,128,256]{2,1,0:T(8,128)(2,1)S(1)} collective-permute-done((bf16[8,128,256]{2,1,0:T(8,128)(2,1)S(1)}, bf16[8,128,256]{2,1,0:T(8,128)(2,1)S(1)}, u32[]{:S(2)}, u32[]{:S(2)}) %collective-permute-start.4) | collective-permute-done | bytes 524320 | tf_op jit(solution)/shard_map/ppermute | solution.py:300
  78.1 0.0 collective-permute-done.5
  78.1 0.0 collective-permute-done.8
  78.1 0.3 add_convert_fusion
  78.4 17.1 %all_to_all.10 = bf16[8,128,256]{2,1,0:T(8,128)(2,1)S(1)} all-to-all(bf16[8,128,256]{2,1,0:T(8,128)(2,1)S(1)} %add_convert_fusion), channel_id=1, replica_groups={{0,32,64,96,128,160,192,224},{8,40,72,104,136,168,200,232},{16,48,80,11..., dimensions={0} | all-to-all | bytes 1048576 | tf_op jit(solution)/shard_map/all_to_all | solution.py:304
  95.5 0.1 reduce_sum.12
  95.6 0.6 fusion
  (9 shorter events, 0.0 us)
Async XLA Ops:
  0.6 14.0 %copy-start = (bf16[512,1024]{1,0:T(8,128)(2,1)S(1)}, bf16[512,1024]{1,0:T(8,128)(2,1)}, u32[]{:S(2)}) copy-start(bf16[512,1024]{1,0:T(8,128)(2,1)} %query.3) | copy-start | bytes 3145732
  2.4 12.2 %copy-start.7 = (bf16[512,128]{1,0:T(8,128)(2,1)S(1)}, bf16[512,128]{1,0:T(8,128)(2,1)}, u32[]{:S(2)}) copy-start(bf16[512,128]{1,0:T(8,128)(2,1)} %key.3) | copy-start | bytes 393220
  2.4 12.2 %copy-start.8 = (bf16[512,128]{1,0:T(8,128)(2,1)S(1)}, bf16[512,128]{1,0:T(8,128)(2,1)}, u32[]{:S(2)}) copy-start(bf16[512,128]{1,0:T(8,128)(2,1)} %value.3) | copy-start | bytes 393220
  2.4 29.7 %all-to-all-start = ((bf16[64,2,16,128]{3,2,1,0:T(8,128)(2,1)}), bf16[64,2,16,128]{3,2,1,0:T(8,128)(2,1)S(1)}, u32[]{:S(2)}, u32[]{:S(2)}) async-start(bf16[64,2,16,128]{3,2,1,0:T(8,128)(2,1)} %shard_map.129), calls=%async_computation | async-start | bytes 1048576 | tf_op jit(solution)/shard_map/all_to_all | solution.py:266
  14.6 0.7 copy-start.9
  14.6 0.7 copy-start.10
  14.6 0.7 copy-start.11
  15.3 1.2 %copy-start.1 = (bf16[512,1024]{1,0:T(8,128)(2,1)S(1)}, bf16[512,1024]{1,0:T(8,128)(2,1)}, u32[]{:S(2)}) copy-start(bf16[512,1024]{1,0:T(8,128)(2,1)} %cotangent.3) | copy-start | bytes 3145732
  16.5 22.0 %copy-start.2 = (bf16[512,1024]{1,0:T(8,128)(2,1)S(1)}, bf16[512,1024]{1,0:T(8,128)(2,1)}, u32[]{:S(2)}) copy-start(bf16[512,1024]{1,0:T(8,128)(2,1)} %cotangent.3) | copy-start | bytes 3145732
  19.3 1.0 %copy-start.3 = (bf16[8,2,256,128]{3,2,1,0:T(8,128)(2,1)}, bf16[8,2,256,128]{3,2,1,0:T(8,128)(2,1)S(1)}, u32[]{:S(2)}) copy-start(bf16[8,2,256,128]{3,2,1,0:T(8,128)(2,1)S(1)} %get-tuple-element.57.wide) | copy-start | bytes 3145732
  20.2 1.0 %copy-start.5 = (bf16[8,2,256,128]{3,2,1,0:T(8,128)(2,1)}, bf16[8,2,256,128]{3,2,1,0:T(8,128)(2,1)S(1)}, u32[]{:S(2)}) copy-start(bf16[8,2,256,128]{3,2,1,0:T(8,128)(2,1)S(1)} %get-tuple-element.62.wide) | copy-start | bytes 3145732
  32.2 9.8 %collective-permute-start.2 = (bf16[4,8,2,16,128]{4,3,2,1,0:T(8,128)(2,1)S(1)}, bf16[4,8,2,16,128]{4,3,2,1,0:T(8,128)(2,1)S(1)}, u32[]{:S(2)}, u32[]{:S(2)}) collective-permute-start(bf16[4,8,2,16,128]{4,3,2,1,0:T(8,128)(2,1)S(1)} %get-tuple-element.60), channel_id=1, source_target_pairs={{0,24},{8,0},{16,8},{24,16},{32,56},{40,32},{48,40},{56,48},{64,88... | collective-permute-start | bytes 786440 | tf_op jit(solution)/shard_map/ppermute | solution.py:283
  35.3 12.4 %copy-start.6 = (bf16[8,2,256,128]{3,2,1,0:T(8,128)(2,1)S(1)}, bf16[8,2,256,128]{3,2,1,0:T(8,128)(2,1)}, u32[]{:S(2)}) copy-start(bf16[8,2,256,128]{3,2,1,0:T(8,128)(2,1)} %copy-done.5) | copy-start | bytes 3145732
  35.3 10.4 %collective-permute-start.3 = (bf16[4,8,2,16,128]{4,3,2,1,0:T(8,128)(2,1)S(1)}, bf16[4,8,2,16,128]{4,3,2,1,0:T(8,128)(2,1)S(1)}, u32[]{:S(2)}, u32[]{:S(2)}) collective-permute-start(bf16[4,8,2,16,128]{4,3,2,1,0:T(8,128)(2,1)S(1)} %get-tuple-element.61), channel_id=1, source_target_pairs={{0,8},{8,16},{16,24},{24,0},{32,40},{40,48},{48,56},{56,32},{64,72... | collective-permute-start | bytes 786440 | tf_op jit(solution)/shard_map/ppermute | solution.py:284
  35.3 16.0 %collective-permute-start = (bf16[4,8,2,16,128]{4,3,2,1,0:T(8,128)(2,1)S(1)}, bf16[4,8,2,16,128]{4,3,2,1,0:T(8,128)(2,1)S(1)}, u32[]{:S(2)}, u32[]{:S(2)}) collective-permute-start(bf16[4,8,2,16,128]{4,3,2,1,0:T(8,128)(2,1)S(1)} %get-tuple-element.60), channel_id=1, source_target_pairs={{0,8},{8,16},{16,24},{24,0},{32,40},{40,48},{48,56},{56,32},{64,72... | collective-permute-start | bytes 786440 | tf_op jit(solution)/shard_map/ppermute | solution.py:286
  35.9 15.4 %collective-permute-start.1 = (bf16[4,8,2,16,128]{4,3,2,1,0:T(8,128)(2,1)S(1)}, bf16[4,8,2,16,128]{4,3,2,1,0:T(8,128)(2,1)S(1)}, u32[]{:S(2)}, u32[]{:S(2)}) collective-permute-start(bf16[4,8,2,16,128]{4,3,2,1,0:T(8,128)(2,1)S(1)} %get-tuple-element.61), channel_id=1, source_target_pairs={{0,24},{8,0},{16,8},{24,16},{32,56},{40,32},{48,40},{56,48},{64,88... | collective-permute-start | bytes 786440 | tf_op jit(solution)/shard_map/ppermute | solution.py:285
  41.3 10.0 %copy-start.4 = (bf16[8,2,256,128]{3,2,1,0:T(8,128)(2,1)S(1)}, bf16[8,2,256,128]{3,2,1,0:T(8,128)(2,1)}, u32[]{:S(2)}) copy-start(bf16[8,2,256,128]{3,2,1,0:T(8,128)(2,1)} %copy-done.3) | copy-start | bytes 3145732
  45.7 11.4 %collective-permute-start.6 = (bf16[4,8,2,16,128]{4,3,2,1,0:T(8,128)(2,1)S(1)}, bf16[4,8,2,16,128]{4,3,2,1,0:T(8,128)(2,1)S(1)}, u32[]{:S(2)}, u32[]{:S(2)}) collective-permute-start(bf16[4,8,2,16,128]{4,3,2,1,0:T(8,128)(2,1)S(1)} %collective-permute-done.2.refs_0_), channel_id=1, source_target_pairs={{0,24},{8,0},{16,8},{24,16},{32,56},{40,32},{48,40},{56,48},{64,88... | collective-permute-start | bytes 786440 | tf_op jit(solution)/shard_map/ppermute | solution.py:289
  45.7 11.4 %collective-permute-start.7 = (bf16[4,8,2,16,128]{4,3,2,1,0:T(8,128)(2,1)S(1)}, bf16[4,8,2,16,128]{4,3,2,1,0:T(8,128)(2,1)S(1)}, u32[]{:S(2)}, u32[]{:S(2)}) collective-permute-start(bf16[4,8,2,16,128]{4,3,2,1,0:T(8,128)(2,1)S(1)} %collective-permute-done.3.refs_1_), channel_id=1, source_target_pairs={{0,8},{8,16},{16,24},{24,0},{32,40},{40,48},{48,56},{56,32},{64,72... | collective-permute-start | bytes 786440 | tf_op jit(solution)/shard_map/ppermute | solution.py:290
  53.8 24.4 %collective-permute-start.4 = (bf16[8,128,256]{2,1,0:T(8,128)(2,1)S(1)}, bf16[8,128,256]{2,1,0:T(8,128)(2,1)S(1)}, u32[]{:S(2)}, u32[]{:S(2)}) collective-permute-start(bf16[8,128,256]{2,1,0:T(8,128)(2,1)S(1)} %get-tuple-element.72), channel_id=1, source_target_pairs={{0,8},{8,16},{16,24},{24,0},{32,40},{40,48},{48,56},{56,32},{64,72... | collective-permute-start | bytes 1572872 | tf_op jit(solution)/shard_map/ppermute | solution.py:300
  53.9 24.3 %collective-permute-start.5 = (bf16[8,128,256]{2,1,0:T(8,128)(2,1)S(1)}, bf16[8,128,256]{2,1,0:T(8,128)(2,1)S(1)}, u32[]{:S(2)}, u32[]{:S(2)}) collective-permute-start(bf16[8,128,256]{2,1,0:T(8,128)(2,1)S(1)} %get-tuple-element.73), channel_id=1, source_target_pairs={{0,24},{8,0},{16,8},{24,16},{32,56},{40,32},{48,40},{56,48},{64,88... | collective-permute-start | bytes 1572872 | tf_op jit(solution)/shard_map/ppermute | solution.py:300
  59.5 18.6 %collective-permute-start.8 = (bf16[8,128,256]{2,1,0:T(8,128)(2,1)S(1)}, bf16[8,128,256]{2,1,0:T(8,128)(2,1)S(1)}, u32[]{:S(2)}, u32[]{:S(2)}) collective-permute-start(bf16[8,128,256]{2,1,0:T(8,128)(2,1)S(1)} %get-tuple-element.77), channel_id=1, source_target_pairs={{0,16},{8,24},{16,0},{24,8},{32,48},{40,56},{48,32},{56,40},{64,80... | collective-permute-start | bytes 1572872 | tf_op jit(solution)/shard_map/ppermute | solution.py:300

commit v8 on v6

--- a/solution.py
+++ b/solution.py
@@ -116,14 +116,15 @@
     token_at = lax.broadcasted_iota(jnp.int32, (SPAN, GROUP * SPAN), 1) % SPAN
     near_bias = jnp.where(key_at <= token_at, 0.0, far_below)
     per_part = NZ // n_parts
-    for z in range(NZ):
-        prompt = parts[z // per_part]
-        i = z % per_part
-        q, g = wide[z, 0], wide[z, 1]
-        k = jnp.concatenate([prompt[i, :, 0].reshape(PROMPT, HEAD_DIMENSION), near[z, 0]])
-        v = jnp.concatenate([prompt[i, :, 1].reshape(PROMPT, HEAD_DIMENSION), near[z, 1]])
-        scores = dot(k, q, ((1,), (1,)))
-        dots = dot(v, g, ((1,), (1,)))
+
+    def rows_of(z, j):
+        far = parts[z // per_part][z % per_part, :, j].reshape(PROMPT, HEAD_DIMENSION)
+        return jnp.concatenate([far, near[z, j]])
+
+    def products(z):
+        return [dot(rows_of(z, j), wide[z, j], ((1,), (1,))) for j in range(2)]
+
+    def soften(z, scores, dots):
         far, own = scores[:PROMPT], scores[PROMPT:] + near_bias
         hidden = bias[z]
         highest = jnp.maximum(
@@ -135,15 +136,26 @@
         inverse = 1.0 / jnp.sum(weights, axis=0, keepdims=True)
         delta = jnp.sum(weights * dots, axis=0, keepdims=True) * inverse
         probs = weights * inverse
-        slopes = (probs * (dots - delta)).astype(jnp.bfloat16)
-        probs = probs.astype(jnp.bfloat16)
-        k_grad = (dot(slopes, q) * scale).astype(jnp.bfloat16)
-        v_grad = dot(probs, g).astype(jnp.bfloat16)
-        dq[z] = (dot(k, slopes, ((0,), (0,))) * scale).astype(jnp.bfloat16)
+        return (probs * (dots - delta)).astype(jnp.bfloat16), probs.astype(jnp.bfloat16)
+
+    def gradients(z, slopes, probs):
+        k_grad = (dot(slopes, wide[z, 0]) * scale).astype(jnp.bfloat16)
+        v_grad = dot(probs, wide[z, 1]).astype(jnp.bfloat16)
+        dq[z] = (dot(rows_of(z, 0), slopes, ((0,), (0,))) * scale).astype(jnp.bfloat16)
         dprompt[z, :, :HEAD_DIMENSION] = k_grad[:PROMPT]
         dprompt[z, :, HEAD_DIMENSION:] = v_grad[:PROMPT]
         dnear[z, 0] = k_grad[PROMPT:]
         dnear[z, 1] = v_grad[PROMPT:]
+
+    ahead, behind = products(0), None
+    for z in range(NZ):
+        held = ahead
+        if z + 1 < NZ:
+            ahead = products(z + 1)
+        if behind is not None:
+            gradients(z - 1, *behind)
+        behind = soften(z, *held)
+    gradients(NZ - 1, *behind)
 
 
 def spread(keys, values, out, held, sems):
@@ -278,7 +290,7 @@
     ]
     after = [after_low, lax.ppermute(high, "dp", along_y(-1))]
     before = [lax.ppermute(low, "dp", along_y(1)), before_high]
-    after, before = lax.optimization_barrier((after, before))
+    after, before, far = lax.optimization_barrier((after, before, far))
     dq, dnear, sums = [], [], []
     order = (1, 2, 3, 0)
     for turn, packed, prompts in (

time: 99.1 us -> 96.9 us (0.978)
  Pallas kernels: 23.4 us -> 18.6 us
  waiting for transfers between devices: 28.1 us -> 30.3 us
    pallas_call x4, Pallas kernels: 9.79 us -> 5.07 us  [attend_call(): call(body, outs, 0, 3 + len(parts), 0, 10 ** 6, 2 ** 10)(*packed, *parts)]
    ppermute x3, waiting for transfers between devices: 10.7 us -> 12.9 us  [per_device(): lax.ppermute(prompt_part, 'dp', along_y(turn))]
  transfers between devices with their start and end apart: 10 -> 10, of which waited for: 4 -> 5; matrix products, arithmetic and copies ran while one was open for 0% -> 0% of each run, Pallas kernels for 22% -> 18%
where the time goes in v8:
time: 96.9 us; the launch traced here: 96 us
  waiting for transfers between devices  30.3 us (31%)
  starting transfers between devices  24.6 us (25%)
  Pallas kernels  18.6 us (19%)
  blocking collectives  16.8 us (17%)
  local copies, waits for them, and re-layouts  4.48 us (5%)
    all_to_all x1, blocking collectives, per_device(): lax.all_to_all(summed, 'dp', split_axis=0, concat_axis=0, axis_index_grou...  16.8 us
    ppermute x3, waiting for transfers between devices, per_device(): lax.ppermute(prompt_part, 'dp', along_y(turn))  12.9 us
    all_to_all x1, starting transfers between devices, per_device(): lax.all_to_all(spread_call(prompt_key_rows, prompt_value_rows), ('dp', 'h...  12.2 us
    all_to_all x1, waiting for transfers between devices, per_device(): lax.all_to_all(spread_call(prompt_key_rows, prompt_value_rows), ('dp', 'h...  11 us
    pallas_call x1, Pallas kernels, unpack_call(): call(body, outs, 3, 2 * len(turns), 2, 10 ** 6, 2 ** 10)  6.44 us
    pallas_call x2, Pallas kernels, pack_call(): call(functools.partial(pack, turns), outs, 4, 4, 3, 10 ** 8, 2 ** 10)(*args)  5.38 us
    pallas_call x4, Pallas kernels, attend_call(): call(body, outs, 0, 3 + len(parts), 0, 10 ** 6, 2 ** 10)(*packed, *parts)  5.07 us
    unnamed x24, local copies, waits for them, and re-layouts  3.84 us
  transfers between devices with their start and end apart: 10, of which 5 were waited for; matrix products, arithmetic and copies ran while one was open for 0% of the time, Pallas kernels for 18%

profile of v8, /device:TPU:2, one launch (start us, length us, event | category | flops | bytes accessed | tf_op | source)
XLA Modules:
  0.0 96.0 jit_solution(16650538516436025297)
XLA Ops:
  0.6 0.0 copy-start
  0.6 1.7 %shard_map.128 = bf16[64,2,16,128]{3,2,1,0:T(8,128)(2,1)} custom-call(bf16[16,1024]{1,0:T(8,128)(2,1)} %keys.1, bf16[16,1024]{1,0:T(8,128)(2,1)} %values.1), custom_call_target="tpu_custom_call" | custom-call | tf_op jit(solution)/shard_map/pallas_call | solution.py:235
  2.4 0.0 copy-start.7
  2.4 0.0 copy-start.8
  2.4 12.2 %all-to-all-start = ((bf16[64,2,16,128]{3,2,1,0:T(8,128)(2,1)}), bf16[64,2,16,128]{3,2,1,0:T(8,128)(2,1)S(1)}, u32[]{:S(2)}, u32[]{:S(2)}) async-start(bf16[64,2,16,128]{3,2,1,0:T(8,128)(2,1)} %shard_map.128), calls=%async_computation | async-start | bytes 1048576 | tf_op jit(solution)/shard_map/all_to_all | solution.py:269
  14.6 0.0 copy-start.9
  14.6 0.0 copy-start.10
  14.6 0.0 copy-start.11
  14.6 0.0 copy-done
  14.6 0.0 copy-done.7
  14.6 0.6 copy-done.9
  15.2 0.0 copy-done.10
  15.3 0.0 copy-done.11
  15.3 1.2 %copy-done.1 = bf16[512,1024]{1,0:T(8,128)(2,1)S(1)} copy-done((bf16[512,1024]{1,0:T(8,128)(2,1)S(1)}, bf16[512,1024]{1,0:T(8,128)(2,1)}, u32[]{:S(2)}) %copy-start.1) | copy-done | bytes 1048600
  16.5 2.7 %shard_map.129 = (bf16[8,2,256,128]{3,2,1,0:T(8,128)(2,1)S(1)}, bf16[8,2,256,128]{3,2,1,0:T(8,128)(2,1)S(1)}, bf16[8,2,32,128]{3,2,1,0:T(8,128)(2,1)S(1)}, bf16[...) custom-call(s32[1]{0:T(128)} %bitcast.1.own_y, s32[1,32]{1,0:T(1,128)S(1)} %copy-done.9, ...), custom_call_target="tpu_custom_call" | custom-call | flops 100000000 | bytes 1024 | tf_op jit(solution)/shard_map/pallas_call | solution.py:200
  19.2 0.0 copy-start.3
  19.2 1.0 %copy-done.3 = bf16[8,2,256,128]{3,2,1,0:T(8,128)(2,1)} copy-done((bf16[8,2,256,128]{3,2,1,0:T(8,128)(2,1)}, bf16[8,2,256,128]{3,2,1,0:T(8,128)(2,1)S(1)}, u32[]{:S(2)}) %copy-start.3) | copy-done | bytes 1048600
  20.2 1.0 %copy-done.5 = bf16[8,2,256,128]{3,2,1,0:T(8,128)(2,1)} copy-done((bf16[8,2,256,128]{3,2,1,0:T(8,128)(2,1)}, bf16[8,2,256,128]{3,2,1,0:T(8,128)(2,1)S(1)}, u32[]{:S(2)}) %copy-start.5) | copy-done | bytes 1048600
  21.2 11.0 %all-to-all-done = bf16[64,2,16,128]{3,2,1,0:T(8,128)(2,1)S(1)} async-done(((bf16[64,2,16,128]{3,2,1,0:T(8,128)(2,1)}), bf16[64,2,16,128]{3,2,1,0:T(8,128)(2,1)S(1)}, u32[]{:S(2)}, u32[]{:S(2)}) %all-to-all-start) | async-done | bytes 524320 | tf_op jit(solution)/shard_map/all_to_all | solution.py:269
  32.2 3.1 %collective-permute-start = (bf16[4,8,2,16,128]{4,3,2,1,0:T(8,128)(2,1)S(1)}, bf16[4,8,2,16,128]{4,3,2,1,0:T(8,128)(2,1)S(1)}, u32[]{:S(2)}, u32[]{:S(2)}) collective-permute-start(bf16[4,8,2,16,128]{4,3,2,1,0:T(8,128)(2,1)S(1)} %get-tuple-element.56), channel_id=1, source_target_pairs={{0,24},{8,0},{16,8},{24,16},{32,56},{40,32},{48,40},{56,48},{64,88... | collective-permute-start | bytes 786440 | tf_op jit(solution)/shard_map/ppermute | solution.py:285
  35.3 0.0 collective-permute-start.3
  35.3 3.2 %collective-permute-start.1 = (bf16[4,8,2,16,128]{4,3,2,1,0:T(8,128)(2,1)S(1)}, bf16[4,8,2,16,128]{4,3,2,1,0:T(8,128)(2,1)S(1)}, u32[]{:S(2)}, u32[]{:S(2)}) collective-permute-start(bf16[4,8,2,16,128]{4,3,2,1,0:T(8,128)(2,1)S(1)} %get-tuple-element.57), channel_id=1, source_target_pairs={{0,24},{8,0},{16,8},{24,16},{32,56},{40,32},{48,40},{56,48},{64,88... | collective-permute-start | bytes 786440 | tf_op jit(solution)/shard_map/ppermute | solution.py:291
  38.5 0.0 collective-permute-start.2
  38.5 3.4 %collective-permute-done.refs_0_ = bf16[4,8,2,16,128]{4,3,2,1,0:T(8,128)(2,1)S(1)} collective-permute-done((bf16[4,8,2,16,128]{4,3,2,1,0:T(8,128)(2,1)S(1)}, bf16[4,8,2,16,128]{4,3,2,1,0:T(8,128)(2,1)S(1)}, u32[]{:S(2)}, u32[]{:S(2)}) %collective-permute-start) | collective-permute-done | bytes 262176 | tf_op jit(solution)/shard_map/ppermute | solution.py:285
  42.0 3.7 %collective-permute-start.5 = (bf16[4,8,2,16,128]{4,3,2,1,0:T(8,128)(2,1)S(1)}, bf16[4,8,2,16,128]{4,3,2,1,0:T(8,128)(2,1)S(1)}, u32[]{:S(2)}, u32[]{:S(2)}) collective-permute-start(bf16[4,8,2,16,128]{4,3,2,1,0:T(8,128)(2,1)S(1)} %collective-permute-done.refs_0_), channel_id=1, source_target_pairs={{0,24},{8,0},{16,8},{24,16},{32,56},{40,32},{48,40},{56,48},{64,88... | collective-permute-start | bytes 786440 | tf_op jit(solution)/shard_map/ppermute | solution.py:288
  45.6 0.0 collective-permute-done.3.refs_1_
  45.7 0.0 collective-permute-start.6
  45.7 2.7 %shard_map.131 = (bf16[8,2,256,128]{3,2,1,0:T(8,128)(2,1)S(1)}, bf16[8,2,256,128]{3,2,1,0:T(8,128)(2,1)S(1)}, bf16[8,2,32,128]{3,2,1,0:T(8,128)(2,1)S(1)}, bf16[...) custom-call(s32[1]{0:T(128)} %bitcast.1.own_y, s32[1,32]{1,0:T(1,128)S(1)} %copy-done.9, ...), custom_call_target="tpu_custom_call" | custom-call | flops 100000000 | bytes 1024 | tf_op jit(solution)/shard_map/pallas_call | solution.py:200
  48.4 0.0 copy-start.4
  48.4 0.0 collective-permute-done.1.refs_1_
  48.4 2.9 %collective-permute-done.2.refs_0_ = bf16[4,8,2,16,128]{4,3,2,1,0:T(8,128)(2,1)S(1)} collective-permute-done((bf16[4,8,2,16,128]{4,3,2,1,0:T(8,128)(2,1)S(1)}, bf16[4,8,2,16,128]{4,3,2,1,0:T(8,128)(2,1)S(1)}, u32[]{:S(2)}, u32[]{:S(2)}) %collective-permute-start.2) | collective-permute-done | bytes 262176 | tf_op jit(solution)/shard_map/ppermute | solution.py:292
  51.3 1.3 %shard_map.134 = (bf16[8,128,256]{2,1,0:T(8,128)(2,1)S(1)}, bf16[8,2,32,128]{3,2,1,0:T(8,128)(2,1)S(1)}, bf16[8,128,256]{2,1,0:T(8,128)(2,1)S(1)}) custom-call(bf16[8,2,256,128]{3,2,1,0:T(8,128)(2,1)S(1)} %copy-done.6, bf16[8,2,32,128]{3,2,1,0:T(8,128)(2,1)S(1)} %get-tuple-element.69.near, f32[8,1,256]{2,1,0:T(1,128)S(1)} %get-tuple-element.70.bias, ...), custom_call_target="tpu_custom_call" | custom-call | flops 1000000 | bytes 1024 | tf_op jit(solution)/shard_map/pallas_call | solution.py:219
  52.6 0.4 collective-permute-start.8
  53.0 1.3 %shard_map.132 = (bf16[8,128,256]{2,1,0:T(8,128)(2,1)S(1)}, bf16[8,2,32,128]{3,2,1,0:T(8,128)(2,1)S(1)}, bf16[8,128,256]{2,1,0:T(8,128)(2,1)S(1)}) custom-call(bf16[8,2,256,128]{3,2,1,0:T(8,128)(2,1)S(1)} %copy-done.4, bf16[8,2,32,128]{3,2,1,0:T(8,128)(2,1)S(1)} %get-tuple-element.53.near, f32[8,1,256]{2,1,0:T(1,128)S(1)} %get-tuple-element.54.bias, ...), custom_call_target="tpu_custom_call" | custom-call | flops 1000000 | bytes 1024 | tf_op jit(solution)/shard_map/pallas_call | solution.py:219
  54.3 1.7 %collective-permute-start.4 = (bf16[8,128,256]{2,1,0:T(8,128)(2,1)S(1)}, bf16[8,128,256]{2,1,0:T(8,128)(2,1)S(1)}, u32[]{:S(2)}, u32[]{:S(2)}) collective-permute-start(bf16[8,128,256]{2,1,0:T(8,128)(2,1)S(1)} %get-tuple-element.63), channel_id=1, source_target_pairs={{0,8},{8,16},{16,24},{24,0},{32,40},{40,48},{48,56},{56,32},{64,72... | collective-permute-start | bytes 1572872 | tf_op jit(solution)/shard_map/ppermute | solution.py:305
  56.0 0.0 collective-permute-done.5.refs_0_
  56.0 0.0 collective-permute-done.6.refs_1_
  56.0 1.2 %shard_map.133 = (bf16[8,128,256]{2,1,0:T(8,128)(2,1)S(1)}, bf16[8,2,32,128]{3,2,1,0:T(8,128)(2,1)S(1)}, bf16[8,128,256]{2,1,0:T(8,128)(2,1)S(1)}) custom-call(bf16[8,2,256,128]{3,2,1,0:T(8,128)(2,1)S(1)} %get-tuple-element.64.wide, bf16[8,2,32,128]{3,2,1,0:T(8,128)(2,1)S(1)} %get-tuple-element.65.near, f32[8,1,256]{2,1,0:T(1,128)S(1)} %get-tuple-element.66.bias, ...), custom_call_target="tpu_custom_call" | custom-call | flops 1000000 | bytes 1024 | tf_op jit(solution)/shard_map/pallas_call | solution.py:219
  57.3 0.3 collective-permute-start.7
  57.6 1.3 %shard_map.135 = (bf16[8,128,256]{2,1,0:T(8,128)(2,1)S(1)}, bf16[8,2,32,128]{3,2,1,0:T(8,128)(2,1)S(1)}, bf16[8,128,256]{2,1,0:T(8,128)(2,1)S(1)}) custom-call(bf16[8,2,256,128]{3,2,1,0:T(8,128)(2,1)S(1)} %get-tuple-element.74.wide, bf16[8,2,32,128]{3,2,1,0:T(8,128)(2,1)S(1)} %get-tuple-element.75.near, f32[8,1,256]{2,1,0:T(1,128)S(1)} %get-tuple-element.76.bias, ...), custom_call_target="tpu_custom_call" | custom-call | flops 1000000 | bytes 1024 | tf_op jit(solution)/shard_map/pallas_call | solution.py:219
  58.9 6.4 %shard_map.136 = (bf16[512,1024]{1,0:T(8,128)(2,1)}, bf16[512,128]{1,0:T(8,128)(2,1)}, bf16[512,128]{1,0:T(8,128)(2,1)}) custom-call(s32[1]{0:T(128)} %bitcast.1.own_y, s32[1,32]{1,0:T(1,128)S(1)} %copy-done.9, s32[1,32]{1,0:T(1,128)S(1)} %copy-done.10, bf16[8,128,256]{2,1,0:T(8,128)(2,1)S(1)} %get-tuple-element.78.refs_0_, ...), custom_call_target="tpu_custom_call" | custom-call | flops 1000000 | bytes 1024 | tf_op jit(solution)/shard_map/pallas_call | solution.py:207
  65.3 9.5 %collective-permute-done.8 = bf16[8,128,256]{2,1,0:T(8,128)(2,1)S(1)} collective-permute-done((bf16[8,128,256]{2,1,0:T(8,128)(2,1)S(1)}, bf16[8,128,256]{2,1,0:T(8,128)(2,1)S(1)}, u32[]{:S(2)}, u32[]{:S(2)}) %collective-permute-start.8) | collective-permute-done | bytes 524320 | tf_op jit(solution)/shard_map/ppermute | solution.py:305
  74.8 3.5 %collective-permute-done.4 = bf16[8,128,256]{2,1,0:T(8,128)(2,1)S(1)} collective-permute-done((bf16[8,128,256]{2,1,0:T(8,128)(2,1)S(1)}, bf16[8,128,256]{2,1,0:T(8,128)(2,1)S(1)}, u32[]{:S(2)}, u32[]{:S(2)}) %collective-permute-start.4) | collective-permute-done | bytes 524320 | tf_op jit(solution)/shard_map/ppermute | solution.py:305
  78.2 0.0 collective-permute-done.7
  78.2 0.3 add_convert_fusion
  78.5 16.8 %all_to_all.10 = bf16[8,128,256]{2,1,0:T(8,128)(2,1)S(1)} all-to-all(bf16[8,128,256]{2,1,0:T(8,128)(2,1)S(1)} %add_convert_fusion), channel_id=1, replica_groups={{0,32,64,96,128,160,192,224},{8,40,72,104,136,168,200,232},{16,48,80,11..., dimensions={0} | all-to-all | bytes 1048576 | tf_op jit(solution)/shard_map/all_to_all | solution.py:311
  95.3 0.1 reduce_sum.12
  95.4 0.6 fusion
  (9 shorter events, 0.0 us)
Async XLA Ops:
  0.6 14.0 %copy-start = (bf16[512,1024]{1,0:T(8,128)(2,1)S(1)}, bf16[512,1024]{1,0:T(8,128)(2,1)}, u32[]{:S(2)}) copy-start(bf16[512,1024]{1,0:T(8,128)(2,1)} %query.3) | copy-start | bytes 3145732
  2.4 12.2 %copy-start.7 = (bf16[512,128]{1,0:T(8,128)(2,1)S(1)}, bf16[512,128]{1,0:T(8,128)(2,1)}, u32[]{:S(2)}) copy-start(bf16[512,128]{1,0:T(8,128)(2,1)} %key.3) | copy-start | bytes 393220
  2.4 12.2 %copy-start.8 = (bf16[512,128]{1,0:T(8,128)(2,1)S(1)}, bf16[512,128]{1,0:T(8,128)(2,1)}, u32[]{:S(2)}) copy-start(bf16[512,128]{1,0:T(8,128)(2,1)} %value.3) | copy-start | bytes 393220
  2.4 29.7 %all-to-all-start = ((bf16[64,2,16,128]{3,2,1,0:T(8,128)(2,1)}), bf16[64,2,16,128]{3,2,1,0:T(8,128)(2,1)S(1)}, u32[]{:S(2)}, u32[]{:S(2)}) async-start(bf16[64,2,16,128]{3,2,1,0:T(8,128)(2,1)} %shard_map.128), calls=%async_computation | async-start | bytes 1048576 | tf_op jit(solution)/shard_map/all_to_all | solution.py:269
  14.6 0.7 copy-start.9
  14.6 0.7 copy-start.10
  14.6 0.7 copy-start.11
  15.3 1.2 %copy-start.1 = (bf16[512,1024]{1,0:T(8,128)(2,1)S(1)}, bf16[512,1024]{1,0:T(8,128)(2,1)}, u32[]{:S(2)}) copy-start(bf16[512,1024]{1,0:T(8,128)(2,1)} %cotangent.3) | copy-start | bytes 3145732
  16.5 29.2 %copy-start.2 = (bf16[512,1024]{1,0:T(8,128)(2,1)S(1)}, bf16[512,1024]{1,0:T(8,128)(2,1)}, u32[]{:S(2)}) copy-start(bf16[512,1024]{1,0:T(8,128)(2,1)} %cotangent.3) | copy-start | bytes 3145732
  19.2 1.0 %copy-start.3 = (bf16[8,2,256,128]{3,2,1,0:T(8,128)(2,1)}, bf16[8,2,256,128]{3,2,1,0:T(8,128)(2,1)S(1)}, u32[]{:S(2)}) copy-start(bf16[8,2,256,128]{3,2,1,0:T(8,128)(2,1)S(1)} %get-tuple-element.52.wide) | copy-start | bytes 3145732
  20.2 1.0 %copy-start.5 = (bf16[8,2,256,128]{3,2,1,0:T(8,128)(2,1)}, bf16[8,2,256,128]{3,2,1,0:T(8,128)(2,1)S(1)}, u32[]{:S(2)}) copy-start(bf16[8,2,256,128]{3,2,1,0:T(8,128)(2,1)S(1)} %get-tuple-element.68.wide) | copy-start | bytes 3145732
  32.2 9.8 %collective-permute-start = (bf16[4,8,2,16,128]{4,3,2,1,0:T(8,128)(2,1)S(1)}, bf16[4,8,2,16,128]{4,3,2,1,0:T(8,128)(2,1)S(1)}, u32[]{:S(2)}, u32[]{:S(2)}) collective-permute-start(bf16[4,8,2,16,128]{4,3,2,1,0:T(8,128)(2,1)S(1)} %get-tuple-element.56), channel_id=1, source_target_pairs={{0,24},{8,0},{16,8},{24,16},{32,56},{40,32},{48,40},{56,48},{64,88... | collective-permute-start | bytes 786440 | tf_op jit(solution)/shard_map/ppermute | solution.py:285
  35.3 16.0 %copy-start.6 = (bf16[8,2,256,128]{3,2,1,0:T(8,128)(2,1)S(1)}, bf16[8,2,256,128]{3,2,1,0:T(8,128)(2,1)}, u32[]{:S(2)}) copy-start(bf16[8,2,256,128]{3,2,1,0:T(8,128)(2,1)} %copy-done.5) | copy-start | bytes 3145732
  35.3 10.4 %collective-permute-start.3 = (bf16[4,8,2,16,128]{4,3,2,1,0:T(8,128)(2,1)S(1)}, bf16[4,8,2,16,128]{4,3,2,1,0:T(8,128)(2,1)S(1)}, u32[]{:S(2)}, u32[]{:S(2)}) collective-permute-start(bf16[4,8,2,16,128]{4,3,2,1,0:T(8,128)(2,1)S(1)} %get-tuple-element.57), channel_id=1, source_target_pairs={{0,8},{8,16},{16,24},{24,0},{32,40},{40,48},{48,56},{56,32},{64,72... | collective-permute-start | bytes 786440 | tf_op jit(solution)/shard_map/ppermute | solution.py:286
  35.3 13.1 %collective-permute-start.1 = (bf16[4,8,2,16,128]{4,3,2,1,0:T(8,128)(2,1)S(1)}, bf16[4,8,2,16,128]{4,3,2,1,0:T(8,128)(2,1)S(1)}, u32[]{:S(2)}, u32[]{:S(2)}) collective-permute-start(bf16[4,8,2,16,128]{4,3,2,1,0:T(8,128)(2,1)S(1)} %get-tuple-element.57), channel_id=1, source_target_pairs={{0,24},{8,0},{16,8},{24,16},{32,56},{40,32},{48,40},{56,48},{64,88... | collective-permute-start | bytes 786440 | tf_op jit(solution)/shard_map/ppermute | solution.py:291
  38.5 12.8 %collective-permute-start.2 = (bf16[4,8,2,16,128]{4,3,2,1,0:T(8,128)(2,1)S(1)}, bf16[4,8,2,16,128]{4,3,2,1,0:T(8,128)(2,1)S(1)}, u32[]{:S(2)}, u32[]{:S(2)}) collective-permute-start(bf16[4,8,2,16,128]{4,3,2,1,0:T(8,128)(2,1)S(1)} %get-tuple-element.56), channel_id=1, source_target_pairs={{0,8},{8,16},{16,24},{24,0},{32,40},{40,48},{48,56},{56,32},{64,72... | collective-permute-start | bytes 786440 | tf_op jit(solution)/shard_map/ppermute | solution.py:292
  42.0 14.1 %collective-permute-start.5 = (bf16[4,8,2,16,128]{4,3,2,1,0:T(8,128)(2,1)S(1)}, bf16[4,8,2,16,128]{4,3,2,1,0:T(8,128)(2,1)S(1)}, u32[]{:S(2)}, u32[]{:S(2)}) collective-permute-start(bf16[4,8,2,16,128]{4,3,2,1,0:T(8,128)(2,1)S(1)} %collective-permute-done.refs_0_), channel_id=1, source_target_pairs={{0,24},{8,0},{16,8},{24,16},{32,56},{40,32},{48,40},{56,48},{64,88... | collective-permute-start | bytes 786440 | tf_op jit(solution)/shard_map/ppermute | solution.py:288
  45.7 10.4 %collective-permute-start.6 = (bf16[4,8,2,16,128]{4,3,2,1,0:T(8,128)(2,1)S(1)}, bf16[4,8,2,16,128]{4,3,2,1,0:T(8,128)(2,1)S(1)}, u32[]{:S(2)}, u32[]{:S(2)}) collective-permute-start(bf16[4,8,2,16,128]{4,3,2,1,0:T(8,128)(2,1)S(1)} %collective-permute-done.3.refs_1_), channel_id=1, source_target_pairs={{0,8},{8,16},{16,24},{24,0},{32,40},{40,48},{48,56},{56,32},{64,72... | collective-permute-start | bytes 786440 | tf_op jit(solution)/shard_map/ppermute | solution.py:289
  48.4 4.6 %copy-start.4 = (bf16[8,2,256,128]{3,2,1,0:T(8,128)(2,1)S(1)}, bf16[8,2,256,128]{3,2,1,0:T(8,128)(2,1)}, u32[]{:S(2)}) copy-start(bf16[8,2,256,128]{3,2,1,0:T(8,128)(2,1)} %copy-done.3) | copy-start | bytes 3145732
  52.6 22.2 %collective-permute-start.8 = (bf16[8,128,256]{2,1,0:T(8,128)(2,1)S(1)}, bf16[8,128,256]{2,1,0:T(8,128)(2,1)S(1)}, u32[]{:S(2)}, u32[]{:S(2)}) collective-permute-start(bf16[8,128,256]{2,1,0:T(8,128)(2,1)S(1)} %get-tuple-element.73), channel_id=1, source_target_pairs={{0,24},{8,0},{16,8},{24,16},{32,56},{40,32},{48,40},{56,48},{64,88... | collective-permute-start | bytes 1572872 | tf_op jit(solution)/shard_map/ppermute | solution.py:305
  54.3 23.9 %collective-permute-start.4 = (bf16[8,128,256]{2,1,0:T(8,128)(2,1)S(1)}, bf16[8,128,256]{2,1,0:T(8,128)(2,1)S(1)}, u32[]{:S(2)}, u32[]{:S(2)}) collective-permute-start(bf16[8,128,256]{2,1,0:T(8,128)(2,1)S(1)} %get-tuple-element.63), channel_id=1, source_target_pairs={{0,8},{8,16},{16,24},{24,0},{32,40},{40,48},{48,56},{56,32},{64,72... | collective-permute-start | bytes 1572872 | tf_op jit(solution)/shard_map/ppermute | solution.py:305
  57.3 20.9 %collective-permute-start.7 = (bf16[8,128,256]{2,1,0:T(8,128)(2,1)S(1)}, bf16[8,128,256]{2,1,0:T(8,128)(2,1)S(1)}, u32[]{:S(2)}, u32[]{:S(2)}) collective-permute-start(bf16[8,128,256]{2,1,0:T(8,128)(2,1)S(1)} %get-tuple-element.67), channel_id=1, source_target_pairs={{0,16},{8,24},{16,0},{24,8},{32,48},{40,56},{48,32},{56,40},{64,80... | collective-permute-start | bytes 1572872 | tf_op jit(solution)/shard_map/ppermute | solution.py:305
